TPU v7x, 32 devices: a whole 2x2x4 slice. The times are simulated.
32 devices in a mesh: ctx: 8 (over y, x, core), fsdp: 4 (over z).
Axes of the slice: x: 2, y: 2, z: 4, core: 2. Of those that a mesh axis runs over, the one named last changes fastest.
Arguments:
- tokens: bfloat16 [16384, 1024], P(('fsdp', 'ctx')), may hold values from -6 to 6
- encoder_out: bfloat16 [8192, 1024], P(('fsdp', 'ctx')), may hold values from -6 to 6
- prompt_offsets: int32 [4, 1], P('fsdp'), may hold values from 512 to 2048, as said below
- gains: bfloat16 [3, 1024], P(None, 'fsdp'), may hold values from 0.5 to 1.5
- shifts: bfloat16 [9, 1024], P(None, 'fsdp'), may hold values from -0.59765625 to 0.59765625
- self_in: bfloat16 [1024, 3072], P('fsdp'), may hold values from -0.1875 to 0.1875
- self_out: bfloat16 [1024, 1024], P('fsdp'), may hold values from -3 to 3
- cross_q: bfloat16 [1024, 1024], P('fsdp'), may hold values from -0.1875 to 0.1875
- cross_kv: bfloat16 [1024, 2048], P('fsdp'), may hold values from -0.1875 to 0.1875
- cross_out: bfloat16 [1024, 1024], P('fsdp'), may hold values from -3 to 3
- ffn_in: bfloat16 [1024, 4096], P('fsdp'), may hold values from -0.1875 to 0.1875
- ffn_bias: bfloat16 [4096], P('fsdp'), may hold values from -0.59765625 to 0.59765625
- ffn_out: bfloat16 [4096, 1024], P('fsdp'), may hold values from -0.09375 to 0.09375
- out_bias: bfloat16 [1024], P('fsdp'), may hold values from -1 to 1
- cotangent: bfloat16 [16384, 1024], P(('fsdp', 'ctx')), may hold values from -6 to 6
Outputs:
- layer_out: bfloat16 [16384, 1024], P(('fsdp', 'ctx'))
- input_grad: float32 [16384, 1024], P(('fsdp', 'ctx'))
- enc_grad: float32 [8192, 1024], P(('fsdp', 'ctx'))
- grad_gains: float32 [3, 1024], P(None, 'fsdp')
- grad_shifts: float32 [9, 1024], P(None, 'fsdp')
- grad_self_in: float32 [1024, 3072], P('fsdp')
- grad_self_out: float32 [1024, 1024], P('fsdp')
- grad_cross_q: float32 [1024, 1024], P('fsdp')
- grad_cross_kv: float32 [1024, 2048], P('fsdp')
- grad_cross_out: float32 [1024, 1024], P('fsdp')
- grad_ffn_in: float32 [1024, 4096], P('fsdp')
- grad_ffn_bias: float32 [4096], P('fsdp')
- grad_ffn_out: float32 [4096, 1024], P('fsdp')
- grad_out_bias: float32 [1024], P('fsdp')
Inputs may be any that keep to these rules, and one draw needn't show every extreme that they name: prompt_offsets[g, c] is the number of leading prompt rows that continuation c of group g sees; each row of it has an entry equal to 2048.
All inputs are finite; a program needn't handle non-finite values.
Results may differ from a plain program's by a relative error of at most 0.024.
Values may be sent and summed in bfloat16 or wider, within the bound.
A program may use at most 640 MiB of HBM per device.

v0:
```python
import math

import jax
import jax.numpy as jnp
from jax import lax
from jax.sharding import PartitionSpec as P

HEADS = 16
CONT = 2048


epsilon = 1e-05
negative = -1e30
group_heads = 4


def from_behind(value, axis, steps):
    count = lax.axis_size(axis)
    pairs = [(source, (source + steps) % count) for source in range(count)]
    return lax.ppermute(value, axis, pairs)


def layer_norm(values, gain, shift):
    center = values - jnp.mean(values, axis=-1, keepdims=True)
    spread = jnp.mean(center * center, axis=-1, keepdims=True)
    return center * lax.rsqrt(spread + epsilon) * gain + shift


def exact_gelu(inputs):
    return jax.nn.gelu(inputs, approximate=False)


def product(left, right):
    return jnp.dot(left, right, preferred_element_type=jnp.float32)


def inner_rows(left, right):
    return lax.dot_general(
        left, right, (((0,), (0,)), ((), ())), preferred_element_type=jnp.float32
    )


def times_transposed(left, right):
    return lax.dot_general(
        left, right, (((1,), (1,)), ((), ())), preferred_element_type=jnp.float32
    )


def allowed(query_pos, key_pos, offsets, prompt):
    cont_index = jnp.maximum(query_pos - prompt, 0) // CONT
    cont_table = jnp.arange(offsets.shape[0], dtype=jnp.int32)
    prompt_limit = jnp.sum(jnp.where(cont_index[..., None] == cont_table, offsets, 0), axis=-1)
    own_start = prompt + cont_index * CONT
    return (key_pos <= query_pos) & (
        (query_pos < prompt) | (key_pos >= own_start) | (key_pos < prompt_limit)
    )


def split_groups(array, head_dim):
    row_total = array.shape[0]
    return jnp.moveaxis(array.reshape(row_total, HEADS // group_heads, group_heads, head_dim), 1, 0)


def merge_groups(array):
    moved = jnp.moveaxis(array, 0, 1)
    return moved.reshape(moved.shape[0], -1)


def head_delta(gradient, attended, head_count, head_dim):
    row_total = attended.shape[0]
    return jnp.sum(
        (gradient.astype(jnp.float32) * attended).reshape(row_total, head_count, head_dim), axis=-1
    ).T


def cross_forward(inputs):
    query_group, key_group, value_group = inputs
    scores = jnp.einsum("qhd,khd->hqk", query_group, key_group, preferred_element_type=jnp.float32)
    peaks = jnp.max(scores, axis=-1, keepdims=True)
    logsum = peaks + jnp.log(jnp.sum(jnp.exp(scores - peaks), axis=-1, keepdims=True))
    weights = jnp.exp(scores - logsum).astype(jnp.bfloat16)
    return (
        jnp.einsum("hqk,khd->qhd", weights, value_group, preferred_element_type=jnp.float32),
        logsum,
    )


def cross_backward(inputs):
    query_group, key_group, value_group, logsum, grad_group, delta_group = inputs
    scores = jnp.einsum("qhd,khd->hqk", query_group, key_group, preferred_element_type=jnp.float32)
    weights = jnp.exp(scores - logsum)
    value_grad = jnp.einsum(
        "hqk,qhd->khd", weights.astype(jnp.bfloat16), grad_group, preferred_element_type=jnp.float32
    )
    weight_grad = jnp.einsum(
        "qhd,khd->hqk", grad_group, value_group, preferred_element_type=jnp.float32
    )
    score_grad = (weights * (weight_grad - delta_group)).astype(jnp.bfloat16)
    query_grad = jnp.einsum(
        "hqk,khd->qhd", score_grad, key_group, preferred_element_type=jnp.float32
    )
    key_grad = jnp.einsum(
        "hqk,qhd->khd", score_grad, query_group, preferred_element_type=jnp.float32
    )
    return (query_grad, key_grad, value_grad)


def body(
    tokens,
    encoder_out,
    prompt_offsets,
    gains,
    shifts,
    self_in,
    self_out,
    cross_q,
    cross_kv,
    cross_out,
    ffn_in,
    ffn_bias,
    ffn_out,
    out_bias,
    cotangent,
):
    row_count, width = tokens.shape
    head_dim = width // HEADS
    scale = 1.0 / math.sqrt(head_dim)
    ctx_size = lax.axis_size("ctx")
    position = lax.axis_index("ctx")
    prompt = row_count * ctx_size // 2
    offsets = prompt_offsets[0]
    query_pos = (position * row_count + jnp.arange(row_count, dtype=jnp.int32))[:, None]
    (
        full_gains,
        full_shifts,
        full_self_in,
        full_self_out,
        full_cross_q,
        full_cross_kv,
        full_cross_out,
        full_ffn_in,
        full_ffn_bias,
        full_ffn_out,
        full_out_bias,
    ) = (
        lax.all_gather(gains, "fsdp", axis=1, tiled=True),
        lax.all_gather(shifts, "fsdp", axis=1, tiled=True),
        lax.all_gather(self_in, "fsdp", axis=0, tiled=True),
        lax.all_gather(self_out, "fsdp", axis=0, tiled=True),
        lax.all_gather(cross_q, "fsdp", axis=0, tiled=True),
        lax.all_gather(cross_kv, "fsdp", axis=0, tiled=True),
        lax.all_gather(cross_out, "fsdp", axis=0, tiled=True),
        lax.all_gather(ffn_in, "fsdp", axis=0, tiled=True),
        lax.all_gather(ffn_bias, "fsdp", axis=0, tiled=True),
        lax.all_gather(ffn_out, "fsdp", axis=0, tiled=True),
        lax.all_gather(out_bias, "fsdp", axis=0, tiled=True),
    )
    gain_values = full_gains.astype(jnp.float32)
    shift_values = full_shifts.astype(jnp.float32)
    token_values = tokens.astype(jnp.float32)
    normed_one, norm_back_one = jax.vjp(layer_norm, token_values, gain_values[0], shift_values[0])
    normed_one = normed_one.astype(jnp.bfloat16)
    projected = product(normed_one, full_self_in)
    queries = (scale * (projected[:, :width] + shift_values[3])).astype(jnp.bfloat16)
    keys = projected[:, width : 2 * width].astype(jnp.bfloat16)
    values = (projected[:, 2 * width :] + shift_values[4]).astype(jnp.bfloat16)
    key_value = jnp.concatenate([keys, values], axis=1)
    query_heads = queries.reshape(row_count, HEADS, head_dim)

    def block_mask(first_row, key_count):
        key_pos = first_row + jnp.arange(key_count, dtype=jnp.int32)[None, :]
        return allowed(query_pos, key_pos, offsets, prompt)

    incoming = lax.all_gather(keys, "ctx", axis=0, tiled=True)
    maxima = jnp.full((HEADS, row_count), negative, jnp.float32)
    totals = jnp.zeros((HEADS, row_count), jnp.float32)
    key_count = incoming.shape[0]
    live_mask = block_mask(jnp.int32(0), key_count)

    def update(unused):
        scores = jnp.einsum(
            "qhd,khd->hqk",
            query_heads,
            incoming.reshape(key_count, HEADS, head_dim),
            preferred_element_type=jnp.float32,
        )
        scores = jnp.where(live_mask[None], scores, negative)
        larger = jnp.maximum(maxima, jnp.max(scores, axis=-1))
        raised = jnp.where(live_mask[None], jnp.exp(scores - larger[..., None]), 0.0)
        return (larger, jnp.sum(raised, axis=-1))

    def unchanged(unused):
        return (maxima, totals)

    maxima, totals = lax.cond(jnp.any(live_mask), update, unchanged, 0)
    logsum = maxima + jnp.log(totals)
    running = jnp.zeros((row_count, HEADS, head_dim), jnp.float32)
    fold_incoming = lax.all_gather(key_value, "ctx", axis=0, tiled=True)
    fold_key_count = fold_incoming.shape[0]
    fold_live_mask = block_mask(jnp.int32(0), fold_key_count)

    def update(unused):
        key_heads = fold_incoming[:, :width].reshape(fold_key_count, HEADS, head_dim)
        value_heads = fold_incoming[:, width:].reshape(fold_key_count, HEADS, head_dim)
        scores = jnp.einsum(
            "qhd,khd->hqk", query_heads, key_heads, preferred_element_type=jnp.float32
        )
        weights = jnp.where(fold_live_mask[None], jnp.exp(scores - logsum[..., None]), 0.0).astype(
            jnp.bfloat16
        )
        return jnp.einsum("hqk,khd->qhd", weights, value_heads, preferred_element_type=jnp.float32)

    def unchanged(unused):
        return running

    attended = lax.cond(jnp.any(fold_live_mask), update, unchanged, 0)
    attended = attended.reshape(row_count, width)
    mixed = attended.astype(jnp.bfloat16)
    first_sum = token_values + product(mixed, full_self_out) + shift_values[5]
    normed_two, norm_back_two = jax.vjp(layer_norm, first_sum, gain_values[1], shift_values[1])
    normed_two = normed_two.astype(jnp.bfloat16)
    cross_queries = (scale * (product(normed_two, full_cross_q) + shift_values[6])).astype(
        jnp.bfloat16
    )
    enc_projected = product(encoder_out, full_cross_kv)
    enc_keys_local = enc_projected[:, :width].astype(jnp.bfloat16)
    enc_values_local = (enc_projected[:, width:] + shift_values[7]).astype(jnp.bfloat16)
    enc_local = jnp.concatenate([enc_keys_local, enc_values_local], axis=1)
    enc_pairs = lax.all_gather(enc_local, "ctx", axis=0, tiled=True)
    query_groups = split_groups(cross_queries, head_dim)
    key_groups = split_groups(enc_pairs[:, :width], head_dim)
    value_groups = split_groups(enc_pairs[:, width:], head_dim)
    cross_groups, cross_logsum = lax.map(cross_forward, (query_groups, key_groups, value_groups))
    cross_attended = merge_groups(cross_groups)
    cross_mixed = cross_attended.astype(jnp.bfloat16)
    second_sum = first_sum + product(cross_mixed, full_cross_out) + shift_values[8]
    normed_three, norm_back_three = jax.vjp(layer_norm, second_sum, gain_values[2], shift_values[2])
    normed_three = normed_three.astype(jnp.bfloat16)
    pre_hidden = product(normed_three, full_ffn_in) + full_ffn_bias.astype(jnp.float32)
    activated, gelu_back = jax.vjp(exact_gelu, pre_hidden)
    hidden = activated.astype(jnp.bfloat16)
    layer_out = (
        second_sum + product(hidden, full_ffn_out) + full_out_bias.astype(jnp.float32)
    ).astype(jnp.bfloat16)
    (
        full_gains,
        full_shifts,
        full_self_in,
        full_self_out,
        full_cross_q,
        full_cross_kv,
        full_cross_out,
        full_ffn_in,
        full_ffn_bias,
        full_ffn_out,
        full_out_bias,
    ) = (
        lax.all_gather(gains, "fsdp", axis=1, tiled=True),
        lax.all_gather(shifts, "fsdp", axis=1, tiled=True),
        lax.all_gather(self_in, "fsdp", axis=0, tiled=True),
        lax.all_gather(self_out, "fsdp", axis=0, tiled=True),
        lax.all_gather(cross_q, "fsdp", axis=0, tiled=True),
        lax.all_gather(cross_kv, "fsdp", axis=0, tiled=True),
        lax.all_gather(cross_out, "fsdp", axis=0, tiled=True),
        lax.all_gather(ffn_in, "fsdp", axis=0, tiled=True),
        lax.all_gather(ffn_bias, "fsdp", axis=0, tiled=True),
        lax.all_gather(ffn_out, "fsdp", axis=0, tiled=True),
        lax.all_gather(out_bias, "fsdp", axis=0, tiled=True),
    )
    grad_out_values = cotangent.astype(jnp.float32)
    grad_ffn_out = inner_rows(hidden, cotangent)
    grad_out_bias = jnp.sum(grad_out_values, axis=0)
    grad_hidden = times_transposed(cotangent, full_ffn_out)
    grad_pre = gelu_back(grad_hidden)[0].astype(jnp.bfloat16)
    grad_ffn_in = inner_rows(normed_three, grad_pre)
    grad_ffn_bias = jnp.sum(grad_pre.astype(jnp.float32), axis=0)
    back_three = norm_back_three(times_transposed(grad_pre, full_ffn_in))
    grad_second = grad_out_values + back_three[0]
    branch_two = grad_second.astype(jnp.bfloat16)
    grad_cross_out = inner_rows(cross_mixed, branch_two)
    grad_cross_mixed = times_transposed(branch_two, full_cross_out).astype(jnp.bfloat16)
    delta_two = head_delta(grad_cross_mixed, cross_attended, HEADS, head_dim)
    delta_groups = delta_two.reshape(HEADS // group_heads, group_heads, row_count)[..., None]
    query_back, key_back, value_back = lax.map(
        cross_backward,
        (
            query_groups,
            key_groups,
            value_groups,
            cross_logsum,
            split_groups(grad_cross_mixed, head_dim),
            delta_groups,
        ),
    )
    cross_query_grad = (
        merge_groups(query_back).astype(jnp.bfloat16).astype(jnp.float32) * scale
    ).astype(jnp.bfloat16)
    enc_partial = jnp.concatenate([merge_groups(key_back), merge_groups(value_back)], axis=1)
    enc_grad_sum = lax.psum_scatter(
        enc_partial.astype(jnp.bfloat16), "ctx", scatter_dimension=0, tiled=True
    )
    grad_cross_kv = inner_rows(encoder_out, enc_grad_sum)
    grad_encoder = times_transposed(enc_grad_sum, full_cross_kv)
    grad_cross_q = inner_rows(normed_two, cross_query_grad)
    back_two = norm_back_two(times_transposed(cross_query_grad, full_cross_q))
    grad_first = grad_second + back_two[0]
    branch_one = grad_first.astype(jnp.bfloat16)
    grad_self_out = inner_rows(mixed, branch_one)
    grad_mixed = times_transposed(branch_one, full_self_out).astype(jnp.bfloat16)
    delta_one = head_delta(grad_mixed, attended, HEADS, head_dim)
    grad_heads = grad_mixed.reshape(row_count, HEADS, head_dim)

    def back_block(key_pair, first_row):
        live_mask = block_mask(first_row, row_count)

        def update(unused):
            key_heads = key_pair[:, :width].reshape(row_count, HEADS, head_dim)
            value_heads = key_pair[:, width:].reshape(row_count, HEADS, head_dim)
            scores = jnp.einsum(
                "qhd,khd->hqk", query_heads, key_heads, preferred_element_type=jnp.float32
            )
            weights = jnp.where(live_mask[None], jnp.exp(scores - logsum[..., None]), 0.0)
            value_grad = jnp.einsum(
                "hqk,qhd->khd",
                weights.astype(jnp.bfloat16),
                grad_heads,
                preferred_element_type=jnp.float32,
            )
            weight_grad = jnp.einsum(
                "qhd,khd->hqk", grad_heads, value_heads, preferred_element_type=jnp.float32
            )
            score_grad = (weights * (weight_grad - delta_one[..., None])).astype(jnp.bfloat16)
            query_grad = jnp.einsum(
                "hqk,khd->qhd", score_grad, key_heads, preferred_element_type=jnp.float32
            )
            key_grad = jnp.einsum(
                "hqk,qhd->khd", score_grad, query_heads, preferred_element_type=jnp.float32
            )
            return (
                query_grad,
                jnp.concatenate(
                    [key_grad.reshape(row_count, width), value_grad.reshape(row_count, width)],
                    axis=1,
                ),
            )

        def nothing(unused):
            return (
                jnp.zeros((row_count, HEADS, head_dim), jnp.float32),
                jnp.zeros((row_count, 2 * width), jnp.float32),
            )

        return lax.cond(jnp.any(live_mask), update, nothing, 0)

    def pass_keys(key_pair):
        return from_behind(key_pair, "ctx", -1)

    def pass_grads(carried):
        return from_behind(carried.astype(jnp.bfloat16), "ctx", -1).astype(carried.dtype)

    def turn_step(turn_index, loop_state):
        query_total, key_pair, carried = loop_state
        anchor = (position + turn_index) % ctx_size
        query_part, block_grads = back_block(key_pair, anchor * row_count)
        return (query_total + query_part, pass_keys(key_pair), pass_grads(carried + block_grads))

    loop_state = (
        jnp.zeros((row_count, HEADS, head_dim), jnp.float32),
        key_value,
        jnp.zeros((row_count, 2 * width), jnp.float32),
    )
    query_total, key_pair, carried = lax.fori_loop(0, ctx_size - 1, turn_step, loop_state)
    anchor = (position + (ctx_size - 1)) % ctx_size
    query_part, block_grads = back_block(key_pair, anchor * row_count)
    query_total = query_total + query_part
    carried = pass_grads(carried + block_grads)
    self_query_grad = (
        query_total.reshape(row_count, width).astype(jnp.bfloat16).astype(jnp.float32) * scale
    ).astype(jnp.bfloat16)
    key_grad_low = carried[:, :width].astype(jnp.bfloat16)
    value_grad_low = carried[:, width:].astype(jnp.bfloat16)
    grad_project = jnp.concatenate([self_query_grad, key_grad_low, value_grad_low], axis=1)
    grad_self_in = inner_rows(normed_one, grad_project)
    back_one = norm_back_one(times_transposed(grad_project, full_self_in))
    grad_tokens = grad_first + back_one[0]
    grad_gains = jnp.stack([back_one[1], back_two[1], back_three[1]])
    grad_shifts = jnp.stack(
        [
            back_one[2],
            back_two[2],
            back_three[2],
            jnp.sum(self_query_grad.astype(jnp.float32), axis=0),
            jnp.sum(value_grad_low.astype(jnp.float32), axis=0),
            jnp.sum(branch_one.astype(jnp.float32), axis=0),
            jnp.sum(cross_query_grad.astype(jnp.float32), axis=0),
            jnp.sum(enc_grad_sum[:, width:].astype(jnp.float32), axis=0),
            jnp.sum(branch_two.astype(jnp.float32), axis=0),
        ]
    )
    reduced = (
        lax.psum_scatter(
            grad_gains.astype(jnp.bfloat16), "fsdp", scatter_dimension=1, tiled=True
        ).astype(jnp.float32),
        lax.psum_scatter(
            grad_shifts.astype(jnp.bfloat16), "fsdp", scatter_dimension=1, tiled=True
        ).astype(jnp.float32),
        lax.psum_scatter(
            grad_self_in.astype(jnp.bfloat16), "fsdp", scatter_dimension=0, tiled=True
        ).astype(jnp.float32),
        lax.psum_scatter(
            grad_self_out.astype(jnp.bfloat16), "fsdp", scatter_dimension=0, tiled=True
        ).astype(jnp.float32),
        lax.psum_scatter(
            grad_cross_q.astype(jnp.bfloat16), "fsdp", scatter_dimension=0, tiled=True
        ).astype(jnp.float32),
        lax.psum_scatter(
            grad_cross_kv.astype(jnp.bfloat16), "fsdp", scatter_dimension=0, tiled=True
        ).astype(jnp.float32),
        lax.psum_scatter(
            grad_cross_out.astype(jnp.bfloat16), "fsdp", scatter_dimension=0, tiled=True
        ).astype(jnp.float32),
        lax.psum_scatter(
            grad_ffn_in.astype(jnp.bfloat16), "fsdp", scatter_dimension=0, tiled=True
        ).astype(jnp.float32),
        lax.psum_scatter(
            grad_ffn_bias.astype(jnp.bfloat16), "fsdp", scatter_dimension=0, tiled=True
        ).astype(jnp.float32),
        lax.psum_scatter(
            grad_ffn_out.astype(jnp.bfloat16), "fsdp", scatter_dimension=0, tiled=True
        ).astype(jnp.float32),
        lax.psum_scatter(
            grad_out_bias.astype(jnp.bfloat16), "fsdp", scatter_dimension=0, tiled=True
        ).astype(jnp.float32),
    )
    totals_all = (
        lax.psum(reduced[0].astype(jnp.bfloat16), "ctx").astype(jnp.float32),
        lax.psum(reduced[1].astype(jnp.bfloat16), "ctx").astype(jnp.float32),
        lax.psum(reduced[2].astype(jnp.bfloat16), "ctx").astype(jnp.float32),
        lax.psum(reduced[3].astype(jnp.bfloat16), "ctx").astype(jnp.float32),
        lax.psum(reduced[4].astype(jnp.bfloat16), "ctx").astype(jnp.float32),
        lax.psum(reduced[5].astype(jnp.bfloat16), "ctx").astype(jnp.float32),
        lax.psum(reduced[6].astype(jnp.bfloat16), "ctx").astype(jnp.float32),
        lax.psum(reduced[7].astype(jnp.bfloat16), "ctx").astype(jnp.float32),
        lax.psum(reduced[8].astype(jnp.bfloat16), "ctx").astype(jnp.float32),
        lax.psum(reduced[9].astype(jnp.bfloat16), "ctx").astype(jnp.float32),
        lax.psum(reduced[10].astype(jnp.bfloat16), "ctx").astype(jnp.float32),
    )
    return (
        layer_out,
        grad_tokens,
        grad_encoder,
        totals_all[0],
        totals_all[1],
        totals_all[2],
        totals_all[3],
        totals_all[4],
        totals_all[5],
        totals_all[6],
        totals_all[7],
        totals_all[8],
        totals_all[9],
        totals_all[10],
    )


def solution(mesh):
    return jax.shard_map(
        body,
        mesh=mesh,
        in_specs=(
            P(("fsdp", "ctx"), None),
            P(("fsdp", "ctx"), None),
            P("fsdp", None),
            P(None, "fsdp"),
            P(None, "fsdp"),
            P("fsdp", None),
            P("fsdp", None),
            P("fsdp", None),
            P("fsdp", None),
            P("fsdp", None),
            P("fsdp", None),
            P("fsdp"),
            P("fsdp", None),
            P("fsdp"),
            P(("fsdp", "ctx"), None),
        ),
        out_specs=(
            P(("fsdp", "ctx"), None),
            P(("fsdp", "ctx"), None),
            P(("fsdp", "ctx"), None),
            P(None, "fsdp"),
            P(None, "fsdp"),
            P("fsdp", None),
            P("fsdp", None),
            P("fsdp", None),
            P("fsdp", None),
            P("fsdp", None),
            P("fsdp", None),
            P("fsdp"),
            P("fsdp", None),
            P("fsdp"),
        ),
        check_vma=False,
    )
```

profile of v0, /device:TPU:0, one launch (start us, length us, event | category | flops | bytes accessed | tf_op | source)
XLA Modules:
  0.0 2545.9 jit_solution(1733907206586447124)
XLA Ops:
  8.7 15.0 all_gather.50
  24.4 68.7 %all-gather.20.cloned.1.call-done = bf16[1024,2048]{1,0:T(8,128)(2,1)} async-done(((bf16[256,2048]{1,0:T(8,128)(2,1)}), bf16[1024,2048]{1,0:T(8,128)(2,1)}) %all-gather.20.cloned.1.call-update) | async-done | bytes 4194320 | tf_op jit(solution)/shard_map/all_gather | solution.py:151
  97.9 12.1 all_gather.49
  111.8 96.8 %all-gather.12.cloned.1.call-done = bf16[1024,3072]{1,0:T(8,128)(2,1)} async-done(((bf16[256,3072]{1,0:T(8,128)(2,1)}), bf16[1024,3072]{1,0:T(8,128)(2,1)}) %all-gather.12.cloned.1.call-update) | async-done | bytes 6291472 | tf_op jit(solution)/shard_map/all_gather | solution.py:148
  237.6 11.9 all_gather.60
  250.6 13.1 all-gather.22.cloned.1.call-done
  282.7 37.8 %all-gather.16.cloned.1.call-done = bf16[4096,1024]{1,0:T(8,128)(2,1)} async-done(((bf16[512,1024]{1,0:T(8,128)(2,1)}), bf16[4096,1024]{1,0:T(8,128)(2,1)}) %all-gather.16.cloned.1.call-update) | async-done | bytes 8388624 | tf_op jit(solution)/shard_map/all_gather | solution.py:174
  320.5 109.0 %conditional.4 = (f32[16,512]{1,0:T(8,128)}, f32[16,512]{1,0:T(8,128)S(1)}) conditional(s32[]{:T(128)} %convert_element_type.286, () %tuple.75, (pred[512,4096]{1,0:T(8,128)(4,1)}, bf16[4096,1024]{1,0:T(8,128)(2,1)}, bf16[512,16,64]{0,2,1:T(8,128)(2,1)S(1)}) %tuple.267), branch_computations={%region_3.4_spmd, %region_4.7_spmd} | conditional | flops 4496285696 | bytes 299073536 | solution.py:195
  320.7 11.4 copy.60
  332.0 52.1 %select_reduce_fusion.1 = (f32[16,512]{1,0:T(8,128)S(1)}, f32[16,512,4096]{2,1,0:T(8,128)}) fusion(pred[512,4096]{1,0:T(8,128)(4,1)} %get-tuple-element.361, bf16[512,16,64]{0,2,1:T(8,128)(2,1)S(1)} %get-tuple-element.362, bf16[4096,16,64]{0,2,1:T(8,128)(2,1)} %bitcast.274), kind=kOutput, calls=%fused_computation.2 | convolution fusion | flops 4362067968 | bytes 145784832 | tf_op jit(solution)/shard_map/cond/branch_1_fun/qhd,khd->hqk/dot_general | solution.py:181
  384.8 44.7 %select_reduce_fusion = f32[16,512]{1,0:T(8,128)S(1)} fusion(f32[16,512,4096]{2,1,0:T(8,128)} %get-tuple-element.699, f32[16,512]{1,0:T(8,128)} %broadcast_maximum_fusion, pred[512,4096]{1,0:T(8,128)(4,1)} %get-tuple-element.361), kind=kLoop, calls=%fused_computation.1 | loop fusion | flops 134209536 | bytes 136380416 | tf_op jit(solution)/shard_map/cond/branch_1_fun/reduce_sum | solution.py:190
  430.9 82.6 %conditional.5 = (bf16[512,1024]{0,1:T(8,128)(2,1)}, f32[512,1024]{1,0:T(8,128)}) conditional(s32[]{:T(128)} %convert_element_type.286, () %tuple.74, (pred[512,4096]{1,0:T(8,128)(4,1)}, bf16[4096,2048]{1,0:T(8,128)(2,1)}, bf16[512,16,64]{0,2,1:T(8,128)(2,1)S(1)}, f32[16,512]{1,0:T(8,128)}) %tuple.268), branch_computations={%region_7.8_spmd, %region_8.9_spmd} | conditional | flops 8691122176 | bytes 96501776 | solution.py:216
  430.9 20.9 copy.61
  451.9 11.8 fusion.123
  463.7 43.8 %fusion.2 = f32[16,512,64]{1,2,0:T(8,128)} fusion(bf16[4096,16,64]{0,2,1:T(8,128)(2,1)} %bitcast.284, f32[16,512]{1,0:T(8,128)} %get-tuple-element.367, pred[512,4096]{1,0:T(8,128)(4,1)} %get-tuple-element.364, bf16[512,16,64]{0,2,1:T(8,128)(2,1)S(1)} %get-tuple-element.365, bf16[4096,16,64]{0,2,1:T(8,128)(2,1)} %bitcast.283), kind=kOutput, calls=%fused_computation.5 | convolution fusion | flops 8690597888 | bytes 22052864 | tf_op jit(solution)/shard_map/cond/branch_1_fun/hqk,khd->qhd/dot_general | solution.py:211
  523.4 113.7 %while.49 = (s32[]{:T(128)}, f32[4,512,4,64]{1,3,2,0:T(8,128)}, f32[4,4,512,1]{2,1,3,0:T(4,128)}, bf16[4,2048,4,64]{1,3,2,0:T(8,128)(2,1)}, bf16[4,512,4,64]{1,3...) while((s32[]{:T(128)}, f32[4,512,4,64]{1,3,2,0:T(8,128)}, f32[4,4,512,1]{2,1,3,0:T(4,128)}, ...), condition=%wide.region_14.15_spmd.clone, body=%wide.region_11.14_spmd.sunk.clone | while | flops 1094711296 | bytes 53283396 | solution.py:233
  523.4 9.5 fusion.232
  541.7 9.7 fusion.233
  551.4 10.1 fusion.232
  571.4 9.7 fusion.233
  581.1 9.5 fusion.232
  599.4 9.7 fusion.233
  627.4 9.7 fusion.233
  646.1 56.4 %all-gather.28.cloned.1.call-done = bf16[1024,4096]{1,0:T(8,128)(2,1)} async-done(((bf16[256,4096]{1,0:T(8,128)(2,1)}), bf16[1024,4096]{1,0:T(8,128)(2,1)}) %all-gather.28.cloned.1.call-update) | async-done | bytes 8388624 | tf_op jit(solution)/shard_map/all_gather | solution.py:153
  702.6 12.3 fusion.110
  714.9 137.0 %all-gather.30.cloned.1.call-done = bf16[4096,1024]{1,0:T(8,128)(2,1)} async-done(((bf16[1024,1024]{1,0:T(8,128)(2,1)}), bf16[4096,1024]{1,0:T(8,128)(2,1)}) %all-gather.30.cloned.1.call-update) | async-done | bytes 8388624 | tf_op jit(solution)/shard_map/all_gather | solution.py:155
  851.9 28.4 %fusion.113 = (bf16[4096]{0:T(1024)(128)(2,1)}, bf16[512,4096]{1,0:T(8,128)(2,1)}, f32[512,4096]{1,0:T(8,128)}) fusion(f32[512,4096]{1,0:T(8,128)} %fusion.110, f32[4096]{0:T(1024)S(1)} %copy-done.48, bf16[512,1024]{1,0:T(8,128)(2,1)S(1)} %copy-done.31, bf16[4096,1024]{1,0:T(8,128)(2,1)} %all-gather.30.cloned.1.call-done), kind=kOutput, calls=%fused_computation.223 | convolution fusion | flops 4450152448 | bytes 30433280 | tf_op jit(solution)/shard_map/dot_general | solution.py:44
  902.0 116.5 %while.50 = (s32[]{:T(128)}, bf16[4,512,4,64]{1,3,2,0:T(8,128)(2,1)}, bf16[4,2048,4,64]{1,3,2,0:T(8,128)(2,1)}, bf16[4,2048,4,64]{1,3,2,0:T(8,128)(2,1)}, bf16[4...) while((s32[]{:T(128)}, ...), condition=%wide.region_21.22_spmd.clone, body=%wide.region_20.21_spmd.sunk.clone | while | flops 2709520384 | bytes 84472936 | solution.py:284
  1068.1 716.5 %while.51 = (s32[]{:T(128)}, f32[512,16,64]{0,2,1:T(8,128)}, bf16[512,2048]{0,1:T(8,128)(2,1)}, f32[512,2048]{0,1:T(8,128)}, s32[]{:T(128)}, /*index=5*/s32[1]{0...) while((s32[]{:T(128)}, f32[512,16,64]{0,2,1:T(8,128)}, ...), condition=%wide.region_29.30_spmd.clone.clone, body=%wide.region_25.29_spmd.clone.sunk.clone | while | flops 2726044160 | bytes 238933616 | solution.py:372
  1073.9 42.3 %conditional.10 = (f32[512,16,64]{0,2,1:T(8,128)}, f32[512,2048]{0,1:T(8,128)}) conditional(s32[]{:T(128)} %convert_element_type.483, () %tuple.204, (pred[512,512]{1,0:T(8,128)(4,1)S(1)}, bf16[512,2048]{0,1:T(8,128)(2,1)}, bf16[512,16,64]{0,2,1:T(8,128)(2,1)S(1)}, f32[16,512]{1,0:T(8,128)}, bf16[512,16,64]{0,2,1:T(8,128)(2,1)}, ...), branch_computations={%region_27.27_spmd, %region_28.28_spmd} | conditional | flops 2718957568 | bytes 194609360 | solution.py:353
  1085.2 11.8 multiply_convert_fusion.1
  1127.5 19.9 collective-permute-done.1
  1151.6 18.3 collective-permute-done
  1185.6 40.6 %collective-permute-start.1 = (bf16[512,2048]{0,1:T(8,128)(2,1)}, bf16[512,2048]{0,1:T(8,128)(2,1)}, u32[]{:S(2)}, u32[]{:S(2)}) collective-permute-start(bf16[512,2048]{0,1:T(8,128)(2,1)} %fusion.249), channel_id=1, source_target_pairs={{0,28},{4,0},{8,4},{12,8},{16,12},{20,16},{24,20},{28,24},{1,29},{... | collective-permute-start | bytes 6291464 | tf_op jit(solution)/shard_map/while/body/eval_jaxpr/ppermute | solution.py:20
  1230.4 19.6 collective-permute-done.1
  1254.2 18.3 collective-permute-done
  1288.2 40.3 %collective-permute-start.1 = (bf16[512,2048]{0,1:T(8,128)(2,1)}, bf16[512,2048]{0,1:T(8,128)(2,1)}, u32[]{:S(2)}, u32[]{:S(2)}) collective-permute-start(bf16[512,2048]{0,1:T(8,128)(2,1)} %fusion.249), channel_id=1, source_target_pairs={{0,28},{4,0},{8,4},{12,8},{16,12},{20,16},{24,20},{28,24},{1,29},{... | collective-permute-start | bytes 6291464 | tf_op jit(solution)/shard_map/while/body/eval_jaxpr/ppermute | solution.py:20
  1332.8 19.6 collective-permute-done.1
  1356.6 18.3 collective-permute-done
  1390.5 40.3 %collective-permute-start.1 = (bf16[512,2048]{0,1:T(8,128)(2,1)}, bf16[512,2048]{0,1:T(8,128)(2,1)}, u32[]{:S(2)}, u32[]{:S(2)}) collective-permute-start(bf16[512,2048]{0,1:T(8,128)(2,1)} %fusion.249), channel_id=1, source_target_pairs={{0,28},{4,0},{8,4},{12,8},{16,12},{20,16},{24,20},{28,24},{1,29},{... | collective-permute-start | bytes 6291464 | tf_op jit(solution)/shard_map/while/body/eval_jaxpr/ppermute | solution.py:20
  1435.1 19.6 collective-permute-done.1
  1458.9 18.3 collective-permute-done
  1492.9 40.3 %collective-permute-start.1 = (bf16[512,2048]{0,1:T(8,128)(2,1)}, bf16[512,2048]{0,1:T(8,128)(2,1)}, u32[]{:S(2)}, u32[]{:S(2)}) collective-permute-start(bf16[512,2048]{0,1:T(8,128)(2,1)} %fusion.249), channel_id=1, source_target_pairs={{0,28},{4,0},{8,4},{12,8},{16,12},{20,16},{24,20},{28,24},{1,29},{... | collective-permute-start | bytes 6291464 | tf_op jit(solution)/shard_map/while/body/eval_jaxpr/ppermute | solution.py:20
  1537.4 19.6 collective-permute-done.1
  1561.3 18.3 collective-permute-done
  1595.2 40.3 %collective-permute-start.1 = (bf16[512,2048]{0,1:T(8,128)(2,1)}, bf16[512,2048]{0,1:T(8,128)(2,1)}, u32[]{:S(2)}, u32[]{:S(2)}) collective-permute-start(bf16[512,2048]{0,1:T(8,128)(2,1)} %fusion.249), channel_id=1, source_target_pairs={{0,28},{4,0},{8,4},{12,8},{16,12},{20,16},{24,20},{28,24},{1,29},{... | collective-permute-start | bytes 6291464 | tf_op jit(solution)/shard_map/while/body/eval_jaxpr/ppermute | solution.py:20
  1639.8 19.6 collective-permute-done.1
  1663.6 18.3 collective-permute-done
  1697.5 40.3 %collective-permute-start.1 = (bf16[512,2048]{0,1:T(8,128)(2,1)}, bf16[512,2048]{0,1:T(8,128)(2,1)}, u32[]{:S(2)}, u32[]{:S(2)}) collective-permute-start(bf16[512,2048]{0,1:T(8,128)(2,1)} %fusion.249), channel_id=1, source_target_pairs={{0,28},{4,0},{8,4},{12,8},{16,12},{20,16},{24,20},{28,24},{1,29},{... | collective-permute-start | bytes 6291464 | tf_op jit(solution)/shard_map/while/body/eval_jaxpr/ppermute | solution.py:20
  1742.1 19.6 collective-permute-done.1
  1765.9 18.3 collective-permute-done
  1793.1 39.2 %collective-permute-start.2 = (bf16[512,2048]{0,1:T(8,128)(2,1)S(1)}, bf16[512,2048]{0,1:T(8,128)(2,1)S(1)}, u32[]{:S(2)}, u32[]{:S(2)}) collective-permute-start(bf16[512,2048]{0,1:T(8,128)(2,1)S(1)} %add_convert_fusion.1), channel_id=1, source_target_pairs={{0,28},{4,0},{8,4},{12,8},{16,12},{20,16},{24,20},{28,24},{1,29},{... | collective-permute-start | bytes 6291464 | tf_op jit(solution)/shard_map/ppermute | solution.py:20
  1834.4 21.5 collective-permute-done.2
  1865.1 10.9 convolution_convert_fusion.1
  1876.7 10.0 multiply_convert_fusion.3
  1913.7 60.2 %reduce-scatter.17.cloned.1.call-done = bf16[256,3072]{1,0:T(8,128)(2,1)} async-done(((bf16[1024,3072]{1,0:T(8,128)(2,1)}), bf16[256,3072]{1,0:T(8,128)(2,1)}) %reduce-scatter.17.cloned.1.call-update) | async-done | bytes 1572880 | tf_op jit(solution)/shard_map/reduce_scatter | solution.py:407
  1973.9 147.2 %reduce-scatter.27.cloned.1.call-done = bf16[256,4096]{1,0:T(8,128)(2,1)} async-done(((bf16[1024,4096]{1,0:T(8,128)(2,1)}), bf16[256,4096]{1,0:T(8,128)(2,1)}) %reduce-scatter.27.cloned.1.call-update) | async-done | bytes 2097168 | tf_op jit(solution)/shard_map/reduce_scatter | solution.py:422
  2121.2 147.4 %reduce-scatter.29.cloned.1.call-done = bf16[1024,1024]{1,0:T(8,128)(2,1)} async-done(((bf16[4096,1024]{1,0:T(8,128)(2,1)}), bf16[1024,1024]{1,0:T(8,128)(2,1)}) %reduce-scatter.29.cloned.1.call-update) | async-done | bytes 2097168 | tf_op jit(solution)/shard_map/reduce_scatter | solution.py:428
  2268.6 80.2 %reduce-scatter.23.cloned.1.call-done = bf16[256,2048]{0,1:T(8,128)(2,1)} async-done(((bf16[1024,2048]{0,1:T(8,128)(2,1)}), bf16[256,2048]{0,1:T(8,128)(2,1)}) %reduce-scatter.23.cloned.1.call-update) | async-done | bytes 1048592 | tf_op jit(solution)/shard_map/reduce_scatter | solution.py:416
  2351.4 10.1 all-gather
  2361.5 15.8 all-reduce.4
  2377.4 10.8 add_convert_fusion.3
  2395.7 23.6 all-reduce.2
  2421.6 103.3 %all-reduce.7.cloned.1.call-done = (bf16[256,2048]{0,1:T(8,128)(2,1)}, bf16[256,3072]{1,0:T(8,128)(2,1)}, bf16[256,1024]{1,0:T(8,128)(2,1)}, bf16[256,1024]{1,0:...) async-done(((bf16[256,2048]{0,1:T(8,128)(2,1)}, bf16[256,3072]{1,0:T(8,128)(2,1)}, bf16[256,1024]{1,0:T(8,128)(2,1)}, ...) | async-done | bytes 8388624 | tf_op jit(solution)/shard_map/psum | solution.py:441
  (502 shorter events, 607.8 us)
Async XLA Ops:
  7.2 85.9 %copy-start = (bf16[256,1024]{1,0:T(8,128)(2,1)S(1)}, bf16[256,1024]{1,0:T(8,128)(2,1)}, u32[]{:S(2)}) copy-start(bf16[256,1024]{1,0:T(8,128)(2,1)} %param.30) | copy-start | bytes 1572868
  7.2 85.9 %all-gather.20.cloned.1.call-start = ((), (), s32[]{:S(2)}) async-start(), calls=%async_computation.14 | async-start | bytes 5242880 | tf_op jit(solution)/shard_map/all_gather | solution.py:151
  7.9 200.7 %all-gather.12.cloned.1.call-start = ((), (), s32[]{:S(2)}) async-start(), calls=%async_computation.10 | async-start | bytes 7864320 | tf_op jit(solution)/shard_map/all_gather | solution.py:148
  8.7 255.1 %all-gather.22.cloned.1.call-start = ((), (), s32[]{:S(2)}) async-start(), calls=%async_computation.15 | async-start | bytes 9437184 | tf_op jit(solution)/shard_map/all_gather | solution.py:229
  24.4 184.3 %copy-start.88 = (f32[1,1024]{1,0:T(1,128)}, f32[1,1024]{1,0:T(1,128)S(1)}, u32[]{:S(2)}) copy-start(f32[1,1024]{1,0:T(1,128)S(1)} %get-tuple-element.726) | copy-start | bytes 12292
  97.8 222.6 %all-gather.16.cloned.1.call-start = ((), (), s32[]{:S(2)}) async-start(), calls=%async_computation.12 | async-start | bytes 9437184 | tf_op jit(solution)/shard_map/all_gather | solution.py:174
  110.2 104.2 %copy-start.52 = (f32[512]{0:T(512)}, f32[512]{0:T(512)S(1)}, u32[]{:S(2)}) copy-start(f32[512]{0:T(512)S(1)} %broadcast_multiply_fusion.2) | copy-start | bytes 6148
  111.2 103.2 %copy-start.70 = (f32[512]{0:T(512)}, f32[512]{0:T(512)S(1)}, u32[]{:S(2)}) copy-start(f32[512]{0:T(512)S(1)} %fusion.99) | copy-start | bytes 6148
  111.8 102.6 %copy-start.50 = (f32[1,1024]{1,0:T(1,128)}, f32[1,1024]{1,0:T(1,128)S(1)}, u32[]{:S(2)}) copy-start(f32[1,1024]{1,0:T(1,128)S(1)} %get-tuple-element.729) | copy-start | bytes 12292
  218.4 212.6 %all-gather.14.cloned.1.call-start = ((), (), s32[]{:S(2)}) async-start(), calls=%async_computation.11 | async-start | bytes 18874368 | tf_op jit(solution)/shard_map/all_gather | solution.py:198
  223.9 289.6 %all-gather.18.cloned.1.call-start = ((), (), s32[]{:S(2)}) async-start(), calls=%async_computation.13 | async-start | bytes 2621440 | tf_op jit(solution)/shard_map/all_gather | solution.py:149
  224.5 25.6 %copy-start.34 = (bf16[512,1024]{1,0:T(8,128)(2,1)S(1)}, bf16[512,1024]{1,0:T(8,128)(2,1)}, u32[]{:S(2)}) copy-start(bf16[512,1024]{1,0:T(8,128)(2,1)} %get-tuple-element.715) | copy-start | bytes 3145732
  224.5 294.8 %all-gather.24.cloned.1.call-start = ((), (), s32[]{:S(2)}) async-start(), calls=%async_computation.16 | async-start | bytes 2621440 | tf_op jit(solution)/shard_map/all_gather | solution.py:150
  225.2 414.9 %all-gather.26.cloned.1.call-start = ((), (), s32[]{:S(2)}) async-start(), calls=%async_computation.17 | async-start | bytes 2621440 | tf_op jit(solution)/shard_map/all_gather | solution.py:152
  226.0 476.6 %all-gather.28.cloned.1.call-start = ((), (), s32[]{:S(2)}) async-start(), calls=%async_computation.18 | async-start | bytes 10485760 | tf_op jit(solution)/shard_map/all_gather | solution.py:153
  226.7 625.2 %all-gather.30.cloned.1.call-start = ((), (), s32[]{:S(2)}) async-start(), calls=%async_computation.19 | async-start | bytes 10485760 | tf_op jit(solution)/shard_map/all_gather | solution.py:155
  227.3 1668.7 %reduce-scatter.13.cloned.1.call-start = ((), (), s32[]{:S(2)}) async-start(), calls=%async_computation.20 | async-start | bytes 9437184 | tf_op jit(solution)/shard_map/reduce_scatter | solution.py:299
  227.4 22.7 copy-start.56
  227.4 22.7 copy-start.58
  227.4 22.6 copy-start.94
  229.8 20.3 copy-start.60
  250.6 180.3 %copy-start.2 = (bf16[512,1024]{0,1:T(8,128)(2,1)}, bf16[512,1024]{0,1:T(8,128)(2,1)S(1)}, u32[]{:S(2)}) copy-start(bf16[512,1024]{0,1:T(8,128)(2,1)S(1)} %copy.59) | copy-start | bytes 3145732
  430.9 82.6 %copy-start.10 = (bf16[512,1024]{1,0:T(8,128)(2,1)S(1)}, bf16[512,1024]{1,0:T(8,128)(2,1)}, u32[]{:S(2)}) copy-start(bf16[512,1024]{1,0:T(8,128)(2,1)} %param.29) | copy-start | bytes 3145732
  430.9 82.6 %copy-start.47 = (f32[1,1024]{1,0:T(1,128)S(1)}, f32[1,1024]{1,0:T(1,128)}, u32[]{:S(2)}) copy-start(f32[1,1024]{1,0:T(1,128)} %get-tuple-element.723) | copy-start | bytes 12292
  640.2 62.4 %copy-start.73 = (f32[1,1024]{1,0:T(1,128)S(1)}, f32[1,1024]{1,0:T(1,128)}, u32[]{:S(2)}) copy-start(f32[1,1024]{1,0:T(1,128)} %get-tuple-element.727) | copy-start | bytes 12292
  640.2 62.3 %copy-start.86 = (f32[1,1024]{1,0:T(1,128)S(1)}, f32[1,1024]{1,0:T(1,128)}, u32[]{:S(2)}) copy-start(f32[1,1024]{1,0:T(1,128)} %get-tuple-element.718) | copy-start | bytes 12292
  644.5 244.0 %copy-start.64 = (f32[512]{0:T(512)}, f32[512]{0:T(512)S(1)}, u32[]{:S(2)}) copy-start(f32[512]{0:T(512)S(1)} %broadcast_multiply_fusion) | copy-start | bytes 6148
  646.1 242.4 %copy-start.80 = (f32[512]{0:T(512)}, f32[512]{0:T(512)S(1)}, u32[]{:S(2)}) copy-start(f32[512]{0:T(512)S(1)} %fusion.101) | copy-start | bytes 6148
  702.6 149.3 %copy-start.31 = (bf16[512,1024]{1,0:T(8,128)(2,1)S(1)}, bf16[512,1024]{1,0:T(8,128)(2,1)}, u32[]{:S(2)}) copy-start(bf16[512,1024]{1,0:T(8,128)(2,1)} %param.43) | copy-start | bytes 3145732
  702.6 149.3 %copy-start.48 = (f32[4096]{0:T(1024)S(1)}, f32[4096]{0:T(1024)}, u32[]{:S(2)}) copy-start(f32[4096]{0:T(1024)} %convert_element_type.297) | copy-start | bytes 49156
  851.9 28.4 %copy-start.24 = (f32[512,1024]{1,0:T(8,128)S(1)}, f32[512,1024]{1,0:T(8,128)}, u32[]{:S(2)}) copy-start(f32[512,1024]{1,0:T(8,128)} %copy-done.23) | copy-start | bytes 6291460
  851.9 28.4 %copy-start.102 = (bf16[1024,4096]{1,0:T(8,128)(2,1)S(1)}, bf16[1024,4096]{1,0:T(8,128)(2,1)}, u32[]{:S(2)}) copy-start(bf16[1024,4096]{1,0:T(8,128)(2,1)} %all-gather.28.cloned.1.call-done) | copy-start | bytes 25165828
  1026.9 886.7 %reduce-scatter.21.cloned.1.call-start = ((), (), s32[]{:S(2)}) async-start(), calls=%async_computation.24 | async-start | bytes 2621440 | tf_op jit(solution)/shard_map/reduce_scatter | solution.py:413
  1033.2 880.5 %reduce-scatter.25.cloned.1.call-start = ((), (), s32[]{:S(2)}) async-start(), calls=%async_computation.26 | async-start | bytes 2621440 | tf_op jit(solution)/shard_map/reduce_scatter | solution.py:419
  1039.4 874.3 %reduce-scatter.19.cloned.1.call-start = ((), (), s32[]{:S(2)}) async-start(), calls=%async_computation.23 | async-start | bytes 2621440 | tf_op jit(solution)/shard_map/reduce_scatter | solution.py:410
  1068.0 905.9 %reduce-scatter.17.cloned.1.call-start = ((), (), s32[]{:S(2)}) async-start(), calls=%async_computation.22 | async-start | bytes 7864320 | tf_op jit(solution)/shard_map/reduce_scatter | solution.py:407
  1085.2 17.3 slice-start.2
  1120.9 26.5 %collective-permute-start.1 = (bf16[512,2048]{0,1:T(8,128)(2,1)}, bf16[512,2048]{0,1:T(8,128)(2,1)}, u32[]{:S(2)}, u32[]{:S(2)}) collective-permute-start(bf16[512,2048]{0,1:T(8,128)(2,1)} %fusion.249), channel_id=1, source_target_pairs={{0,28},{4,0},{8,4},{12,8},{16,12},{20,16},{24,20},{28,24},{1,29},{... | collective-permute-start | bytes 6291464 | tf_op jit(solution)/shard_map/while/body/eval_jaxpr/ppermute | solution.py:20
  1123.5 46.3 %collective-permute-start = (bf16[512,2048]{0,1:T(8,128)(2,1)}, bf16[512,2048]{0,1:T(8,128)(2,1)}, u32[]{:S(2)}, u32[]{:S(2)}) collective-permute-start(bf16[512,2048]{0,1:T(8,128)(2,1)} %copy.121), channel_id=1, source_target_pairs={{0,28},{4,0},{8,4},{12,8},{16,12},{20,16},{24,20},{28,24},{1,29},{... | collective-permute-start | bytes 6291464 | tf_op jit(solution)/shard_map/while/body/eval_jaxpr/ppermute | solution.py:20
  1185.6 64.5 %collective-permute-start.1 = (bf16[512,2048]{0,1:T(8,128)(2,1)}, bf16[512,2048]{0,1:T(8,128)(2,1)}, u32[]{:S(2)}, u32[]{:S(2)}) collective-permute-start(bf16[512,2048]{0,1:T(8,128)(2,1)} %fusion.249), channel_id=1, source_target_pairs={{0,28},{4,0},{8,4},{12,8},{16,12},{20,16},{24,20},{28,24},{1,29},{... | collective-permute-start | bytes 6291464 | tf_op jit(solution)/shard_map/while/body/eval_jaxpr/ppermute | solution.py:20
  1226.2 46.3 %collective-permute-start = (bf16[512,2048]{0,1:T(8,128)(2,1)}, bf16[512,2048]{0,1:T(8,128)(2,1)}, u32[]{:S(2)}, u32[]{:S(2)}) collective-permute-start(bf16[512,2048]{0,1:T(8,128)(2,1)} %copy.121), channel_id=1, source_target_pairs={{0,28},{4,0},{8,4},{12,8},{16,12},{20,16},{24,20},{28,24},{1,29},{... | collective-permute-start | bytes 6291464 | tf_op jit(solution)/shard_map/while/body/eval_jaxpr/ppermute | solution.py:20
  1288.2 64.2 %collective-permute-start.1 = (bf16[512,2048]{0,1:T(8,128)(2,1)}, bf16[512,2048]{0,1:T(8,128)(2,1)}, u32[]{:S(2)}, u32[]{:S(2)}) collective-permute-start(bf16[512,2048]{0,1:T(8,128)(2,1)} %fusion.249), channel_id=1, source_target_pairs={{0,28},{4,0},{8,4},{12,8},{16,12},{20,16},{24,20},{28,24},{1,29},{... | collective-permute-start | bytes 6291464 | tf_op jit(solution)/shard_map/while/body/eval_jaxpr/ppermute | solution.py:20
  1328.5 46.3 %collective-permute-start = (bf16[512,2048]{0,1:T(8,128)(2,1)}, bf16[512,2048]{0,1:T(8,128)(2,1)}, u32[]{:S(2)}, u32[]{:S(2)}) collective-permute-start(bf16[512,2048]{0,1:T(8,128)(2,1)} %copy.121), channel_id=1, source_target_pairs={{0,28},{4,0},{8,4},{12,8},{16,12},{20,16},{24,20},{28,24},{1,29},{... | collective-permute-start | bytes 6291464 | tf_op jit(solution)/shard_map/while/body/eval_jaxpr/ppermute | solution.py:20
  1390.5 64.2 %collective-permute-start.1 = (bf16[512,2048]{0,1:T(8,128)(2,1)}, bf16[512,2048]{0,1:T(8,128)(2,1)}, u32[]{:S(2)}, u32[]{:S(2)}) collective-permute-start(bf16[512,2048]{0,1:T(8,128)(2,1)} %fusion.249), channel_id=1, source_target_pairs={{0,28},{4,0},{8,4},{12,8},{16,12},{20,16},{24,20},{28,24},{1,29},{... | collective-permute-start | bytes 6291464 | tf_op jit(solution)/shard_map/while/body/eval_jaxpr/ppermute | solution.py:20
  1430.8 46.3 %collective-permute-start = (bf16[512,2048]{0,1:T(8,128)(2,1)}, bf16[512,2048]{0,1:T(8,128)(2,1)}, u32[]{:S(2)}, u32[]{:S(2)}) collective-permute-start(bf16[512,2048]{0,1:T(8,128)(2,1)} %copy.121), channel_id=1, source_target_pairs={{0,28},{4,0},{8,4},{12,8},{16,12},{20,16},{24,20},{28,24},{1,29},{... | collective-permute-start | bytes 6291464 | tf_op jit(solution)/shard_map/while/body/eval_jaxpr/ppermute | solution.py:20
  1492.9 64.2 %collective-permute-start.1 = (bf16[512,2048]{0,1:T(8,128)(2,1)}, bf16[512,2048]{0,1:T(8,128)(2,1)}, u32[]{:S(2)}, u32[]{:S(2)}) collective-permute-start(bf16[512,2048]{0,1:T(8,128)(2,1)} %fusion.249), channel_id=1, source_target_pairs={{0,28},{4,0},{8,4},{12,8},{16,12},{20,16},{24,20},{28,24},{1,29},{... | collective-permute-start | bytes 6291464 | tf_op jit(solution)/shard_map/while/body/eval_jaxpr/ppermute | solution.py:20
  1533.2 46.3 %collective-permute-start = (bf16[512,2048]{0,1:T(8,128)(2,1)}, bf16[512,2048]{0,1:T(8,128)(2,1)}, u32[]{:S(2)}, u32[]{:S(2)}) collective-permute-start(bf16[512,2048]{0,1:T(8,128)(2,1)} %copy.121), channel_id=1, source_target_pairs={{0,28},{4,0},{8,4},{12,8},{16,12},{20,16},{24,20},{28,24},{1,29},{... | collective-permute-start | bytes 6291464 | tf_op jit(solution)/shard_map/while/body/eval_jaxpr/ppermute | solution.py:20
  1595.2 64.2 %collective-permute-start.1 = (bf16[512,2048]{0,1:T(8,128)(2,1)}, bf16[512,2048]{0,1:T(8,128)(2,1)}, u32[]{:S(2)}, u32[]{:S(2)}) collective-permute-start(bf16[512,2048]{0,1:T(8,128)(2,1)} %fusion.249), channel_id=1, source_target_pairs={{0,28},{4,0},{8,4},{12,8},{16,12},{20,16},{24,20},{28,24},{1,29},{... | collective-permute-start | bytes 6291464 | tf_op jit(solution)/shard_map/while/body/eval_jaxpr/ppermute | solution.py:20
  1635.5 46.3 %collective-permute-start = (bf16[512,2048]{0,1:T(8,128)(2,1)}, bf16[512,2048]{0,1:T(8,128)(2,1)}, u32[]{:S(2)}, u32[]{:S(2)}) collective-permute-start(bf16[512,2048]{0,1:T(8,128)(2,1)} %copy.121), channel_id=1, source_target_pairs={{0,28},{4,0},{8,4},{12,8},{16,12},{20,16},{24,20},{28,24},{1,29},{... | collective-permute-start | bytes 6291464 | tf_op jit(solution)/shard_map/while/body/eval_jaxpr/ppermute | solution.py:20
  1697.5 64.2 %collective-permute-start.1 = (bf16[512,2048]{0,1:T(8,128)(2,1)}, bf16[512,2048]{0,1:T(8,128)(2,1)}, u32[]{:S(2)}, u32[]{:S(2)}) collective-permute-start(bf16[512,2048]{0,1:T(8,128)(2,1)} %fusion.249), channel_id=1, source_target_pairs={{0,28},{4,0},{8,4},{12,8},{16,12},{20,16},{24,20},{28,24},{1,29},{... | collective-permute-start | bytes 6291464 | tf_op jit(solution)/shard_map/while/body/eval_jaxpr/ppermute | solution.py:20
  1737.9 46.3 %collective-permute-start = (bf16[512,2048]{0,1:T(8,128)(2,1)}, bf16[512,2048]{0,1:T(8,128)(2,1)}, u32[]{:S(2)}, u32[]{:S(2)}) collective-permute-start(bf16[512,2048]{0,1:T(8,128)(2,1)} %copy.121), channel_id=1, source_target_pairs={{0,28},{4,0},{8,4},{12,8},{16,12},{20,16},{24,20},{28,24},{1,29},{... | collective-permute-start | bytes 6291464 | tf_op jit(solution)/shard_map/while/body/eval_jaxpr/ppermute | solution.py:20
  1788.8 43.6 %copy-start.5 = (f32[512,16,64]{0,2,1:T(8,128)S(1)}, f32[512,16,64]{0,2,1:T(8,128)}, u32[]{:S(2)}) copy-start(f32[512,16,64]{0,2,1:T(8,128)} %get-tuple-element.447) | copy-start | bytes 6291460
  1793.1 64.2 %copy-start.11 = (bf16[512,1024]{1,0:T(8,128)(2,1)S(1)}, bf16[512,1024]{1,0:T(8,128)(2,1)}, u32[]{:S(2)}) copy-start(bf16[512,1024]{1,0:T(8,128)(2,1)} %param.29) | copy-start | bytes 3145732
  1793.1 64.2 %copy-start.51 = (f32[1,1024]{1,0:T(1,128)S(1)}, f32[1,1024]{1,0:T(1,128)}, u32[]{:S(2)}) copy-start(f32[1,1024]{1,0:T(1,128)} %copy-done.50) | copy-start | bytes 12292
  1793.1 64.2 %copy-start.53 = (f32[512]{0:T(512)S(1)}, f32[512]{0:T(512)}, u32[]{:S(2)}) copy-start(f32[512]{0:T(512)} %copy-done.52) | copy-start | bytes 6148
  1793.1 64.2 %copy-start.71 = (f32[512]{0:T(512)S(1)}, f32[512]{0:T(512)}, u32[]{:S(2)}) copy-start(f32[512]{0:T(512)} %copy-done.70) | copy-start | bytes 6148
  1793.1 64.1 %copy-start.89 = (f32[1,1024]{1,0:T(1,128)S(1)}, f32[1,1024]{1,0:T(1,128)}, u32[]{:S(2)}) copy-start(f32[1,1024]{1,0:T(1,128)} %copy-done.88) | copy-start | bytes 12292
  1793.1 62.8 %collective-permute-start.2 = (bf16[512,2048]{0,1:T(8,128)(2,1)S(1)}, bf16[512,2048]{0,1:T(8,128)(2,1)S(1)}, u32[]{:S(2)}, u32[]{:S(2)}) collective-permute-start(bf16[512,2048]{0,1:T(8,128)(2,1)S(1)} %add_convert_fusion.1), channel_id=1, source_target_pairs={{0,28},{4,0},{8,4},{12,8},{16,12},{20,16},{24,20},{28,24},{1,29},{... | collective-permute-start | bytes 6291464 | tf_op jit(solution)/shard_map/ppermute | solution.py:20
  1864.4 256.7 %reduce-scatter.27.cloned.1.call-start = ((), (), s32[]{:S(2)}) async-start(), calls=%async_computation.27 | async-start | bytes 10485760 | tf_op jit(solution)/shard_map/reduce_scatter | solution.py:422
  1876.0 392.6 %reduce-scatter.29.cloned.1.call-start = ((), (), s32[]{:S(2)}) async-start(), calls=%async_computation.28 | async-start | bytes 10485760 | tf_op jit(solution)/shard_map/reduce_scatter | solution.py:428
  1895.7 453.1 %reduce-scatter.23.cloned.1.call-start = ((), (), s32[]{:S(2)}) async-start(), calls=%async_computation.25 | async-start | bytes 5242880 | tf_op jit(solution)/shard_map/reduce_scatter | solution.py:416
  1900.6 489.7 %reduce-scatter.31.cloned.1.call-start = ((), (), s32[]{:S(2)}) async-start(), calls=%async_computation.29 | async-start | bytes 327680
  1912.0 483.7 %reduce-scatter.15.cloned.1.call-start = ((), (), s32[]{:S(2)}) async-start(), calls=%async_computation.21 | async-start | bytes 40960 | tf_op jit(solution)/shard_map/reduce_scatter | solution.py:404
  1913.6 611.3 %all-reduce.7.cloned.1.call-start = ((), (), s32[]{:S(2)}) async-start(), calls=%async_computation.30 | async-start | bytes 16777216 | tf_op jit(solution)/shard_map/psum | solution.py:441
  (76 other events, 350.2 us)
Sparse Core Ops, SparseCore 0:
  9.6 83.4 all-gather.19
  94.7 113.9 all-gather.11
  211.1 52.5 all-gather.21
  266.1 54.3 all-gather.15
  322.8 89.8 all-gather.13
  414.1 45.8 all-gather.17
  461.6 44.6 all-gather.23
  507.9 44.6 all-gather.25
  554.2 148.3 all-gather.27
  704.0 147.8 all-gather.29
  1027.1 69.4 reduce-scatter.12
  1098.8 43.8 reduce-scatter.20
  1145.0 43.1 reduce-scatter.24
  1190.5 43.1 reduce-scatter.18
  1864.5 109.3 reduce-scatter.16
  1976.1 144.9 reduce-scatter.26
  2123.4 145.1 reduce-scatter.28
  2271.3 77.4 reduce-scatter.22
  2351.8 20.2 reduce-scatter.30
  2374.7 17.0 reduce-scatter.14
  2397.3 127.4 all-reduce.6
where the time goes:
time: 2560 us; the launch traced here: 2550 us
  waiting for transfers between devices  1240 us (48%)
  matrix products  472 us (18%)
  starting transfers between devices  286 us (11%)
  other arithmetic  270 us (11%)
  local copies, waits for them, and re-layouts  164 us (6%)
  blocking collectives  88.4 us (3%)
    ppermute x15, waiting for transfers between devices, from_behind(): return lax.ppermute(value, axis, pairs)  287 us
    ppermute x15, starting transfers between devices, from_behind(): return lax.ppermute(value, axis, pairs)  285 us
    reduce_scatter x1, waiting for transfers between devices, body(): lax.psum_scatter(grad_ffn_out.astype(jnp.bfloat16), 'fsdp', scatter_dimen...  147 us
    reduce_scatter x1, waiting for transfers between devices, body(): lax.psum_scatter(grad_ffn_in.astype(jnp.bfloat16), 'fsdp', scatter_dimens...  147 us
    all_gather x1, waiting for transfers between devices, body(): lax.all_gather(ffn_out, 'fsdp', axis=0, tiled=True)  137 us
    psum x1, waiting for transfers between devices, body(): lax.psum(reduced[5].astype(jnp.bfloat16), 'ctx').astype(jnp.float32)  103 us
    all_gather x1, waiting for transfers between devices, body(): lax.all_gather(self_in, 'fsdp', axis=0, tiled=True)  96.8 us
    reduce_scatter x1, waiting for transfers between devices, body(): lax.psum_scatter(grad_cross_kv.astype(jnp.bfloat16), 'fsdp', scatter_dime...  80.2 us
  transfers between devices with their start and end apart: 36, of which 26 were waited for; matrix products, arithmetic and copies ran while one was open for 28% of the time, Pallas kernels for 0%

commit v1 on v0

v1 whole, which is shorter than its diff:
```python
import functools
import math

import jax
import jax.numpy as jnp
from jax import lax
from jax.experimental import pallas as pl
from jax.experimental.pallas import tpu as pltpu
from jax.sharding import PartitionSpec as P

HEADS = 16
CONT = 2048
EPS = 1e-05
NEG = -1e30
TILE = 512
BF = jnp.bfloat16
F32 = jnp.float32
VMEM_BYTES = 56 * 2**20


def nn(left, right):
    return lax.dot_general(left, right, (((1,), (0,)), ((), ())), preferred_element_type=F32)


def nt(left, right):
    return lax.dot_general(left, right, (((1,), (1,)), ((), ())), preferred_element_type=F32)


def tn(left, right):
    return lax.dot_general(left, right, (((0,), (0,)), ((), ())), preferred_element_type=F32)


def normalize(values):
    center = values - jnp.mean(values, axis=-1, keepdims=True)
    scale = lax.rsqrt(jnp.mean(center * center, axis=-1, keepdims=True) + EPS)
    return center * scale, scale


def normalize_back(unit, scale, gain, grad):
    q = gain * grad
    back = scale * (
        q - jnp.mean(q, axis=-1, keepdims=True) - unit * jnp.mean(q * unit, axis=-1, keepdims=True)
    )
    return back, jnp.sum(grad * unit, axis=0), jnp.sum(grad, axis=0)


def head_lanes(head, array):
    lane = lax.broadcasted_iota(jnp.int32, array.shape, 1)
    keep = (lane < 64) if head == 0 else (lane >= 64)
    return jnp.where(keep, array, jnp.zeros_like(array))


def transposed(array):
    return array.astype(F32).T.astype(BF)


def visible(key_start, query_start, key_count, query_count, own_start, limit):
    key = key_start + lax.broadcasted_iota(jnp.int32, (key_count, query_count), 0)
    query = query_start + lax.broadcasted_iota(jnp.int32, (key_count, query_count), 1)
    shown = key <= query
    if limit is not None:
        shown = shown & ((key >= own_start) | (key < limit))
    return shown


def soften(scores, total, peak, value_t):
    old = peak[:1]
    new = jnp.maximum(old, jnp.max(scores, axis=0, keepdims=True))
    raised = jnp.exp(scores - new).astype(BF)
    total[...] = total[...] * jnp.exp(old - new) + nn(value_t, raised)
    peak[...] = jnp.broadcast_to(new, peak.shape)


def set_value_rows(value_t, head, columns, value):
    value_t[head, :64, columns] = value[64 * head : 64 * head + 64]
    value_t[head, 64:, columns] = jnp.ones((16, value.shape[1]), BF)


def tile_rows(tile):
    return pl.ds(pl.multiple_of(tile * TILE, TILE), TILE)


def flipped_bits(index, mask):
    out, bit = index, 1
    while bit <= mask:
        if mask & bit:
            out = out + bit - 2 * bit * ((index // bit) % 2)
        bit *= 2
    return out


def greet(peers):
    barrier = pltpu.get_barrier_semaphore()
    for peer in peers:
        pl.semaphore_signal(
            barrier, inc=1, device_id=peer, device_id_type=pl.DeviceIdType.MESH
        )
    pl.semaphore_wait(barrier, len(peers))


def others(axis):
    me, count = lax.axis_index(axis), lax.axis_size(axis)
    return [{axis: (me + step) % count} for step in range(1, count)]


def remote(source, target, send_sem, recv_sem, device):
    return pltpu.make_async_remote_copy(
        source, target, send_sem, recv_sem, device_id=device,
        device_id_type=pl.DeviceIdType.MESH,
    )


def exchange(source, target, send_sems, recv_sems, own_sem):
    me, count = lax.axis_index("ctx"), lax.axis_size("ctx")

    def copy(there, slot):
        return remote(
            source.at[there], target.at[slot], send_sems.at[there], recv_sems.at[slot],
            {"ctx": there},
        )

    def send(there):
        @pl.when(there != me)
        def _():
            copy(there, me).start()

        @pl.when(there == me)
        def _():
            pltpu.make_async_copy(source.at[me], target.at[me], own_sem).start()

    def arrived(there):
        @pl.when(there != me)
        def _():
            copy(there, there).wait_recv()

        @pl.when(there == me)
        def _():
            pltpu.make_async_copy(source.at[me], target.at[me], own_sem).wait()

    def sent():
        for step in range(1, count):
            copy((me + step) % count, me).wait_send()

    return send, arrived, sent


def attend_forward_kernel(cross, heads, conts, offs_ref, q_ref, k_ref, v_ref, *refs):
    if cross:
        mixed_ref, att_ref, lse_ref, q_out, *refs = refs
    else:
        mixed_ref, att_ref, lse_ref, *refs = refs
    total, peak, value_t, score_a, score_b, stage, send_sem, recv_sem, own_sem, *refs = refs
    me, count = lax.axis_index("ctx"), lax.axis_size("ctx")
    rows = att_ref.shape[1]
    tiles = rows // TILE
    key_tiles = k_ref.shape[0] // TILE
    prompt = rows - conts * CONT
    prompt_tiles = prompt // TILE
    greet(others("ctx"))
    send, arrived, sent = exchange(stage, mixed_ref, send_sem, recv_sem, own_sem)
    if cross:
        q_all, q_send, q_recv, q_own = refs
        put, got, put_done = exchange(q_ref, q_all, q_send, q_recv, q_own)
        for step in range(count):
            put((me + step) % count)

    for tile in range(key_tiles):
        at = pl.ds(tile * TILE, TILE)
        turned = transposed(v_ref[at, :])
        for head in range(heads):
            set_value_rows(value_t, head, at, turned)

    def query_tile(step, carry):
        if cross:
            i = (me + step) % count
            got(i)
            q = q_all[i]
            q_out[i] = q
        else:
            i = step
            q = q_ref[tile_rows(i), :]
        masked = [head_lanes(head, q) for head in range(heads)]
        total[...] = jnp.zeros_like(total)
        peak[...] = jnp.full_like(peak, NEG)

        def score(j, target):
            k = k_ref[tile_rows(j), :]
            for head in range(heads):
                target[head] = nt(k, masked[head])

        def soft(j, source, shown=None):
            for head in range(heads):
                scores = source[head]
                if shown is not None:
                    scores = jnp.where(shown, scores, NEG)
                soften(
                    scores, total.at[head], peak.at[head], value_t[head, :, tile_rows(j)]
                )

        if cross:
            both = (score_a, score_b)
            score(0, score_a)
            for j in range(key_tiles):
                if j + 1 < key_tiles:
                    score(j + 1, both[(j + 1) % 2])
                soft(j, both[j % 2])
        elif conts == 1:
            score(i, score_a)
            diagonal = visible(0, 0, TILE, TILE, 0, None)

            @pl.when(i > 0)
            def _():
                score(i - 1, score_b)
                soft(i, score_a, diagonal)

            @pl.when(i == 0)
            def _():
                soft(i, score_a, diagonal)

            def two(t, carry):
                j = i - 1 - 2 * t
                score(jnp.maximum(j - 1, 0), score_a)
                soft(j, score_b)
                score(jnp.maximum(j - 2, 0), score_b)
                soft(j - 1, score_a)
                return carry

            lax.fori_loop(0, i // 2, two, 0)

            @pl.when(i % 2 == 1)
            def _():
                soft(0, score_b)
        else:
            cont = jnp.maximum(i * TILE - prompt, 0) // CONT
            inside = i * TILE < prompt
            own = jnp.where(inside, 0, prompt + cont * CONT)
            limit = offs_ref[0, cont]

            def one(j, carry):
                score(j, score_a)
                soft(j, score_a, visible(j * TILE, i * TILE, TILE, TILE, own, limit))
                return carry

            lax.fori_loop(jnp.where(inside, 0, own // TILE), i + 1, one, 0)
            lax.fori_loop(0, jnp.where(inside, 0, prompt_tiles), one, 0)

        for head in range(heads):
            part = total[head]
            att_ref[64 * head : 64 * head + 64, tile_rows(i)] = part[:64] / part[64:65]
            lse_ref[head : head + 1, tile_rows(i)] = peak[head][:1] + jnp.log(part[64:65])
        stage[i] = att_ref[:, tile_rows(i)].T.astype(BF)
        send(i)
        return carry

    if heads < 2:
        att_ref[...] = jnp.zeros_like(att_ref)
    lax.fori_loop(0, tiles, query_tile, 0)
    for step in range(count):
        arrived((me + step) % count)
    sent()
    if cross:
        put_done()


def attend_forward(cross, heads, offsets, q, k, v):
    count = lax.axis_size("ctx")
    rows = count * TILE
    vmem = pl.BlockSpec(memory_space=pltpu.VMEM)
    hbm = pl.BlockSpec(memory_space=pl.ANY)
    dma = pltpu.SemaphoreType.DMA
    tiles = jax.ShapeDtypeStruct((count, TILE, 128), BF)
    outs = [
        tiles,
        jax.ShapeDtypeStruct((128, rows), F32),
        jax.ShapeDtypeStruct((8, rows), F32),
    ]
    scratch = [
        pltpu.VMEM((heads, 80, TILE), F32),
        pltpu.VMEM((heads, 8, TILE), F32),
        pltpu.VMEM((heads, 80, k.shape[0]), BF),
        pltpu.VMEM((heads, TILE, TILE), F32),
        pltpu.VMEM((heads, TILE, TILE), F32),
        pltpu.VMEM((count, TILE, 128), BF),
        dma((count,)), dma((count,)), dma,
    ]
    if cross:
        outs.append(tiles)
        scratch += [pltpu.VMEM((count, TILE, 128), BF), dma((count,)), dma((count,)), dma]
    return pl.pallas_call(
        functools.partial(attend_forward_kernel, cross, heads, offsets.shape[1]),
        out_shape=outs,
        in_specs=[pl.BlockSpec(memory_space=pltpu.SMEM), vmem, vmem, vmem],
        out_specs=[hbm] + [vmem] * (len(outs) - 1),
        scratch_shapes=scratch,
        compiler_params=pltpu.CompilerParams(
            vmem_limit_bytes=VMEM_BYTES, collective_id=2 if cross else 1,
            has_side_effects=True,
        ),
        cost_estimate=pl.CostEstimate(
            flops=40 * 10**9, bytes_accessed=2**23, transcendentals=2**24
        ),
    )(offsets, q, k, v)


def rest_copies(sources, targets, send_sem, recv_sem):
    me = lax.axis_index("ctx")
    half = lax.axis_size("ctx") // 4
    out = []
    for other in range(1, half):
        for part in range(2):
            mine = me // 4 if part == 0 else (me // 2) % half
            sem = len(out)
            out.append(
                remote(
                    sources[part].at[:, :, flipped_bits(mine, other)],
                    targets[part].at[other - 1],
                    send_sem.at[sem], recv_sem.at[sem],
                    {"ctx": flipped_bits(me, (4 if part == 0 else 2) * other)},
                )
            )
    return out


def last_copies(sources, targets, send_sem, recv_sem):
    me, zone = lax.axis_index("ctx"), lax.axis_index("fsdp")
    chips, groups = lax.axis_size("ctx") // 2, lax.axis_size("fsdp")
    out = []
    for other in range(1, chips):
        sem = len(out)
        out.append(
            remote(
                sources[0].at[flipped_bits(me // 2, other)], targets[0].at[other - 1],
                send_sem.at[sem], recv_sem.at[sem], {"ctx": flipped_bits(me, 2 * other)},
            )
        )
    for shift in range(1, groups):
        sem = len(out)
        there = (zone + shift) % groups
        out.append(
            remote(
                sources[1].at[there], targets[1].at[shift - 1],
                send_sem.at[sem], recv_sem.at[sem], {"fsdp": there},
            )
        )
    return out


def attend_backward_kernel(
    cross, heads, conts, scale, carried, offs_ref, q_ref, k_ref, v_ref, do_ref, att_ref,
    lse_ref, *refs,
):
    sources, refs = refs[:2], refs[2:]
    if cross:
        moved_ref, dk_ref, dv_ref, *refs = refs
    else:
        moved_ref, stage, *refs = refs
    targets, refs = refs[:2], refs[2:]
    if cross:
        stage, *refs = refs
    (
        do_all, key_t, delta, dq_sum, dk_sum, dv_sum,
        send_sem, recv_sem, own_sem, do_send, do_recv, do_own, carry_send, carry_recv,
    ) = refs
    me, count = lax.axis_index("ctx"), lax.axis_size("ctx")
    tiles = count
    key_tiles = k_ref.shape[0] // TILE
    prompt = tiles * TILE - conts * CONT
    prompt_tiles = prompt // TILE
    greet(others("ctx") + ([] if cross else others("fsdp")))
    put, got, put_done = exchange(do_ref, do_all, do_send, do_recv, do_own)
    for step in range(count):
        put((me + step) % count)
    carry_copies = carried(sources, targets, carry_send, carry_recv)
    for copy in carry_copies:
        copy.start()
    send, arrived, sent = exchange(stage, moved_ref, send_sem, recv_sem, own_sem)
    dk_sum[...] = jnp.zeros_like(dk_sum)
    dv_sum[...] = jnp.zeros_like(dv_sum)
    for tile in range(key_tiles):
        at = pl.ds(tile * TILE, TILE)
        key_t[:, at] = transposed(k_ref[at, :])

    def query_tile(step, carry):
        i = (me + step) % count if cross else tiles - 1 - step
        q = q_ref[tile_rows(i), :]
        got(i)
        do = do_all[i]
        q_masked = [head_lanes(head, q) for head in range(heads)]
        do_masked = [head_lanes(head, do) for head in range(heads)]
        both = do.astype(F32).T * att_ref[:, tile_rows(i)]
        for head in range(heads):
            delta[head : head + 1, :] = jnp.sum(
                both[64 * head : 64 * head + 64], axis=0, keepdims=True
            )
        dq_sum[...] = jnp.zeros_like(dq_sum)

        def key_step(j, shown):
            at = tile_rows(j)
            k, v = k_ref[at, :], v_ref[at, :]
            for head in range(heads):
                scores = nt(k, q_masked[head])
                weights = jnp.exp(scores - lse_ref[head : head + 1, tile_rows(i)])
                if shown is not None:
                    weights = jnp.where(shown, weights, 0.0)
                weight_grad = nt(v, do_masked[head])
                score_grad = (weights * (weight_grad - delta[head : head + 1, :])).astype(BF)
                dv_sum[at, :] += nn(weights.astype(BF), do_masked[head])
                dk_sum[at, :] += nn(score_grad, q_masked[head])
                own = slice(64 * head, 64 * head + 64)
                dq_sum[own, :] += nn(key_t[own, at], score_grad)

        def plain(j, carry):
            key_step(j, None)
            return carry

        if cross:
            lax.fori_loop(0, key_tiles, plain, 0)
        elif conts == 1:
            key_step(i, visible(0, 0, TILE, TILE, 0, None))
            lax.fori_loop(0, i, plain, 0)
        else:
            cont = jnp.maximum(i * TILE - prompt, 0) // CONT
            inside = i * TILE < prompt
            own = jnp.where(inside, 0, prompt + cont * CONT)
            limit = offs_ref[0, cont]

            def one(j, carry):
                key_step(j, visible(j * TILE, i * TILE, TILE, TILE, own, limit))
                return carry

            lax.fori_loop(jnp.where(inside, 0, own // TILE), i + 1, one, 0)
            lax.fori_loop(0, jnp.where(inside, 0, prompt_tiles), one, 0)

        dq = dq_sum[...].T.astype(BF).astype(F32)
        stage[i, :, :128] = (dq * scale).astype(BF)
        if not cross:
            stage[i, :, 128:256] = dk_sum[tile_rows(i), :].astype(BF)
            stage[i, :, 256:] = dv_sum[tile_rows(i), :].astype(BF)
        send(i)
        return carry

    lax.fori_loop(0, tiles, query_tile, 0)
    if cross:
        dk_ref[...] = dk_sum[...].astype(BF)
        dv_ref[...] = dv_sum[...].astype(BF)
    for step in range(count):
        arrived((me + step) % count)
    sent()
    put_done()
    for copy in carry_copies:
        copy.wait_send()
        copy.wait_recv()


def attend_backward(cross, heads, scale, offsets, q, k, v, do, att, lse, sources, target_shapes):
    count = lax.axis_size("ctx")
    vmem = pl.BlockSpec(memory_space=pltpu.VMEM)
    hbm = pl.BlockSpec(memory_space=pl.ANY)
    dma = pltpu.SemaphoreType.DMA
    keys = k.shape[0]
    wide = 128 if cross else 384
    moved = jax.ShapeDtypeStruct((count, TILE, wide), BF)
    if cross:
        local = [jax.ShapeDtypeStruct((keys, 128), BF)] * 2
        carries = 2 * max(count // 4 - 1, 1)
    else:
        local = [jax.ShapeDtypeStruct((count, TILE, wide), BF)]
        carries = count // 2 - 1 + lax.axis_size("fsdp") - 1
    targets = [jax.ShapeDtypeStruct(shape, BF) for shape in target_shapes]
    return pl.pallas_call(
        functools.partial(
            attend_backward_kernel, cross, heads, offsets.shape[1], scale,
            rest_copies if cross else last_copies,
        ),
        out_shape=[moved] + local + targets,
        in_specs=[pl.BlockSpec(memory_space=pltpu.SMEM)] + [vmem] * 6 + [hbm] * 2,
        out_specs=[hbm] + [vmem] * len(local) + [hbm] * 2,
        scratch_shapes=([pltpu.VMEM((count, TILE, wide), BF)] if cross else [])
        + [
            pltpu.VMEM((count, TILE, 128), BF),
            pltpu.VMEM((128, keys), BF),
            pltpu.VMEM((8, TILE), F32),
            pltpu.VMEM((128, TILE), F32),
            pltpu.VMEM((keys, 128), F32),
            pltpu.VMEM((keys, 128), F32),
            dma((count,)), dma((count,)), dma,
            dma((count,)), dma((count,)), dma,
            dma((carries,)), dma((carries,)),
        ],
        compiler_params=pltpu.CompilerParams(
            vmem_limit_bytes=VMEM_BYTES, collective_id=3 if cross else 4,
            has_side_effects=True,
        ),
        cost_estimate=pl.CostEstimate(
            flops=60 * 10**9, bytes_accessed=2**23, transcendentals=2**24
        ),
    )(offsets, q, k, v, do, att, lse, *sources)


def ffn_kernel(
    steps, groups, n_ref, dy_ref, base_ref, bias_ref, win_ref, wout_ref,
    out_ref, gn_ref, gb_ref, in_ref, sum_ref,
    n_t, own_in, own_out, post_in, post_out, got_in, got_out,
    keep_in, keep_out, flow_in, flow_out, near_in, near_out,
    send_sem, recv_sem, flow_send, flow_recv, save_sem,
):
    f = pl.program_id(0)
    me = lax.axis_index("ctx")
    count = lax.axis_size("ctx")
    chips = count // 2
    core = me % 2
    low_bit = (me // 2) % 2
    high_bit = me // chips
    cols = keep_in.shape[2]
    slot = f % 2
    sibling = {"ctx": flipped_bits(me, 1)}
    low = {"ctx": flipped_bits(me, 2)}
    high = {"ctx": flipped_bits(me, chips)}

    def copies(step, place):
        return (
            remote(post_in.at[place], got_in.at[step], send_sem.at[0, place],
                   recv_sem.at[0, step], sibling),
            remote(post_out.at[place], got_out.at[step], send_sem.at[1, place],
                   recv_sem.at[1, step], sibling),
        )

    def flows(step, place):
        return (
            remote(flow_in.at[place], near_in.at[step], flow_send.at[0, place],
                   flow_recv.at[0, step], low),
            remote(flow_out.at[place], near_out.at[step], flow_send.at[1, place],
                   flow_recv.at[1, step], high),
        )

    @pl.when(f == 0)
    def _():
        greet([sibling, low, high])
        n_t[...] = transposed(n_ref[...])
        gn_ref[...] = jnp.zeros_like(gn_ref)
        out_ref[...] = base_ref[...]

    @pl.when(f < steps)
    def _():
        @pl.when(f >= 2)
        def _():
            for copy in copies(jnp.maximum(f - 2, 0), slot):
                copy.wait_send()

        pre = nn(n_ref[...], win_ref[...]) + bias_ref[0, :1]
        below = 0.5 * (1.0 + lax.erf(pre * (1.0 / math.sqrt(2.0))))
        hidden = (pre * below).astype(BF)
        out_ref[...] += nn(hidden, wout_ref[...])
        slope = below + pre * (jnp.exp(-0.5 * pre * pre) * (1.0 / math.sqrt(2.0 * math.pi)))
        dy = dy_ref[...]
        grad_pre = (nt(dy, wout_ref[...]) * slope).astype(BF)
        gb_ref[0] = jnp.broadcast_to(
            jnp.sum(grad_pre.astype(F32), axis=0, keepdims=True), gb_ref.shape[1:]
        )
        gn_ref[...] += nt(grad_pre, win_ref[...])

        def split(part, keep, post, half):
            left, right = part[:, :half], part[:, half:]
            keep[slot] = jnp.where(core == 0, left, right)
            post[slot] = jnp.where(core == 0, right, left).astype(BF)

        first, second = copies(jnp.minimum(f, steps - 1), slot)
        split(nn(n_t[...], grad_pre), own_in, post_in, cols)
        first.start()
        split(tn(hidden, dy), own_out, post_out, 2 * cols)
        second.start()

    @pl.when(f > 0)
    def _():
        past = jnp.maximum(f - 1, 0)
        place = (f + 1) % 2
        for copy in copies(past, place):
            copy.wait_recv()

        @pl.when(f >= 3)
        def _():
            for copy in flows(jnp.maximum(f - 3, 0), place):
                copy.wait_send()

        unit = keep_in.shape[1] // (groups * (chips // 2))
        for slab in range(groups * (chips // 2)):
            for kept in (True, False):
                take = low_bit if kept else 1 - low_bit
                rows = pl.ds(pl.multiple_of((2 * slab + take) * unit, unit), unit)
                both = own_in[place, rows, :] + got_in[past, rows, :].astype(F32)
                at = slice(unit * slab, unit * slab + unit)
                if kept:
                    keep_in[past, at, :] = both.astype(BF)
                else:
                    flow_in[place, at, :] = both.astype(BF)
        unit = n_t.shape[0] // groups // 2
        for slab in range(own_out.shape[1] // (2 * unit)):
            for kept in (True, False):
                take = high_bit if kept else 1 - high_bit
                rows = pl.ds(pl.multiple_of((2 * slab + take) * unit, unit), unit)
                both = own_out[place, rows, :] + got_out[past, rows, :].astype(F32)
                at = slice(unit * slab, unit * slab + unit)
                for half in range(2):
                    value = both[:, half * cols : half * cols + cols].astype(BF)
                    if kept:
                        keep_out[past, half, at, :] = value
                    else:
                        flow_out[place, half, at, :] = value
        for copy in flows(past, place):
            copy.start()

    @pl.when(f == steps)
    def _():
        for back in (2, 1):
            for copy in copies(steps - back, (steps - back) % 2):
                copy.wait_send()
            for copy in flows(steps - back, (steps - back) % 2):
                copy.wait_send()
        per = steps // sum_ref.shape[0]
        height = keep_out.shape[2]

        def saves(step):
            rows = pl.ds(pl.multiple_of((step % per) * height, height), height)
            return (
                pltpu.make_async_copy(
                    keep_in.at[step], in_ref.at[step], save_sem.at[0, step]
                ),
                pltpu.make_async_copy(
                    keep_out.at[step], sum_ref.at[step // per, :, rows], save_sem.at[1, step]
                ),
            )

        def join(step, carry):
            for copy in flows(step, step % 2):
                copy.wait_recv()
            keep_in[step] = (
                keep_in[step].astype(F32) + near_in[step].astype(F32)
            ).astype(BF)
            keep_out[step] = (
                keep_out[step].astype(F32) + near_out[step].astype(F32)
            ).astype(BF)
            for copy in saves(step):
                copy.start()
            return carry

        def saved(step, carry):
            for copy in saves(step):
                copy.wait()
            return carry

        lax.fori_loop(0, steps, join, 0)
        lax.fori_loop(0, steps, saved, 0)


def ffn(normed, dy, base, bias, weights):
    rows, width = normed.shape
    hidden = weights.shape[1] // 2
    groups = lax.axis_size("fsdp")
    step = 512
    cols = step // 2
    steps = hidden // step
    per = width // step
    last = steps - 1

    def now(f):
        return jnp.minimum(f, last)

    whole = lambda f: (0, 0)
    hbm = pl.BlockSpec(memory_space=pl.ANY)
    dma = pltpu.SemaphoreType.DMA
    once = pl.BlockSpec((rows, width), whole, pipeline_mode=pl.Buffered(1))
    return pl.pallas_call(
        functools.partial(ffn_kernel, steps, groups),
        grid=(steps + 1,),
        out_shape=(
            jax.ShapeDtypeStruct((rows, width), F32),
            jax.ShapeDtypeStruct((rows, width), F32),
            jax.ShapeDtypeStruct((steps, 8, step), F32),
            jax.ShapeDtypeStruct((steps, width // 2, cols), BF),
            jax.ShapeDtypeStruct((hidden // width, 2, width // 2, cols), BF),
        ),
        in_specs=[
            once, once, once,
            pl.BlockSpec((1, 8, step), lambda f: (now(f), 0, 0)),
            pl.BlockSpec((width, step), lambda f: (0, now(f))),
            pl.BlockSpec(
                (step, width), lambda f: (now(f) % per, hidden // width + now(f) // per)
            ),
        ],
        out_specs=(
            pl.BlockSpec((rows, width), whole),
            pl.BlockSpec((rows, width), whole),
            pl.BlockSpec((1, 8, step), lambda f: (now(f), 0, 0)),
            hbm, hbm,
        ),
        scratch_shapes=[
            pltpu.VMEM((width, rows), BF),
            pltpu.VMEM((2, width, cols), F32),
            pltpu.VMEM((2, step, 2 * cols), F32),
            pltpu.VMEM((2, width, cols), BF),
            pltpu.VMEM((2, step, 2 * cols), BF),
            pltpu.VMEM((steps, width, cols), BF),
            pltpu.VMEM((steps, step, 2 * cols), BF),
            pltpu.VMEM((steps, width // 2, cols), BF),
            pltpu.VMEM((steps, 2, step // 2, cols), BF),
            pltpu.VMEM((2, width // 2, cols), BF),
            pltpu.VMEM((2, 2, step // 2, cols), BF),
            pltpu.VMEM((steps, width // 2, cols), BF),
            pltpu.VMEM((steps, 2, step // 2, cols), BF),
            dma((2, 2)), dma((2, steps)), dma((2, 2)), dma((2, steps)), dma((2, steps)),
        ],
        compiler_params=pltpu.CompilerParams(
            vmem_limit_bytes=60 * 2**20, collective_id=0, has_side_effects=True
        ),
        cost_estimate=pl.CostEstimate(
            flops=30 * 10**9, bytes_accessed=2**26, transcendentals=2**22
        ),
    )(normed, dy, base, bias, weights, weights)


def token_grad_kernel(
    own, moved_ref, wq_ref, wk_ref, wv_ref, tokens_ref, gain_ref, first_ref, out_ref
):
    step = pl.program_id(0)

    @pl.when(step == 0)
    def _():
        out_ref[...] = jnp.zeros_like(out_ref)

    grads = moved_ref[0]
    total = out_ref[...]
    for part, weight in enumerate((wq_ref, wk_ref, wv_ref)):
        total = total + nt(grads[:, part * 128 : part * 128 + own], weight[...])
    out_ref[...] = total

    @pl.when(step == pl.num_programs(0) - 1)
    def _():
        unit, scale = normalize(tokens_ref[...].astype(F32))
        q = gain_ref[...] * out_ref[...]
        mean = jnp.mean(q, axis=-1, keepdims=True)
        slant = jnp.mean(q * unit, axis=-1, keepdims=True)
        out_ref[...] = first_ref[...] + scale * (q - mean - unit * slant)


def token_grad(moved, weights, tokens, gain, first):
    ctx, rows, wide = moved.shape
    width = tokens.shape[1]
    own = width // ctx
    if own < 128:
        cut = moved.reshape(ctx, rows, 3, 128)[:, :, :, :own]
        grads = jnp.transpose(cut, (1, 2, 0, 3)).reshape(rows, 3 * width)
        unit, scale = normalize(tokens.astype(F32))
        return first + normalize_back(unit, scale, gain, nt(grads, weights))[0]
    whole = pl.BlockSpec((rows, width), lambda s: (0, 0))
    return pl.pallas_call(
        functools.partial(token_grad_kernel, own),
        grid=(ctx,),
        out_shape=jax.ShapeDtypeStruct((rows, width), F32),
        in_specs=[
            pl.BlockSpec((1, rows, wide), lambda s: (s, 0, 0)),
            pl.BlockSpec((width, own), lambda s: (0, s)),
            pl.BlockSpec((width, own), lambda s: (0, ctx + s)),
            pl.BlockSpec((width, own), lambda s: (0, 2 * ctx + s)),
            whole,
            pl.BlockSpec((1, width), lambda s: (0, 0)),
            whole,
        ],
        out_specs=whole,
        compiler_params=pltpu.CompilerParams(vmem_limit_bytes=VMEM_BYTES),
        cost_estimate=pl.CostEstimate(flops=10**10, bytes_accessed=2**24, transcendentals=0),
    )(moved, weights, weights, weights, tokens, gain, first)


def swap(value, bit):
    count = lax.axis_size("ctx")
    return lax.ppermute(value, "ctx", [(i, i ^ bit) for i in range(count)])


def across_groups(value):
    count = lax.axis_size("fsdp")
    me = lax.axis_index("fsdp")
    total = lax.dynamic_index_in_dim(value, me, 0, keepdims=False).astype(F32)
    for shift in range(1, count):
        send = lax.dynamic_index_in_dim(value, (me + shift) % count, 0, keepdims=False)
        got = lax.ppermute(send, "fsdp", [(i, (i + shift) % count) for i in range(count)])
        total = total + got.astype(F32)
    return total


def pair_product(left, right):
    core = lax.axis_index("ctx") % 2
    half = right.shape[1] // 2
    send = tn(left, lax.dynamic_slice_in_dim(right, (1 - core) * half, half, 1)).astype(BF)
    got = swap(send, 1).astype(F32)
    kept = tn(left, lax.dynamic_slice_in_dim(right, core * half, half, 1))
    return (kept + got).astype(BF)


def ctx_gather(value):
    count = lax.axis_size("ctx")
    full = lax.all_gather(value, "ctx", axis=0)
    return full.reshape((count // 2, 2) + value.shape)


def gather_all(pieces):
    count = lax.axis_size("ctx")
    me = lax.axis_index("ctx")
    rows = pieces[0].shape[0] // count
    cut = [lax.dynamic_slice_in_dim(p, me * rows, rows, 0) for p in pieces]
    joined = jnp.concatenate(cut, axis=1)
    full = lax.all_gather(joined, ("fsdp", "ctx"), axis=0, tiled=True)
    out, at = [], 0
    for p in pieces:
        out.append(full[:, at : at + p.shape[1]])
        at += p.shape[1]
    return out


def gather_ffn(ffn_in, ffn_out):
    count = lax.axis_size("ctx")
    groups = lax.axis_size("fsdp")
    me = lax.axis_index("ctx")
    depth, hidden = ffn_in.shape
    width = ffn_out.shape[1]
    blocks = hidden // width
    rows = depth // count
    left = lax.dynamic_slice_in_dim(ffn_in, me * rows, rows, 0)
    left = left.reshape(rows, groups, blocks, depth)
    left = jnp.transpose(left, (0, 2, 1, 3)).reshape(rows, hidden)
    right = lax.dynamic_index_in_dim(
        ffn_out.reshape(blocks, count, rows, width), me, 1, keepdims=False
    )
    right = jnp.moveaxis(right, 0, 1).reshape(rows, hidden)
    joined = jnp.concatenate([left, right], axis=1)
    return lax.all_gather(joined, ("fsdp", "ctx"), axis=0, tiled=True)


def body(
    tokens, encoder_out, prompt_offsets, gains, shifts, self_in, self_out, cross_q, cross_kv,
    cross_out, ffn_in, ffn_bias, ffn_out, out_bias, cotangent,
):
    row_count, width = tokens.shape
    head_dim = width // HEADS
    scale = 1.0 / math.sqrt(head_dim)
    ctx = lax.axis_size("ctx")
    groups = lax.axis_size("fsdp")
    me = lax.axis_index("ctx")
    heads = HEADS // ctx
    own = heads * head_dim

    shard = gains.shape[1]
    small = jnp.concatenate(
        [gains, shifts, out_bias[None], ffn_bias.reshape(-1, shard)], axis=0
    )
    small = lax.all_gather(small, "fsdp", axis=0).astype(F32)
    vectors = jnp.moveaxis(small[:, :13], 0, 1).reshape(13, width)
    gain, shift, full_out_bias = vectors[:3], vectors[3:12], vectors[12]
    full_ffn_bias = small[:, 13:].reshape(-1)

    head_in = lax.dynamic_index_in_dim(
        self_in.reshape(self_in.shape[0], 3, ctx, own), me, 2, keepdims=False
    )
    head_in = lax.all_gather(head_in, "fsdp", axis=0, tiled=True)
    my_shift = lax.dynamic_index_in_dim(shift[3:5].reshape(2, ctx, own), me, 1, keepdims=False)
    all_tokens = lax.all_gather(tokens, "ctx", axis=0, tiled=True)
    all_encoder = lax.all_gather(encoder_out, "ctx", axis=0, tiled=True)
    full_self_out, full_cross_q, full_cross_kv, full_cross_out = gather_all(
        [self_out, cross_q, cross_kv, cross_out]
    )
    ffn_weights = gather_ffn(ffn_in, ffn_out)
    (full_self_in,) = gather_all([self_in])

    all_unit, _ = normalize(all_tokens.astype(F32))
    all_normed = (all_unit * gain[0] + shift[0]).astype(BF)
    projected = nn(all_normed, head_in.reshape(width, 3 * own))

    def lanes(value):
        gap = [(0, 0)] * (value.ndim - 1) + [(0, 128 - own)]
        return value if own == 128 else jnp.pad(value, gap)

    queries = lanes((scale * (projected[:, :own] + my_shift[0])).astype(BF))
    keys = lanes(projected[:, own : 2 * own].astype(BF))
    values = lanes((projected[:, 2 * own :] + my_shift[1]).astype(BF))
    mixed_heads, att_self, lse_self = attend_forward(
        False, heads, prompt_offsets, queries, keys, values
    )

    def to_rows(value):
        return jnp.moveaxis(value[:, :, :own], 0, 1).reshape(row_count, width)

    def to_heads(value):
        return lanes(jnp.moveaxis(value.reshape(row_count, ctx, own), 1, 0))

    mixed = to_rows(mixed_heads)
    token_values = tokens.astype(F32)
    first = token_values + nn(mixed, full_self_out) + shift[5]
    unit_two, scale_two = normalize(first)
    normed_two = (unit_two * gain[1] + shift[1]).astype(BF)
    cross_queries = (scale * (nn(normed_two, full_cross_q) + shift[6])).astype(BF)
    head_kv = lax.dynamic_index_in_dim(
        full_cross_kv.reshape(width, 2, ctx, own), me, 2, keepdims=False
    ).reshape(width, 2 * own)
    enc_shift = lax.dynamic_slice_in_dim(shift[7], me * own, own, 0)
    enc_projected = nn(all_encoder, head_kv)
    enc_keys = lanes(enc_projected[:, :own].astype(BF))
    enc_values = lanes((enc_projected[:, own:] + enc_shift).astype(BF))
    cross_heads, att_cross, lse_cross, all_cross_q = attend_forward(
        True, heads, prompt_offsets, to_heads(cross_queries), enc_keys, enc_values
    )
    cross_mixed = to_rows(cross_heads)
    second = first + nn(cross_mixed, full_cross_out) + shift[8]
    unit_three, scale_three = normalize(second)
    normed_three = (unit_three * gain[2] + shift[2]).astype(BF)
    depth = ffn_in.shape[0]
    blocks = ffn_in.shape[1] // width
    order = full_ffn_bias.reshape(groups, blocks, depth)
    order = jnp.moveaxis(order, 0, 1).reshape(-1, 1, 512)
    layer_sum, grad_three, bias_parts, in_sum, out_sum = ffn(
        normed_three, cotangent, second + full_out_bias,
        jnp.broadcast_to(order, (order.shape[0], 8, 512)), ffn_weights,
    )
    layer_out = layer_sum.astype(BF)
    chips = ctx // 2
    part = depth // chips
    in_sum = in_sum.reshape(-1, groups, chips // 2, part, 256)
    out_sum = out_sum.reshape(-1, groups, chips // 2, part, 256)

    dy = cotangent.astype(F32)
    back_three = normalize_back(unit_three, scale_three, gain[2], grad_three)
    grad_second = dy + back_three[0]
    branch_two = grad_second.astype(BF)
    middle = [pair_product(cross_mixed, branch_two)]
    grad_cross_mixed = nt(branch_two, full_cross_out).astype(BF)
    got_shape = (max(chips // 2 - 1, 1),) + in_sum.shape[:2] + in_sum.shape[3:]
    cross_moved, cross_dk, cross_dv, in_got, out_got = attend_backward(
        True, heads, scale, prompt_offsets, all_cross_q.reshape(-1, 128), enc_keys, enc_values,
        to_heads(grad_cross_mixed), att_cross, lse_cross, (in_sum, out_sum),
        (got_shape, got_shape),
    )

    def joined(value, mine, dim, got):
        kept = lax.dynamic_index_in_dim(value, mine, dim, keepdims=False).astype(F32)
        return kept + jnp.sum(got.astype(F32), axis=0)

    cross_dq = to_rows(cross_moved)
    back_two = normalize_back(unit_two, scale_two, gain[1], nt(cross_dq, full_cross_q))
    grad_first = grad_second + back_two[0]
    branch_one = grad_first.astype(BF)
    grad_mixed = nt(branch_one, full_self_out).astype(BF)
    middle.append(pair_product(normed_two, cross_dq))
    middle.append(pair_product(mixed, branch_one))
    middle = jnp.stack([m.reshape(groups, chips, part, -1) for m in middle])
    middle = jnp.moveaxis(middle, 2, 0)
    ffn_sums = jnp.concatenate(
        [
            joined(in_sum, me // 4, 2, in_got),
            joined(out_sum, (me // 2) % (chips // 2), 2, out_got),
        ],
        axis=0,
    )
    ffn_sums = jnp.moveaxis(ffn_sums.astype(BF), 1, 0)
    moved, grad_heads, middle_got, ffn_got = attend_backward(
        False, heads, scale, prompt_offsets, queries, keys, values, to_heads(grad_mixed),
        att_self, lse_self, (middle, ffn_sums),
        ((chips - 1,) + middle.shape[1:], (groups - 1,) + ffn_sums.shape[1:]),
    )
    zone = lax.axis_index("fsdp")
    ffn_sums = joined(ffn_sums, zone, 0, ffn_got).astype(BF)
    middle = joined(middle, me // 2, 0, middle_got).astype(BF)
    input_grad = token_grad(moved, full_self_in, tokens, gain[:1], grad_first)
    grad_heads = grad_heads.reshape(-1, 3, 128)[:, :, :own].reshape(-1, 3 * own)

    in_sum, out_sum = jnp.split(ctx_gather(ffn_sums), 2, axis=2)
    grad_ffn_in = jnp.transpose(in_sum, (0, 3, 2, 1, 4)).reshape(depth, blocks, groups, depth)
    grad_ffn_in = jnp.swapaxes(grad_ffn_in, 1, 2).reshape(depth, -1).astype(F32)
    out_sum = out_sum.reshape(chips, 2, blocks, 2, part, -1)
    grad_ffn_out = jnp.transpose(out_sum, (2, 0, 4, 1, 3, 5)).reshape(-1, width).astype(F32)

    grad_head_in = tn(all_normed, grad_heads)
    enc_heads = jnp.concatenate([cross_dk[:, :own], cross_dv[:, :own]], axis=1)
    grad_head_kv = tn(all_encoder, enc_heads)
    column = jnp.sum(grad_heads.astype(F32), axis=0)
    weight = head_in.reshape(width, 3 * own).astype(F32)
    grad_shift_one = jnp.sum(weight * column, axis=1)
    grad_gain_one = jnp.sum(weight * (grad_head_in - shift[0][:, None] * column), axis=1) / gain[0]

    def spread(value):
        return lax.dynamic_update_slice_in_dim(jnp.zeros((width,), F32), value, me * own, 0)

    totals = jnp.stack(
        [
            grad_gain_one, back_two[1], back_three[1],
            grad_shift_one, back_two[2], back_three[2],
            spread(column[:own]), spread(column[2 * own :]),
            jnp.sum(branch_one.astype(F32), axis=0),
            jnp.sum(cross_dq.astype(F32), axis=0),
            spread(jnp.sum(enc_heads[:, own:].astype(F32), axis=0)),
            jnp.sum(branch_two.astype(F32), axis=0),
            jnp.sum(dy, axis=0),
        ]
    )
    totals = jnp.moveaxis(totals.reshape(13, groups, shard), 1, 0).reshape(groups, -1)
    bias = jnp.moveaxis(bias_parts[:, 0].reshape(blocks, groups, depth), 0, 1)
    totals = jnp.concatenate([totals, bias.reshape(groups, -1)], axis=1)
    count = totals.shape[1]
    totals = jnp.pad(totals, ((0, 0), (0, 80 * own - count))).reshape(groups, 16, 5 * own)
    late = jnp.concatenate([grad_head_in, grad_head_kv], axis=1).reshape(groups, depth, 5 * own)
    late = jnp.concatenate([late, totals], axis=1)
    late = across_groups(late.astype(BF)).astype(BF)
    middle = across_groups(jnp.moveaxis(middle, 1, 0)).astype(BF)
    packed = jnp.concatenate([late.reshape(-1, own), middle.reshape(-1, own)], axis=0)
    packed = ctx_gather(packed)
    rows = 5 * (depth + 16)
    late = packed[:, :, :rows].reshape(ctx, depth + 16, 5, own)
    heads_in = jnp.transpose(late[:, :depth], (1, 2, 0, 3)).reshape(depth, 5 * width)
    heads_in = heads_in.astype(F32)
    grad_self_in, grad_cross_kv = heads_in[:, : 3 * width], heads_in[:, 3 * width :]
    sums = jnp.sum(late[:, depth:].astype(F32), axis=0).reshape(-1)[:count]
    mine, grad_ffn_bias = sums[: 13 * shard].reshape(13, shard), sums[13 * shard :]
    middle = packed[:, :, rows:].reshape(chips, 2, 3, part, width // 2)
    middle = jnp.transpose(middle, (2, 0, 3, 1, 4)).reshape(3, depth, width).astype(F32)

    enc_sum = enc_heads.reshape(ctx, -1, 2 * own)
    enc_sum = lax.all_to_all(enc_sum, "ctx", split_axis=0, concat_axis=0, tiled=True)
    enc_sum = jnp.transpose(enc_sum.reshape(ctx, -1, 2, own), (1, 2, 0, 3))
    grad_encoder = nt(enc_sum.reshape(-1, 2 * width), full_cross_kv)
    return (
        layer_out, input_grad, grad_encoder, mine[:3], mine[3:12], grad_self_in, middle[2],
        middle[1], grad_cross_kv, middle[0], grad_ffn_in, grad_ffn_bias, grad_ffn_out, mine[12],
    )


def solution(mesh):
    rows = P(("fsdp", "ctx"), None)
    shard = P("fsdp", None)
    thin = P(None, "fsdp")
    flat = P("fsdp")
    return jax.shard_map(
        body,
        mesh=mesh,
        in_specs=(
            rows, rows, shard, thin, thin, shard, shard, shard, shard, shard, shard, flat, shard,
            flat, rows,
        ),
        out_specs=(
            rows, rows, rows, thin, thin, shard, shard, shard, shard, shard, shard, flat, shard,
            flat,
        ),
        check_vma=False,
    )
```

time: 2560 us -> 818 us (0.32)
  waiting for transfers between devices: 1240 us -> 178 us
  matrix products: 472 us -> 57.2 us
  Pallas kernels: 0 us -> 340 us
  starting transfers between devices: 286 us -> 14.1 us
  other arithmetic: 270 us -> 54.7 us
  blocking collectives: 88.4 us -> 32.6 us
  local copies, waits for them, and re-layouts: 164 us -> 114 us
    reduce_scatter x9 -> x0, waiting for transfers between devices: 435 us -> none  [the longest x1 147 us: body(): lax.psum_scatter(grad_ffn_out.astype(jnp.bfloat16), 'fsdp', scatter_dimen...]
    dot_general x56 -> x17, matrix products: 472 us -> 57.2 us  [the longest x8 24 us: tn(): lax.dot_general(left, right, (((0,), (0,)), ((), ())), preferred_element_...]
    pallas_call x0 -> x6, Pallas kernels: none -> 340 us  [the longest x2 165 us: attend_backward(): pl.pallas_call(functools.partial(attend_backward_kernel, cross, heads, of...]
    all_gather x10 -> x7, waiting for transfers between devices: 410 us -> 135 us  [the longest x1 69.4 us: gather_ffn(): return lax.all_gather(joined, ('fsdp', 'ctx'), axis=0, tiled=True)]
    ppermute x15 -> x9, starting transfers between devices: 285 us -> 10.3 us  [the longest x6 9.69 us: across_groups(): lax.ppermute(send, 'fsdp', [(i, (i + shift) % count) for i in range(count)])]
    ppermute x15 -> x9, waiting for transfers between devices: 287 us -> 26.2 us  [the longest x6 26.2 us: across_groups(): lax.ppermute(send, 'fsdp', [(i, (i + shift) % count) for i in range(count)])]
    psum x1 -> x0, waiting for transfers between devices: 103 us -> none  [body(): lax.psum(reduced[5].astype(jnp.bfloat16), 'ctx').astype(jnp.float32)]
    convert_element_type x31 -> x13, other arithmetic: 105 us -> 18 us  [the longest x1 3.34 us: body(): all_normed = (all_unit * gain[0] + shift[0]).astype(BF)]
  transfers between devices with their start and end apart: 36 -> 17, of which waited for: 26 -> 9; matrix products, arithmetic and copies ran while one was open for 28% -> 22% of each run, Pallas kernels for 0% -> 42%
where the time goes in v1:
time: 818 us; the launch traced here: 807 us
  Pallas kernels  340 us (42%)
  waiting for transfers between devices  178 us (22%)
  local copies, waits for them, and re-layouts  114 us (14%)
  matrix products  57.2 us (7%)
  other arithmetic  54.7 us (7%)
  blocking collectives  32.6 us (4%)
  between operations  16.3 us (2%)
  starting transfers between devices  14.1 us (2%)
    pallas_call x2, Pallas kernels, attend_backward(): pl.pallas_call(functools.partial(attend_backward_kernel, cross, heads, of...  165 us
    pallas_call x2, Pallas kernels, attend_forward(): pl.pallas_call(functools.partial(attend_forward_kernel, cross, heads, off...  81.3 us
    pallas_call x1, Pallas kernels, ffn(): pl.pallas_call(functools.partial(ffn_kernel, steps, groups), grid=(steps...  79.4 us
    all_gather x1, waiting for transfers between devices, gather_ffn(): return lax.all_gather(joined, ('fsdp', 'ctx'), axis=0, tiled=True)  69.4 us
    all_gather x2, waiting for transfers between devices, gather_all(): full = lax.all_gather(joined, ('fsdp', 'ctx'), axis=0, tiled=True)  37.3 us
    unnamed x142, local copies, waits for them, and re-layouts  30.8 us
    ppermute x6, waiting for transfers between devices, across_groups(): lax.ppermute(send, 'fsdp', [(i, (i + shift) % count) for i in range(count)])  26.2 us
    dot_general x8, matrix products, tn(): lax.dot_general(left, right, (((0,), (0,)), ((), ())), preferred_element_...  24 us
  transfers between devices with their start and end apart: 17, of which 9 were waited for; matrix products, arithmetic and copies ran while one was open for 22% of the time, Pallas kernels for 42%

profile of v1, /device:TPU:0, one launch (start us, length us, event | category | flops | bytes accessed | tf_op | source)
XLA Modules:
  0.0 807.2 jit_solution(13457141159650614214)
XLA Ops:
  16.8 14.7 %all-gather.3 = bf16[4,17,256]{2,1,0:T(8,128)(2,1)S(1)} all-gather(bf16[1,17,256]{2,1,0:T(8,128)(2,1)S(1)} %maximum_bitcast_fusion), channel_id=2, replica_groups=mesh['ctx'=8,'fsdp'=4] {'fsdp'}, dimensions={0}, use_global_device_ids=true | all-gather | bytes 43520 | tf_op jit(solution)/shard_map/all_gather | solution.py:855
  32.2 1.7 copy.181
  34.7 17.9 %all-gather.1 = bf16[1024,3,1,128]{0,3,1,2:T(8,128)(2,1)S(1)} all-gather(bf16[256,3,1,128]{0,3,1,2:T(8,128)(2,1)S(1)} %copy.175), channel_id=3, replica_groups=mesh['ctx'=8,'fsdp'=4] {'fsdp'}, dimensions={0}, use_global_device_ids=true | all-gather | bytes 983040 | tf_op jit(solution)/shard_map/all_gather | solution.py:863
  53.5 13.5 %all-gather.12.cloned.1.call-done = bf16[4096,1024]{1,0:T(8,128)(2,1)} async-done(((bf16[512,1024]{1,0:T(8,128)(2,1)}), bf16[4096,1024]{1,0:T(8,128)(2,1)}) %all-gather.12.cloned.1.call-update) | async-done | bytes 8388624 | tf_op jit(solution)/shard_map/all_gather | solution.py:865
  67.0 4.7 convert_reduce_fusion
  72.8 2.8 fusion.2
  75.6 3.3 fusion.5
  79.0 4.6 fusion.93
  86.3 35.8 %shard_map.254 = (bf16[8,512,128]{2,1,0:T(8,128)(2,1)}, f32[128,4096]{1,0:T(8,128)}, f32[8,4096]{1,0:T(8,128)}) custom-call(s32[1,1]{1,0:T(1,128)S(6)} %copy.229.offs_ref, bf16[4096,128]{1,0:T(8,128)(2,1)} %get-tuple-element.113.q_ref, bf16[4096,128]{1,0:T(8,128)(2,1)} %slice.323.k_ref, bf16[4096,128]{1,0:T(8,128)(2,1)} %get-tuple-element.112.v_ref), custom_call_target="tpu_custom_call" | custom-call | flops 40000000000 | bytes 8388608 | tf_op jit(solution)/shard_map/pallas_call | solution.py:289
  122.1 2.7 copy.141
  124.8 37.3 %all-gather.14.cloned.1.call-done = bf16[1024,5120]{1,0:T(8,128)(2,1)} async-done(((bf16[32,5120]{1,0:T(8,128)(2,1)}), bf16[1024,5120]{1,0:T(8,128)(2,1)}) %all-gather.14.cloned.1.call-update) | async-done | bytes 10485776 | tf_op jit(solution)/shard_map/all_gather | solution.py:811
  162.2 3.3 fusion.91
  167.8 2.9 multiply_convert_fusion
  172.6 4.8 slice.237
  177.4 6.4 copy.176
  185.0 14.3 %all-gather.16.cloned.1.call-done = bf16[2048,1024]{1,0:T(8,128)(2,1)} async-done(((bf16[256,1024]{1,0:T(8,128)(2,1)}), bf16[2048,1024]{1,0:T(8,128)(2,1)}) %all-gather.16.cloned.1.call-update) | async-done | bytes 4194320 | tf_op jit(solution)/shard_map/all_gather | solution.py:866
  199.3 3.5 convolution_bitcast_fusion
  204.5 45.6 %shard_map.255 = (bf16[8,512,128]{2,1,0:T(8,128)(2,1)}, f32[128,4096]{1,0:T(8,128)}, f32[8,4096]{1,0:T(8,128)}, bf16[8,512,128]{2,1,0:T(8,128)(2,1)}) custom-call(s32[1,1]{1,0:T(1,128)S(6)} %copy.229.offs_ref, bf16[8,512,128]{2,1,0:T(8,128)(2,1)} %bitcast.257, bf16[2048,128]{1,0:T(8,128)(2,1)} %slice.324.k_ref, bf16[2048,128]{1,0:T(8,128)(2,1)} %fusion.39.v_ref), custom_call_target="tpu_custom_call" | custom-call | flops 40000000000 | bytes 8388608 | tf_op jit(solution)/shard_map/pallas_call | solution.py:289
  251.6 4.0 fusion.92
  256.0 2.2 broadcast_add_fusion
  258.1 69.4 %all-gather.18.cloned.1.call-done.win_ref.wout_ref = bf16[1024,8192]{1,0:T(8,128)(2,1)} async-done(((bf16[32,8192]{1,0:T(8,128)(2,1)}), bf16[1024,8192]{1,0:T(8,128)(2,1)}) %all-gather.18.cloned.1.call-update) | async-done | bytes 16777232 | tf_op jit(solution)/shard_map/all_gather | solution.py:835
  328.2 79.4 %shard_map.256 = (f32[512,1024]{1,0:T(8,128)}, f32[512,1024]{1,0:T(8,128)}, f32[8,8,512]{2,1,0:T(8,128)}, bf16[8,512,256]{2,1,0:T(8,128)(2,1)}, bf16[4,2,512,256]{3,2,1,0:T(8,128)(2,1)}) custom-call(bf16[512,1024]{1,0:T(8,128)(2,1)} %get-tuple-element.122.n_ref, bf16[512,1024]{1,0:T(8,128)(2,1)} %dy_ref.1, f32[512,1024]{1,0:T(8,128)} %get-tuple-element.121.base_ref, ...), custom_call_target="tpu_custom_call" | custom-call | flops 30000001024 | bytes 67108864 | tf_op jit(solution)/shard_map/pallas_call | solution.py:672
  407.7 2.6 multiply_reduce_fusion
  410.3 2.2 fusion.86
  413.5 2.9 fusion.29
  418.4 1.8 convolution_convert_fusion.2
  420.2 62.1 %shard_map.257 = (bf16[8,512,128]{2,1,0:T(8,128)(2,1)}, bf16[2048,128]{1,0:T(8,128)(2,1)}, bf16[2048,128]{1,0:T(8,128)(2,1)}, bf16[1,8,4,64,256]{4,3,2,1,0:T(8,128)(2,1)}, bf16[1,8,4,64,256]{4,3,2,1,0:T(8,128)(2,1)}) custom-call(s32[1,1]{1,0:T(1,128)S(6)} %copy.229.offs_ref, bf16[4096,128]{1,0:T(8,128)(2,1)} %bitcast.293, bf16[2048,128]{1,0:T(8,128)(2,1)} %slice.324.k_ref, ...), custom_call_target="tpu_custom_call" | custom-call | flops 60000002048 | bytes 8388608 | tf_op jit(solution)/shard_map/pallas_call | solution.py:470
  482.3 2.4 copy.151
  484.7 2.9 convolution_convert_fusion.1
  487.8 3.8 multiply_reduce_fusion.1
  491.6 2.1 fusion.87
  493.7 1.7 convolution_convert_fusion
  496.8 3.8 fusion.26
  509.7 1.9 add_convert_fusion.2
  511.7 2.1 add_convert_fusion.1
  513.9 2.0 add_convert_fusion
  515.8 3.2 fusion.90
  519.0 103.0 %shard_map.258 = (bf16[8,512,384]{2,1,0:T(8,128)(2,1)}, bf16[8,512,384]{2,1,0:T(8,128)(2,1)}, bf16[3,3,4,64,512]{4,3,2,1,0:T(8,128)(2,1)}, bf16[3,16,64,256]{3,2,1,0:T(8,128)(2,1)}) custom-call(s32[1,1]{1,0:T(1,128)S(6)} %copy.229.offs_ref, bf16[4096,128]{1,0:T(8,128)(2,1)} %get-tuple-element.113.q_ref, bf16[4096,128]{1,0:T(8,128)(2,1)} %slice.323.k_ref, ...), custom_call_target="tpu_custom_call" | custom-call | flops 60000002048 | bytes 8388608 | tf_op jit(solution)/shard_map/pallas_call | solution.py:470
  622.0 1.8 convert_reduce_fusion.3
  624.9 3.6 fusion.38
  629.7 8.0 multiply_reduce_fusion.8
  638.1 2.2 convert_reduce_fusion.2
  645.1 2.2 collective-permute-start.7
  647.3 2.0 collective-permute-start.8
  652.7 3.8 collective-permute-start.5
  656.5 9.4 %collective-permute-done.7 = bf16[3,64,512]{2,1,0:T(8,128)(2,1)S(1)} collective-permute-done((bf16[3,64,512]{2,1,0:T(8,128)(2,1)}, bf16[3,64,512]{2,1,0:T(8,128)(2,1)S(1)}, u32[]{:S(2)}, u32[]{:S(2)}) %collective-permute-start.7) | collective-permute-done | bytes 196640 | tf_op jit(solution)/shard_map/ppermute | solution.py:785
  668.5 14.2 %collective-permute-done.4 = bf16[272,640]{1,0:T(8,128)(2,1)} collective-permute-done((bf16[272,640]{1,0:T(8,128)(2,1)}, bf16[272,640]{1,0:T(8,128)(2,1)}, u32[]{:S(2)}, u32[]{:S(2)}) %collective-permute-start.4) | collective-permute-done | bytes 348192 | tf_op jit(solution)/shard_map/ppermute | solution.py:785
  686.4 3.6 all-to-all-start
  690.6 2.7 convert_element_type.251
  693.3 15.9 %all-to-all-done = bf16[8,256,256]{1,2,0:T(8,128)(2,1)S(1)} async-done(((bf16[8,256,256]{1,2,0:T(8,128)(2,1)}), bf16[8,256,256]{1,2,0:T(8,128)(2,1)S(1)}, u32[]{:S(2)}, u32[]{:S(2)}) %all-to-all-start) | async-done | bytes 1048608 | tf_op jit(solution)/shard_map/all_to_all | solution.py:1024
  709.3 4.5 fusion.84
  713.7 14.3 %shard_map.259 = f32[512,1024]{1,0:T(8,128)} custom-call(bf16[8,512,384]{2,1,0:T(8,128)(2,1)} %get-tuple-element.49.moved_ref, bf16[1024,3072]{1,0:T(8,128)(2,1)} %all-gather.20.cloned.1.call-done.wq_ref.wk_ref.wv_ref, bf16[1024,3072]{1,0:T(8,128)(2,1)} %all-gather.20.cloned.1.call-done.wq_ref.wk_ref.wv_ref, ...), custom_call_target="tpu_custom_call" | custom-call | flops 10000000000 | bytes 16777216 | tf_op jit(solution)/shard_map/pallas_call | solution.py:755
  728.0 3.1 fusion.88
  731.1 2.3 copy.168
  733.4 5.3 copy.169
  738.7 5.6 copy.171
  744.8 5.2 copy.170
  750.1 6.4 reshape.395
  756.5 2.0 slice.248
  758.4 18.4 %copy.164 = bf16[4,2,1360,128]{3,1,0,2:T(2,128)(2,1)S(1)} copy(bf16[4,2,1360,128]{3,2,1,0:T(8,128)(2,1)S(1)} %slice.248) | data formatting | bytes 5570560 | tf_op jit(solution)/shard_map/slice | solution.py:1014
  778.1 2.0 slice.253
  781.7 3.3 slice_convert_fusion.2
  787.4 4.6 reshape.396
  792.1 2.2 fusion.89
  (279 shorter events, 67.3 us)
Async XLA Ops:
  7.2 6.5 copy-start
  7.2 59.8 %all-gather.12.cloned.1.call-start = ((), (), s32[]{:S(2)}) async-start(), calls=%async_computation.1 | async-start | bytes 9437184 | tf_op jit(solution)/shard_map/all_gather | solution.py:865
  7.9 154.2 %all-gather.14.cloned.1.call-start = ((), (), s32[]{:S(2)}) async-start(), calls=%async_computation.2 | async-start | bytes 10813440 | tf_op jit(solution)/shard_map/all_gather | solution.py:811
  11.4 187.9 %all-gather.16.cloned.1.call-start = ((), (), s32[]{:S(2)}) async-start(), calls=%async_computation.3 | async-start | bytes 4718592 | tf_op jit(solution)/shard_map/all_gather | solution.py:866
  12.1 315.4 %all-gather.18.cloned.1.call-start = ((), (), s32[]{:S(2)}) async-start(), calls=%async_computation.4 | async-start | bytes 17301504 | tf_op jit(solution)/shard_map/all_gather | solution.py:835
  13.5 3.2 copy-start.51
  13.5 3.2 copy-start.52
  13.5 3.2 copy-start.49
  13.5 3.2 copy-start.50
  14.9 698.8 %all-gather.20.cloned.1.call-start = ((), (), s32[]{:S(2)}) async-start(), calls=%async_computation.5 | async-start | bytes 6488064 | tf_op jit(solution)/shard_map/all_gather | solution.py:811
  16.6 711.4 %all-gather.22.cloned.1.call-start = ((), (), s32[]{:S(2)}) async-start(), calls=%async_computation.6 | async-start | bytes 4718592 | tf_op jit(solution)/shard_map/all_gather | solution.py:801
  32.2 43.4 %copy-start.47 = (f32[1,2,4,128]{3,1,2,0:T(2,128)}, f32[1,2,4,128]{3,1,2,0:T(2,128)S(1)}, u32[]{:S(2)}) copy-start(f32[1,2,4,128]{3,1,2,0:T(2,128)S(1)} %copy.180) | copy-start | bytes 12292
  52.6 26.4 %copy-start.10 = (bf16[1024,3,1,128]{0,3,1,2:T(8,128)(2,1)}, bf16[1024,3,1,128]{0,3,1,2:T(8,128)(2,1)S(1)}, u32[]{:S(2)}) copy-start(bf16[1024,3,1,128]{0,3,1,2:T(8,128)(2,1)S(1)} %all-gather.1) | copy-start | bytes 2359300
  53.3 112.6 %copy-start.40 = (f32[1,2,4,128]{3,1,2,0:T(2,128)}, f32[1,2,4,128]{3,1,2,0:T(2,128)S(1)}, u32[]{:S(2)}) copy-start(f32[1,2,4,128]{3,1,2,0:T(2,128)S(1)} %copy.183) | copy-start | bytes 12292
  67.0 5.8 copy-start.2
  79.0 4.6 copy-start.5
  122.1 40.1 %copy-start.17 = (bf16[512,1024]{1,0:T(8,128)(2,1)S(1)}, bf16[512,1024]{1,0:T(8,128)(2,1)}, u32[]{:S(2)}) copy-start(bf16[512,1024]{1,0:T(8,128)(2,1)} %tokens_ref.1) | copy-start | bytes 3145732
  165.5 1.3 copy-start.3
  165.5 1.3 copy-start.42
  251.6 166.8 %copy-start.23 = (bf16[512,8,128]{0,2,1:T(8,128)(2,1)}, bf16[512,8,128]{0,2,1:T(8,128)(2,1)S(1)}, u32[]{:S(2)}) copy-start(bf16[512,8,128]{0,2,1:T(8,128)(2,1)S(1)} %copy.146) | copy-start | bytes 3145732
  407.6 2.7 copy-start.6
  407.7 2.7 copy-start.29
  416.9 1.5 copy-start.31
  420.2 87.9 %collective-permute-start = (bf16[1024,512]{1,0:T(8,128)(2,1)}, bf16[1024,512]{1,0:T(8,128)(2,1)}, u32[]{:S(2)}, u32[]{:S(2)}) collective-permute-start(bf16[1024,512]{1,0:T(8,128)(2,1)} %convolution_convert_fusion.2), channel_id=1, source_target_pairs={{0,4},{4,0},{8,12},{12,8},{16,20},{20,16},{24,28},{28,24},{1,5},{5... | collective-permute-start | bytes 3145736 | tf_op jit(solution)/shard_map/ppermute | solution.py:776
  482.3 2.5 copy-start.21
  482.3 5.5 copy-start.4
  482.3 5.4 copy-start.41
  482.3 5.4 copy-start.43
  482.3 5.4 copy-start.45
  484.7 3.0 copy-start.25
  487.6 4.0 copy-start.7
  487.6 24.1 %collective-permute-start.1 = (bf16[1024,512]{1,0:T(8,128)(2,1)}, bf16[1024,512]{1,0:T(8,128)(2,1)}, u32[]{:S(2)}, u32[]{:S(2)}) collective-permute-start(bf16[1024,512]{1,0:T(8,128)(2,1)} %convolution_convert_fusion.1), channel_id=1, source_target_pairs={{0,4},{4,0},{8,12},{12,8},{16,20},{20,16},{24,28},{28,24},{1,5},{5... | collective-permute-start | bytes 3145736 | tf_op jit(solution)/shard_map/ppermute | solution.py:776
  491.6 2.1 copy-start.18
  491.6 4.8 copy-start.36
  493.7 3.1 copy-start.33
  493.7 2.2 copy-start.15
  493.7 2.5 copy-start.8
  493.7 2.7 copy-start.28
  495.4 18.4 %collective-permute-start.2 = (bf16[1024,512]{1,0:T(8,128)(2,1)}, bf16[1024,512]{1,0:T(8,128)(2,1)}, u32[]{:S(2)}, u32[]{:S(2)}) collective-permute-start(bf16[1024,512]{1,0:T(8,128)(2,1)} %convolution_convert_fusion), channel_id=1, source_target_pairs={{0,4},{4,0},{8,12},{12,8},{16,20},{20,16},{24,28},{28,24},{1,5},{5... | collective-permute-start | bytes 3145736 | tf_op jit(solution)/shard_map/ppermute | solution.py:776
  500.6 3.0 copy-start.27
  506.2 1.5 copy-start.37
  506.2 1.6 copy-start.16
  507.8 1.4 copy-start.24
  507.8 1.9 copy-start.32
  508.0 116.9 %copy-start.13 = (bf16[2048,256]{1,0:T(8,128)(2,1)}, bf16[2048,256]{1,0:T(8,128)(2,1)S(1)}, u32[]{:S(2)}) copy-start(bf16[2048,256]{1,0:T(8,128)(2,1)S(1)} %constant_dynamic-update-slice_fusion) | copy-start | bytes 3145732
  508.0 3.7 copy-start.22
  508.0 3.7 copy-start.26
  511.6 2.2 copy-start.19
  511.6 2.2 copy-start.34
  624.8 131.6 %all-gather.24.cloned.1.call-start = ((), (), s32[]{:S(2)}) async-start(), calls=%async_computation.7 | async-start | bytes 4902912 | tf_op jit(solution)/shard_map/all_gather | solution.py:801
  624.9 3.7 copy-start.9
  640.4 3.9 copy-start.35
  641.9 2.4 copy-start.12
  642.8 9.9 %collective-permute-start.6 = (bf16[3,64,512]{2,1,0:T(8,128)(2,1)}, bf16[3,64,512]{2,1,0:T(8,128)(2,1)S(1)}, u32[]{:S(2)}, u32[]{:S(2)}) collective-permute-start(bf16[3,64,512]{2,1,0:T(8,128)(2,1)} %get-tuple-element.129), channel_id=1, source_target_pairs={{0,1},{1,2},{2,3},{3,0},{4,5},{5,6},{6,7},{7,4},{8,9},{9,10},{10,1... | collective-permute-start | bytes 589832 | tf_op jit(solution)/shard_map/ppermute | solution.py:785
  645.1 20.7 %collective-permute-start.7 = (bf16[3,64,512]{2,1,0:T(8,128)(2,1)}, bf16[3,64,512]{2,1,0:T(8,128)(2,1)S(1)}, u32[]{:S(2)}, u32[]{:S(2)}) collective-permute-start(bf16[3,64,512]{2,1,0:T(8,128)(2,1)} %get-tuple-element.131), channel_id=1, source_target_pairs={{0,2},{1,3},{2,0},{3,1},{4,6},{5,7},{6,4},{7,5},{8,10},{9,11},{10,... | collective-permute-start | bytes 589832 | tf_op jit(solution)/shard_map/ppermute | solution.py:785
  647.3 18.6 %collective-permute-start.8 = (bf16[3,64,512]{2,1,0:T(8,128)(2,1)}, bf16[3,64,512]{2,1,0:T(8,128)(2,1)S(1)}, u32[]{:S(2)}, u32[]{:S(2)}) collective-permute-start(bf16[3,64,512]{2,1,0:T(8,128)(2,1)} %get-tuple-element.130), channel_id=1, source_target_pairs={{0,3},{1,0},{2,1},{3,2},{4,7},{5,4},{6,5},{7,6},{8,11},{9,8},{10,9... | collective-permute-start | bytes 589832 | tf_op jit(solution)/shard_map/ppermute | solution.py:785
  650.3 18.2 %collective-permute-start.3 = (bf16[272,640]{1,0:T(8,128)(2,1)}, bf16[272,640]{1,0:T(8,128)(2,1)S(1)}, u32[]{:S(2)}, u32[]{:S(2)}) collective-permute-start(bf16[272,640]{1,0:T(8,128)(2,1)} %get-tuple-element.125), channel_id=1, source_target_pairs={{0,1},{1,2},{2,3},{3,0},{4,5},{5,6},{6,7},{7,4},{8,9},{9,10},{10,1... | collective-permute-start | bytes 1044488 | tf_op jit(solution)/shard_map/ppermute | solution.py:785
  650.3 32.4 %collective-permute-start.4 = (bf16[272,640]{1,0:T(8,128)(2,1)}, bf16[272,640]{1,0:T(8,128)(2,1)}, u32[]{:S(2)}, u32[]{:S(2)}) collective-permute-start(bf16[272,640]{1,0:T(8,128)(2,1)} %get-tuple-element.126), channel_id=1, source_target_pairs={{0,2},{1,3},{2,0},{3,1},{4,6},{5,7},{6,4},{7,5},{8,10},{9,11},{10,... | collective-permute-start | bytes 1044488 | tf_op jit(solution)/shard_map/ppermute | solution.py:785
  652.7 13.2 %copy-start.39 = (bf16[3,64,512]{2,1,0:T(8,128)(2,1)}, bf16[3,64,512]{2,1,0:T(8,128)(2,1)S(1)}, u32[]{:S(2)}) copy-start(bf16[3,64,512]{2,1,0:T(8,128)(2,1)S(1)} %collective-permute-done.6) | copy-start | bytes 589828
  652.7 30.0 %collective-permute-start.5 = (bf16[272,640]{1,0:T(8,128)(2,1)}, bf16[272,640]{1,0:T(8,128)(2,1)}, u32[]{:S(2)}, u32[]{:S(2)}) collective-permute-start(bf16[272,640]{1,0:T(8,128)(2,1)} %get-tuple-element.127), channel_id=1, source_target_pairs={{0,3},{1,0},{2,1},{3,2},{4,7},{5,4},{6,5},{7,6},{8,11},{9,8},{10,9... | collective-permute-start | bytes 1044488 | tf_op jit(solution)/shard_map/ppermute | solution.py:785
  667.1 17.9 %copy-start.14 = (bf16[2048,256]{1,0:T(8,128)(2,1)S(1)}, bf16[2048,256]{1,0:T(8,128)(2,1)}, u32[]{:S(2)}) copy-start(bf16[2048,256]{1,0:T(8,128)(2,1)} %copy-done.13) | copy-start | bytes 3145732
  685.1 4.9 copy-start.46
  686.4 22.8 %all-to-all-start = ((bf16[8,256,256]{1,2,0:T(8,128)(2,1)}), bf16[8,256,256]{1,2,0:T(8,128)(2,1)S(1)}, u32[]{:S(2)}, u32[]{:S(2)}) async-start(bf16[8,256,256]{1,2,0:T(8,128)(2,1)} %copy.161), calls=%async_computation | async-start | bytes 2097152 | tf_op jit(solution)/shard_map/all_to_all | solution.py:1024
  798.2 2.0 copy-start.1
  (6 other events, 5.9 us)
Sparse Core Ops, SparseCore 0:
  9.9 57.0 all-gather.11
  70.4 91.6 all-gather.13
  164.1 35.2 all-gather.15
  202.0 125.4 all-gather.17
  330.2 83.8 all-gather.19
  624.9 34.3 all-gather.21
  685.2 50.7 all-gather.23

commit v2 on v1

--- a/solution.py
+++ b/solution.py
@@ -148,7 +148,7 @@
     if cross:
         mixed_ref, att_ref, lse_ref, q_out, *refs = refs
     else:
-        mixed_ref, att_ref, lse_ref, *refs = refs
+        enc_ref, kv_ref, mixed_ref, att_ref, lse_ref, enc_all, kv_all, *refs = refs
     total, peak, value_t, score_a, score_b, stage, send_sem, recv_sem, own_sem, *refs = refs
     me, count = lax.axis_index("ctx"), lax.axis_size("ctx")
     rows = att_ref.shape[1]
@@ -156,8 +156,15 @@
     key_tiles = k_ref.shape[0] // TILE
     prompt = rows - conts * CONT
     prompt_tiles = prompt // TILE
-    greet(others("ctx"))
+    greet(others("ctx") + ([] if cross else others("fsdp")))
     send, arrived, sent = exchange(stage, mixed_ref, send_sem, recv_sem, own_sem)
+    if not cross:
+        gather_send, gather_recv, gather_own = refs
+        first, second, local = gather_copies(
+            enc_ref, kv_ref, enc_all, kv_all, gather_send, gather_recv, gather_own
+        )
+        for copy in first + local:
+            copy.start()
     if cross:
         q_all, q_send, q_recv, q_own = refs
         put, got, put_done = exchange(q_ref, q_all, q_send, q_recv, q_own)
@@ -250,6 +257,16 @@
             lse_ref[head : head + 1, tile_rows(i)] = peak[head][:1] + jnp.log(part[64:65])
         stage[i] = att_ref[:, tile_rows(i)].T.astype(BF)
         send(i)
+        if not cross:
+
+            @pl.when(step == tiles - 2)
+            def _():
+                for copy in local:
+                    copy.wait()
+                for copy in first:
+                    copy.wait_recv()
+                second.start()
+
         return carry
 
     if heads < 2:
@@ -260,9 +277,42 @@
     sent()
     if cross:
         put_done()
-
-
-def attend_forward(cross, heads, offsets, q, k, v):
+    else:
+        for copy in first:
+            copy.wait_send()
+        second.wait()
+
+
+def gather_copies(enc_ref, kv_ref, enc_all, kv_all, send_sem, recv_sem, own_sem):
+    me, zone = lax.axis_index("ctx"), lax.axis_index("fsdp")
+    chip, core = me // 2, me % 2
+    chips, groups = lax.axis_size("ctx") // 2, lax.axis_size("fsdp")
+    first = []
+    for other in range(1, chips):
+        sem = len(first)
+        first.append(
+            remote(enc_ref, enc_all.at[chip, core], send_sem.at[sem], recv_sem.at[sem],
+                   {"ctx": flipped_bits(me, 2 * other)})
+        )
+    for shift in range(1, groups):
+        sem = len(first)
+        first.append(
+            remote(kv_ref, kv_all.at[zone], send_sem.at[sem], recv_sem.at[sem],
+                   {"fsdp": (zone + shift) % groups})
+        )
+    sem = len(first)
+    second = remote(
+        enc_all.at[:, core], enc_all.at[:, core], send_sem.at[sem], recv_sem.at[sem],
+        {"ctx": flipped_bits(me, 1)},
+    )
+    local = [
+        pltpu.make_async_copy(enc_ref, enc_all.at[chip, core], own_sem.at[0]),
+        pltpu.make_async_copy(kv_ref, kv_all.at[zone], own_sem.at[1]),
+    ]
+    return first, second, local
+
+
+def attend_forward(cross, heads, offsets, q, k, v, extra=()):
     count = lax.axis_size("ctx")
     rows = count * TILE
     vmem = pl.BlockSpec(memory_space=pltpu.VMEM)
@@ -286,11 +336,20 @@
     if cross:
         outs.append(tiles)
         scratch += [pltpu.VMEM((count, TILE, 128), BF), dma((count,)), dma((count,)), dma]
+        places = [vmem]
+    else:
+        enc, kv = extra
+        groups = lax.axis_size("fsdp")
+        outs.append(jax.ShapeDtypeStruct((count // 2, 2) + enc.shape, BF))
+        outs.append(jax.ShapeDtypeStruct((groups,) + kv.shape, BF))
+        copies = count // 2 + groups - 1
+        scratch += [dma((copies,)), dma((copies,)), dma((2,))]
+        places = [hbm, hbm]
     return pl.pallas_call(
         functools.partial(attend_forward_kernel, cross, heads, offsets.shape[1]),
         out_shape=outs,
-        in_specs=[pl.BlockSpec(memory_space=pltpu.SMEM), vmem, vmem, vmem],
-        out_specs=[hbm] + [vmem] * (len(outs) - 1),
+        in_specs=[pl.BlockSpec(memory_space=pltpu.SMEM), vmem, vmem, vmem] + [hbm] * len(extra),
+        out_specs=[hbm, vmem, vmem] + places,
         scratch_shapes=scratch,
         compiler_params=pltpu.CompilerParams(
             vmem_limit_bytes=VMEM_BYTES, collective_id=2 if cross else 1,
@@ -299,7 +358,7 @@
         cost_estimate=pl.CostEstimate(
             flops=40 * 10**9, bytes_accessed=2**23, transcendentals=2**24
         ),
-    )(offsets, q, k, v)
+    )(offsets, q, k, v, *extra)
 
 
 def rest_copies(sources, targets, send_sem, recv_sem):
@@ -497,6 +556,134 @@
     )(offsets, q, k, v, do, att, lse, *sources)
 
 
+def project_kernel(
+    own, scale, tokens_ref, small_ref, head_ref, normed_ref, q_ref, k_ref, v_ref,
+    small_all, head_all, all_tokens, staged, token_send, token_recv, part_send, part_recv,
+    own_sem, stage_sem,
+):
+    me, zone = lax.axis_index("ctx"), lax.axis_index("fsdp")
+    count, groups = lax.axis_size("ctx"), lax.axis_size("fsdp")
+    chips = count // 2
+    shard = small_ref.shape[1]
+    sibling = {"ctx": flipped_bits(me, 1)}
+    near = [flipped_bits(me, 2 * other) for other in range(1, chips)]
+    greet([sibling] + [{"ctx": there} for there in near] + others("fsdp"))
+
+    parts = []
+    for shift in range(1, groups):
+        there = {"fsdp": (zone + shift) % groups}
+        for index, (source, target) in enumerate(((small_ref, small_all), (head_ref, head_all))):
+            parts.append(
+                remote(source, target.at[zone], part_send.at[index, shift - 1],
+                       part_recv.at[index, shift - 1], there)
+            )
+    local = [
+        pltpu.make_async_copy(small_ref, small_all.at[zone], own_sem.at[0]),
+        pltpu.make_async_copy(head_ref, head_all.at[zone], own_sem.at[1]),
+        pltpu.make_async_copy(tokens_ref, all_tokens.at[me], own_sem.at[2]),
+    ]
+    for copy in local:
+        copy.start()
+    for copy in parts:
+        copy.start()
+
+    def direct(there, block):
+        return remote(tokens_ref, all_tokens.at[block], token_send.at[there],
+                      token_recv.at[block], {"ctx": there})
+
+    def passed(block):
+        return remote(
+            all_tokens.at[block], all_tokens.at[block], token_send.at[flipped_bits(block, 1)],
+            token_recv.at[block], sibling,
+        )
+
+    for there in near + [flipped_bits(me, 1)]:
+        direct(there, me).start()
+    for copy in local:
+        copy.wait()
+    for copy in parts:
+        copy.wait_recv()
+
+    def row(index):
+        pieces = [small_all[z].astype(F32)[index : index + 1] for z in range(groups)]
+        return jnp.concatenate(pieces, axis=1)
+
+    gain, shift = row(0), row(3)
+    mine = small_all[me // (shard // own)].astype(F32)
+    q_shift = jnp.where(me % 2 == 0, mine[6:7, :own], mine[6:7, own : 2 * own])
+    v_shift = jnp.where(me % 2 == 0, mine[7:8, :own], mine[7:8, own : 2 * own])
+    if own < 128:
+        for ref in (q_ref, k_ref, v_ref):
+            ref[...] = jnp.zeros_like(ref)
+
+    def save(block, place):
+        return pltpu.make_async_copy(staged.at[place], normed_ref.at[block], stage_sem.at[place])
+
+    order = [me, flipped_bits(me, 1)] + near + [flipped_bits(there, 1) for there in near]
+    for step, block in enumerate(order):
+        place = step % 2
+        if step == 1:
+            direct(block, block).wait_recv()
+        elif step >= 2:
+            if step <= chips:
+                direct(block, block).wait_recv()
+                passed(block).start()
+            else:
+                passed(block).wait_recv()
+        if step >= 2:
+            save(order[step - 2], place).wait()
+        unit, _ = normalize(all_tokens[block].astype(F32))
+        staged[place] = (unit * gain + shift).astype(BF)
+        save(block, place).start()
+        total = jnp.zeros((staged.shape[1], 3 * own), F32)
+        for z in range(groups):
+            total = total + nn(staged[place, :, z * shard : z * shard + shard], head_all[z])
+        q_ref[block, :, :own] = (scale * (total[:, :own] + q_shift)).astype(BF)
+        k_ref[block, :, :own] = total[:, own : 2 * own].astype(BF)
+        v_ref[block, :, :own] = (total[:, 2 * own :] + v_shift).astype(BF)
+    for step in (count - 2, count - 1):
+        save(order[step], step % 2).wait()
+    for copy in parts:
+        copy.wait_send()
+    for there in near + [flipped_bits(me, 1)]:
+        direct(there, me).wait_send()
+    for there in near:
+        passed(there).wait_send()
+
+
+def project(own, scale, tokens, small, head_in):
+    count, groups = lax.axis_size("ctx"), lax.axis_size("fsdp")
+    rows, width = tokens.shape
+    vmem = pl.BlockSpec(memory_space=pltpu.VMEM)
+    hbm = pl.BlockSpec(memory_space=pl.ANY)
+    dma = pltpu.SemaphoreType.DMA
+    lanes = jax.ShapeDtypeStruct((count, rows, 128), BF)
+    return pl.pallas_call(
+        functools.partial(project_kernel, own, scale),
+        out_shape=(
+            jax.ShapeDtypeStruct((count, rows, width), BF),
+            lanes, lanes, lanes,
+            jax.ShapeDtypeStruct((groups,) + small.shape, BF),
+            jax.ShapeDtypeStruct((groups,) + head_in.shape, BF),
+        ),
+        in_specs=[hbm, hbm, hbm],
+        out_specs=(hbm,) + (vmem,) * 5,
+        scratch_shapes=[
+            pltpu.VMEM((count, rows, width), BF),
+            pltpu.VMEM((2, rows, width), BF),
+            dma((count,)), dma((count,)),
+            dma((2, groups - 1)), dma((2, groups - 1)),
+            dma((3,)), dma((2,)),
+        ],
+        compiler_params=pltpu.CompilerParams(
+            vmem_limit_bytes=VMEM_BYTES, collective_id=5, has_side_effects=True
+        ),
+        cost_estimate=pl.CostEstimate(
+            flops=50 * 10**9, bytes_accessed=2**25, transcendentals=0
+        ),
+    )(tokens, small, head_in)
+
+
 def ffn_kernel(
     steps, groups, n_ref, dy_ref, base_ref, bias_ref, win_ref, wout_ref,
     out_ref, gn_ref, gb_ref, in_ref, sum_ref,
@@ -771,6 +958,81 @@
     )(moved, weights, weights, weights, tokens, gain, first)
 
 
+def place_ffn_kernel(groups, sum_ref, in_ref, out_ref):
+    chips, _, lead, part, cols = sum_ref.shape
+    steps = lead // 2
+    depth, hidden = in_ref.shape
+    blocks = hidden // (depth * groups)
+    per = steps // blocks
+    span = min(depth, cols)
+    for chip in range(chips):
+        rows = slice(chip * part, chip * part + part)
+        for core in range(2):
+            for f in range(steps):
+                value = sum_ref[chip, core, f].astype(F32)
+                for piece in range(cols // span):
+                    unit = (f % per) * 2 * cols + core * cols + piece * span
+                    at = (unit // depth * blocks + f // per) * depth + unit % depth
+                    in_ref[rows, at : at + span] = value[:, piece * span : piece * span + span]
+            for slab in range(steps):
+                block, half = slab // 2, slab % 2
+                top = block * depth + chip * part
+                at = (core * 2 + half) * cols
+                out_ref[top : top + part, at : at + cols] = sum_ref[
+                    chip, core, steps + slab
+                ].astype(F32)
+
+
+def place_ffn(sums, depth, hidden, rows, width):
+    vmem = pl.BlockSpec(memory_space=pltpu.VMEM)
+    return pl.pallas_call(
+        functools.partial(place_ffn_kernel, width // depth),
+        out_shape=(
+            jax.ShapeDtypeStruct((depth, hidden), F32),
+            jax.ShapeDtypeStruct((rows, width), F32),
+        ),
+        in_specs=[vmem],
+        out_specs=(vmem, vmem),
+        compiler_params=pltpu.CompilerParams(vmem_limit_bytes=VMEM_BYTES),
+        cost_estimate=pl.CostEstimate(flops=0, bytes_accessed=2**24, transcendentals=0),
+    )(sums)
+
+
+def place_late_kernel(tall, sum_ref, self_ref, kv_ref, *refs):
+    ctx, _, own = sum_ref.shape
+    depth, width = refs[0].shape
+    part = depth // (ctx // 2)
+    for src in range(ctx):
+        for k in range(5):
+            target = self_ref if k < 3 else kv_ref
+            at = (k if k < 3 else k - 3) * width + src * own
+            top = k * tall
+            target[:, at : at + own] = sum_ref[src, top : top + depth, :].astype(F32)
+        for w, target in enumerate(refs):
+            for block in range(width // 2 // own):
+                top = 5 * tall + (w * (width // 2 // own) + block) * part
+                at = (src % 2) * (width // 2) + block * own
+                rows = slice(src // 2 * part, src // 2 * part + part)
+                target[rows, at : at + own] = sum_ref[src, top : top + part, :].astype(F32)
+
+
+def place_late(sums, tall, depth, width):
+    vmem = pl.BlockSpec(memory_space=pltpu.VMEM)
+    small = jax.ShapeDtypeStruct((depth, width), F32)
+    return pl.pallas_call(
+        functools.partial(place_late_kernel, tall),
+        out_shape=(
+            jax.ShapeDtypeStruct((depth, 3 * width), F32),
+            jax.ShapeDtypeStruct((depth, 2 * width), F32),
+            small, small, small,
+        ),
+        in_specs=[vmem],
+        out_specs=(vmem,) * 5,
+        compiler_params=pltpu.CompilerParams(vmem_limit_bytes=VMEM_BYTES),
+        cost_estimate=pl.CostEstimate(flops=0, bytes_accessed=2**24, transcendentals=0),
+    )(sums)
+
+
 def swap(value, bit):
     count = lax.axis_size("ctx")
     return lax.ppermute(value, "ctx", [(i, i ^ bit) for i in range(count)])
@@ -852,38 +1114,36 @@
     small = jnp.concatenate(
         [gains, shifts, out_bias[None], ffn_bias.reshape(-1, shard)], axis=0
     )
-    small = lax.all_gather(small, "fsdp", axis=0).astype(F32)
+    small_rows = small.shape[0]
+    small = jnp.pad(small, ((0, 32 - small_rows), (0, 0)))
+
+    head_in = lax.dynamic_index_in_dim(
+        self_in.reshape(self_in.shape[0], 3, ctx, own), me, 2, keepdims=False
+    ).reshape(-1, 3 * own)
+    all_normed, queries, keys, values, small, head_in = project(
+        own, scale, tokens, small, head_in
+    )
+    all_normed = all_normed.reshape(-1, width)
+    queries, keys, values = [x.reshape(-1, 128) for x in (queries, keys, values)]
+    small = small[:, :small_rows].astype(F32)
     vectors = jnp.moveaxis(small[:, :13], 0, 1).reshape(13, width)
     gain, shift, full_out_bias = vectors[:3], vectors[3:12], vectors[12]
     full_ffn_bias = small[:, 13:].reshape(-1)
 
-    head_in = lax.dynamic_index_in_dim(
-        self_in.reshape(self_in.shape[0], 3, ctx, own), me, 2, keepdims=False
-    )
-    head_in = lax.all_gather(head_in, "fsdp", axis=0, tiled=True)
-    my_shift = lax.dynamic_index_in_dim(shift[3:5].reshape(2, ctx, own), me, 1, keepdims=False)
-    all_tokens = lax.all_gather(tokens, "ctx", axis=0, tiled=True)
-    all_encoder = lax.all_gather(encoder_out, "ctx", axis=0, tiled=True)
-    full_self_out, full_cross_q, full_cross_kv, full_cross_out = gather_all(
-        [self_out, cross_q, cross_kv, cross_out]
-    )
+    full_self_out, full_cross_q, full_cross_out = gather_all([self_out, cross_q, cross_out])
     ffn_weights = gather_ffn(ffn_in, ffn_out)
-    (full_self_in,) = gather_all([self_in])
-
-    all_unit, _ = normalize(all_tokens.astype(F32))
-    all_normed = (all_unit * gain[0] + shift[0]).astype(BF)
-    projected = nn(all_normed, head_in.reshape(width, 3 * own))
-
     def lanes(value):
         gap = [(0, 0)] * (value.ndim - 1) + [(0, 128 - own)]
         return value if own == 128 else jnp.pad(value, gap)
 
-    queries = lanes((scale * (projected[:, :own] + my_shift[0])).astype(BF))
-    keys = lanes(projected[:, own : 2 * own].astype(BF))
-    values = lanes((projected[:, 2 * own :] + my_shift[1]).astype(BF))
-    mixed_heads, att_self, lse_self = attend_forward(
-        False, heads, prompt_offsets, queries, keys, values
-    )
+    head_kv = lax.dynamic_index_in_dim(
+        cross_kv.reshape(-1, 2, ctx, own), me, 2, keepdims=False
+    ).reshape(-1, 2 * own)
+    mixed_heads, att_self, lse_self, all_encoder, head_kv = attend_forward(
+        False, heads, prompt_offsets, queries, keys, values, (encoder_out, head_kv)
+    )
+    all_encoder = all_encoder.reshape(-1, width)
+    head_kv = head_kv.reshape(width, 2 * own)
 
     def to_rows(value):
         return jnp.moveaxis(value[:, :, :own], 0, 1).reshape(row_count, width)
@@ -897,9 +1157,6 @@
     unit_two, scale_two = normalize(first)
     normed_two = (unit_two * gain[1] + shift[1]).astype(BF)
     cross_queries = (scale * (nn(normed_two, full_cross_q) + shift[6])).astype(BF)
-    head_kv = lax.dynamic_index_in_dim(
-        full_cross_kv.reshape(width, 2, ctx, own), me, 2, keepdims=False
-    ).reshape(width, 2 * own)
     enc_shift = lax.dynamic_slice_in_dim(shift[7], me * own, own, 0)
     enc_projected = nn(all_encoder, head_kv)
     enc_keys = lanes(enc_projected[:, :own].astype(BF))
@@ -920,6 +1177,8 @@
         jnp.broadcast_to(order, (order.shape[0], 8, 512)), ffn_weights,
     )
     layer_out = layer_sum.astype(BF)
+    late_in, late_kv, grad_three = lax.optimization_barrier((self_in, cross_kv, grad_three))
+    full_self_in, full_cross_kv = gather_all([late_in, late_kv])
     chips = ctx // 2
     part = depth // chips
     in_sum = in_sum.reshape(-1, groups, chips // 2, part, 256)
@@ -959,8 +1218,11 @@
         axis=0,
     )
     ffn_sums = jnp.moveaxis(ffn_sums.astype(BF), 1, 0)
+    grad_rows, full_self_in, full_cross_kv = lax.optimization_barrier(
+        (to_heads(grad_mixed), full_self_in, full_cross_kv)
+    )
     moved, grad_heads, middle_got, ffn_got = attend_backward(
-        False, heads, scale, prompt_offsets, queries, keys, values, to_heads(grad_mixed),
+        False, heads, scale, prompt_offsets, queries, keys, values, grad_rows,
         att_self, lse_self, (middle, ffn_sums),
         ((chips - 1,) + middle.shape[1:], (groups - 1,) + ffn_sums.shape[1:]),
     )
@@ -970,11 +1232,9 @@
     input_grad = token_grad(moved, full_self_in, tokens, gain[:1], grad_first)
     grad_heads = grad_heads.reshape(-1, 3, 128)[:, :, :own].reshape(-1, 3 * own)
 
-    in_sum, out_sum = jnp.split(ctx_gather(ffn_sums), 2, axis=2)
-    grad_ffn_in = jnp.transpose(in_sum, (0, 3, 2, 1, 4)).reshape(depth, blocks, groups, depth)
-    grad_ffn_in = jnp.swapaxes(grad_ffn_in, 1, 2).reshape(depth, -1).astype(F32)
-    out_sum = out_sum.reshape(chips, 2, blocks, 2, part, -1)
-    grad_ffn_out = jnp.transpose(out_sum, (2, 0, 4, 1, 3, 5)).reshape(-1, width).astype(F32)
+    grad_ffn_in, grad_ffn_out = place_ffn(
+        ctx_gather(ffn_sums), depth, ffn_in.shape[1], ffn_out.shape[0], width
+    )
 
     grad_head_in = tn(all_normed, grad_heads)
     enc_heads = jnp.concatenate([cross_dk[:, :own], cross_dv[:, :own]], axis=1)
@@ -1003,30 +1263,31 @@
     bias = jnp.moveaxis(bias_parts[:, 0].reshape(blocks, groups, depth), 0, 1)
     totals = jnp.concatenate([totals, bias.reshape(groups, -1)], axis=1)
     count = totals.shape[1]
-    totals = jnp.pad(totals, ((0, 0), (0, 80 * own - count))).reshape(groups, 16, 5 * own)
-    late = jnp.concatenate([grad_head_in, grad_head_kv], axis=1).reshape(groups, depth, 5 * own)
-    late = jnp.concatenate([late, totals], axis=1)
-    late = across_groups(late.astype(BF)).astype(BF)
-    middle = across_groups(jnp.moveaxis(middle, 1, 0)).astype(BF)
-    packed = jnp.concatenate([late.reshape(-1, own), middle.reshape(-1, own)], axis=0)
-    packed = ctx_gather(packed)
-    rows = 5 * (depth + 16)
-    late = packed[:, :, :rows].reshape(ctx, depth + 16, 5, own)
-    heads_in = jnp.transpose(late[:, :depth], (1, 2, 0, 3)).reshape(depth, 5 * width)
-    heads_in = heads_in.astype(F32)
-    grad_self_in, grad_cross_kv = heads_in[:, : 3 * width], heads_in[:, 3 * width :]
-    sums = jnp.sum(late[:, depth:].astype(F32), axis=0).reshape(-1)[:count]
-    mine, grad_ffn_bias = sums[: 13 * shard].reshape(13, shard), sums[13 * shard :]
-    middle = packed[:, :, rows:].reshape(chips, 2, 3, part, width // 2)
-    middle = jnp.transpose(middle, (2, 0, 3, 1, 4)).reshape(3, depth, width).astype(F32)
-
+    totals = jnp.pad(totals, ((0, 0), (0, 80 * own - count))).reshape(groups, 5, 16, own)
+    late = jnp.concatenate([grad_head_in, grad_head_kv], axis=1)
+    late = jnp.moveaxis(late.reshape(groups, depth, 5, own), 2, 1)
+    late = jnp.concatenate([late, totals], axis=2).astype(BF)
     enc_sum = enc_heads.reshape(ctx, -1, 2 * own)
     enc_sum = lax.all_to_all(enc_sum, "ctx", split_axis=0, concat_axis=0, tiled=True)
+    late, enc_sum = lax.optimization_barrier((late, enc_sum))
+    late = across_groups(late).astype(BF)
+    middle = across_groups(jnp.moveaxis(middle, 1, 0)).astype(BF)
+    middle = jnp.moveaxis(middle.reshape(3, part, -1, own), 2, 1)
+    packed = jnp.concatenate([late.reshape(-1, own), middle.reshape(-1, own)], axis=0)
+    packed = lax.all_gather(packed, "ctx", axis=0)
+    tall = depth + 16
+    grad_self_in, grad_cross_kv, grad_cross_out, grad_cross_q, grad_self_out = place_late(
+        packed, tall, depth, width
+    )
+    sums = packed[:, : 5 * tall].reshape(ctx, 5, tall, own)[:, :, depth:]
+    sums = jnp.sum(sums.astype(F32), axis=0).reshape(-1)[:count]
+    mine, grad_ffn_bias = sums[: 13 * shard].reshape(13, shard), sums[13 * shard :]
+
     enc_sum = jnp.transpose(enc_sum.reshape(ctx, -1, 2, own), (1, 2, 0, 3))
     grad_encoder = nt(enc_sum.reshape(-1, 2 * width), full_cross_kv)
     return (
-        layer_out, input_grad, grad_encoder, mine[:3], mine[3:12], grad_self_in, middle[2],
-        middle[1], grad_cross_kv, middle[0], grad_ffn_in, grad_ffn_bias, grad_ffn_out, mine[12],
+        layer_out, input_grad, grad_encoder, mine[:3], mine[3:12], grad_self_in, grad_self_out,
+        grad_cross_q, grad_cross_kv, grad_cross_out, grad_ffn_in, grad_ffn_bias, grad_ffn_out, mine[12],
     )
 
 

time: 818 us -> 693 us (0.85)
  waiting for transfers between devices: 178 us -> 86.4 us
  Pallas kernels: 340 us -> 429 us
  local copies, waits for them, and re-layouts: 114 us -> 50.9 us
  blocking collectives: 32.6 us -> 0 us
  other arithmetic: 54.7 us -> 36.2 us
    pallas_call x0 -> x3, Pallas kernels: none -> 80.8 us  [the longest x1 68.7 us: project(): pl.pallas_call(functools.partial(project_kernel, own, scale), out_shape=(...]
    all_gather x2, waiting for transfers between devices: 37.3 us -> 0.01 us  [gather_all(): full = lax.all_gather(joined, ('fsdp', 'ctx'), axis=0, tiled=True)]
    all_gather x1, waiting for transfers between devices: 69.4 us -> 35.1 us  [gather_ffn(): return lax.all_gather(joined, ('fsdp', 'ctx'), axis=0, tiled=True)]
    all_gather x2 -> x0, blocking collectives: 32.6 us -> none  [the longest x1 17.9 us: body(): head_in = lax.all_gather(head_in, 'fsdp', axis=0, tiled=True)]
    slice x10 -> x5, local copies, waits for them, and re-layouts: 29.6 us -> 6.63 us  [the longest x3 5.83 us: gather_all(): out.append(full[:, at:at + p.shape[1]])]
    unnamed x142 -> x109, local copies, waits for them, and re-layouts: 30.8 us -> 8.11 us
    convert_element_type x5 -> x1, local copies, waits for them, and re-layouts: 23.8 us -> 1.43 us  [body(): weight = head_in.reshape(width, 3 * own).astype(F32)]
    all_to_all x1, waiting for transfers between devices: 15.9 us -> 0.01 us  [body(): lax.all_to_all(enc_sum, 'ctx', split_axis=0, concat_axis=0, tiled=True)]
  transfers between devices with their start and end apart: 17 -> 15, of which waited for: 9 -> 6; matrix products, arithmetic and copies ran while one was open for 22% -> 17% of each run, Pallas kernels for 42% -> 37%
where the time goes in v2:
time: 693 us; the launch traced here: 682 us
  Pallas kernels  429 us (62%)
  waiting for transfers between devices  86.4 us (12%)
  local copies, waits for them, and re-layouts  50.9 us (7%)
  matrix products  49.7 us (7%)
  other arithmetic  36.2 us (5%)
  between operations  16 us (2%)
  starting transfers between devices  14 us (2%)
    pallas_call x2, Pallas kernels, attend_backward(): pl.pallas_call(functools.partial(attend_backward_kernel, cross, heads, of...  178 us
    pallas_call x2, Pallas kernels, attend_forward(): pl.pallas_call(functools.partial(attend_forward_kernel, cross, heads, off...  90.2 us
    pallas_call x1, Pallas kernels, project(): pl.pallas_call(functools.partial(project_kernel, own, scale), out_shape=(...  68.7 us
    pallas_call x1, Pallas kernels, ffn(): pl.pallas_call(functools.partial(ffn_kernel, steps, groups), grid=(steps...  66.1 us
    all_gather x1, waiting for transfers between devices, gather_ffn(): return lax.all_gather(joined, ('fsdp', 'ctx'), axis=0, tiled=True)  35.1 us
    ppermute x6, waiting for transfers between devices, across_groups(): lax.ppermute(send, 'fsdp', [(i, (i + shift) % count) for i in range(count)])  33.3 us
    dot_general x8, matrix products, tn(): lax.dot_general(left, right, (((0,), (0,)), ((), ())), preferred_element_...  22.7 us
    all_gather x1, waiting for transfers between devices, body(): packed = lax.all_gather(packed, 'ctx', axis=0)  17.9 us
  transfers between devices with their start and end apart: 15, of which 6 were waited for; matrix products, arithmetic and copies ran while one was open for 17% of the time, Pallas kernels for 37%

profile of v2, /device:TPU:0, one launch (start us, length us, event | category | flops | bytes accessed | tf_op | source)
XLA Modules:
  0.0 682.3 jit_solution(1664198375055701057)
XLA Ops:
  7.2 1.0 constant_dynamic-slice_fusion.8
  13.0 1.6 copy.112
  19.5 68.7 %shard_map.254 = (bf16[8,512,1024]{2,1,0:T(8,128)(2,1)}, bf16[8,512,128]{2,1,0:T(8,128)(2,1)}, bf16[8,512,128]{2,1,0:T(8,128)(2,1)}, bf16[8,512,128]{2,1,0:T(8,1...) custom-call(bf16[512,1024]{1,0:T(8,128)(2,1)} %tokens_ref.3, bf16[32,256]{1,0:T(8,128)(2,1)} %fusion.65.small_ref, ...), custom_call_target="tpu_custom_call" | custom-call | flops 49999998976 | bytes 33554432 | tf_op jit(solution)/shard_map/pallas_call | solution.py:661
  88.2 42.4 %shard_map.255 = (bf16[8,512,128]{2,1,0:T(8,128)(2,1)}, f32[128,4096]{1,0:T(8,128)}, f32[8,4096]{1,0:T(8,128)}, bf16[4,2,256,1024]{3,2,1,0:T(8,128)(2,1)}, bf16[4,256,256]{2,1,0:T(8,128)(2,1)}) custom-call(s32[1,1]{1,0:T(1,128)S(6)} %copy.175.offs_ref, bf16[4096,128]{1,0:T(8,128)(2,1)} %bitcast.246, bf16[4096,128]{1,0:T(8,128)(2,1)} %bitcast.248, ...), custom_call_target="tpu_custom_call" | custom-call | flops 40000000000 | bytes 8388608 | tf_op jit(solution)/shard_map/pallas_call | solution.py:348
  130.5 1.5 copy.115
  132.1 4.0 fusion.79
  139.2 3.2 fusion.77
  144.7 2.9 multiply_convert_fusion
  148.1 1.3 copy.117
  149.4 47.9 %shard_map.256 = (bf16[8,512,128]{2,1,0:T(8,128)(2,1)}, f32[128,4096]{1,0:T(8,128)}, f32[8,4096]{1,0:T(8,128)}, bf16[8,512,128]{2,1,0:T(8,128)(2,1)}) custom-call(s32[1,1]{1,0:T(1,128)S(6)} %copy.175.offs_ref, bf16[8,512,128]{2,1,0:T(8,128)(2,1)} %bitcast.202, bf16[2048,128]{1,0:T(8,128)(2,1)} %slice.233.k_ref, bf16[2048,128]{1,0:T(8,128)(2,1)} %fusion.30.v_ref), custom_call_target="tpu_custom_call" | custom-call | flops 40000000000 | bytes 8388608 | tf_op jit(solution)/shard_map/pallas_call | solution.py:348
  197.3 1.5 copy.118
  198.8 4.0 fusion.78
  203.1 2.2 broadcast_add_fusion
  205.3 35.1 %all-gather.9.cloned.1.call-done.win_ref.wout_ref = bf16[1024,8192]{1,0:T(8,128)(2,1)} async-done(((bf16[32,8192]{1,0:T(8,128)(2,1)}), bf16[1024,8192]{1,0:T(8,128)(2,1)}) %all-gather.9.cloned.1.call-update) | async-done | bytes 16777232 | tf_op jit(solution)/shard_map/all_gather | solution.py:1097
  241.1 66.1 %shard_map.257 = (f32[512,1024]{1,0:T(8,128)}, f32[512,1024]{1,0:T(8,128)}, f32[8,8,512]{2,1,0:T(8,128)}, bf16[8,512,256]{2,1,0:T(8,128)(2,1)}, bf16[4,2,512,256]{3,2,1,0:T(8,128)(2,1)}) custom-call(bf16[512,1024]{1,0:T(8,128)(2,1)} %get-tuple-element.119.n_ref, bf16[512,1024]{1,0:T(8,128)(2,1)} %dy_ref.1, f32[512,1024]{1,0:T(8,128)} %get-tuple-element.118.base_ref, ...), custom_call_target="tpu_custom_call" | custom-call | flops 30000001024 | bytes 67108864 | tf_op jit(solution)/shard_map/pallas_call | solution.py:859
  310.0 3.2 multiply_reduce_fusion
  313.2 2.8 fusion.73
  316.9 3.0 fusion.21
  320.6 1.3 copy.123
  322.0 1.7 convolution_convert_fusion.2
  323.6 74.6 %shard_map.258 = (bf16[8,512,128]{2,1,0:T(8,128)(2,1)}, bf16[2048,128]{1,0:T(8,128)(2,1)}, bf16[2048,128]{1,0:T(8,128)(2,1)}, bf16[1,8,4,64,256]{4,3,2,1,0:T(8,128)(2,1)}, bf16[1,8,4,64,256]{4,3,2,1,0:T(8,128)(2,1)}) custom-call(s32[1,1]{1,0:T(1,128)S(6)} %copy.175.offs_ref, bf16[4096,128]{1,0:T(8,128)(2,1)} %bitcast.252, bf16[2048,128]{1,0:T(8,128)(2,1)} %slice.233.k_ref, ...), custom_call_target="tpu_custom_call" | custom-call | flops 60000002048 | bytes 8388608 | tf_op jit(solution)/shard_map/pallas_call | solution.py:529
  398.3 2.4 copy.124
  400.8 2.9 convolution_convert_fusion.1
  404.3 3.9 multiply_reduce_fusion.1
  408.2 2.1 fusion.74
  410.3 1.7 convolution_convert_fusion
  412.0 3.8 fusion.18
  415.8 1.6 copy.125
  417.4 1.3 copy.126
  418.8 1.8 fusion.2
  421.4 1.5 fusion.refs_1_
  423.7 1.9 add_convert_fusion.2
  425.7 2.1 add_convert_fusion.1
  427.8 1.9 add_convert_fusion
  429.7 3.2 fusion.75
  432.9 5.8 slice.186.wq_ref.wk_ref.wv_ref
  438.7 103.1 %shard_map.259 = (bf16[8,512,384]{2,1,0:T(8,128)(2,1)}, bf16[8,512,384]{2,1,0:T(8,128)(2,1)}, bf16[3,3,4,64,512]{4,3,2,1,0:T(8,128)(2,1)}, bf16[3,16,64,256]{3,2,1,0:T(8,128)(2,1)}) custom-call(s32[1,1]{1,0:T(1,128)S(6)} %copy.175.offs_ref, bf16[4096,128]{1,0:T(8,128)(2,1)} %bitcast.247, bf16[4096,128]{1,0:T(8,128)(2,1)} %bitcast.249, ...), custom_call_target="tpu_custom_call" | custom-call | flops 60000002048 | bytes 8388608 | tf_op jit(solution)/shard_map/pallas_call | solution.py:529
  541.8 1.8 convert_reduce_fusion.2
  544.8 1.4 copy.136
  547.8 1.3 copy.146
  549.1 4.3 all-to-all-start
  553.8 3.6 convolution_convert_fusion.3
  558.8 6.9 %fusion.17 = (f32[1024]{0:T(1024)S(1)}, bf16[1024,384,1]{0,1,2:T(8,128)(2,1)S(1)}) fusion(f32[1024,384]{0,1:T(8,128)S(1)} %copy-done.13, f32[384]{0:T(512)S(1)} %convert_reduce_fusion, f32[1024]{0:T(1024)S(1)} %bitcast.237, bf16[8,512,1024]{2,1,0:T(8,128)(2,1)} %get-tuple-element.84, bf16[8,512,384]{2,1,0:T(8,128)(2,1)S(1)} %copy-done.8), kind=kOutput, calls=%fused_computation.49 | convolution fusion | flops 3223190528 | bytes 13903360 | tf_op jit(solution)/shard_map/dot_general | solution.py:30
  565.7 1.4 divide_convert_fusion
  567.2 1.9 reshape.348
  569.0 2.8 copy.135
  572.0 2.2 convert_reduce_fusion.1
  574.2 1.4 fusion.15
  576.5 1.7 collective-permute-start.6
  578.4 2.4 collective-permute-start.7
  580.8 1.5 collective-permute-start.8
  584.3 2.1 collective-permute-done.6
  586.4 2.2 collective-permute-start.5
  588.6 6.3 collective-permute-done.7
  594.9 1.0 fusion.54
  596.0 6.3 collective-permute-done.3
  602.3 18.6 %collective-permute-done.4 = bf16[5,272,128]{2,1,0:T(8,128)(2,1)S(1)} collective-permute-done((bf16[5,272,128]{2,1,0:T(8,128)(2,1)}, bf16[5,272,128]{2,1,0:T(8,128)(2,1)S(1)}, u32[]{:S(2)}, u32[]{:S(2)}) %collective-permute-start.4) | collective-permute-done | bytes 348192 | tf_op jit(solution)/shard_map/ppermute | solution.py:1047
  622.0 2.9 convert_element_type.193
  624.8 1.3 copy.147
  626.2 2.3 fusion.80
  628.5 14.1 %shard_map.260 = f32[512,1024]{1,0:T(8,128)} custom-call(bf16[8,512,384]{2,1,0:T(8,128)(2,1)} %get-tuple-element.82.moved_ref, bf16[1024,3072]{1,0:T(8,128)(2,1)} %slice.186.wq_ref.wk_ref.wv_ref, bf16[1024,3072]{1,0:T(8,128)(2,1)} %slice.186.wq_ref.wk_ref.wv_ref, bf16[1024,3072]{1,0:T(8,128)(2,1)} %slice.186.wq_ref.wk_ref.wv_ref, ...), custom_call_target="tpu_custom_call" | custom-call | flops 10000000000 | bytes 16777216 | tf_op jit(solution)/shard_map/pallas_call | solution.py:942
  642.6 6.1 shard_map.262
  648.7 17.9 %all-gather.15.cloned.1.call-done = bf16[17024,128]{1,0:T(8,128)(2,1)} async-done(((bf16[2128,128]{1,0:T(8,128)(2,1)}), bf16[17024,128]{1,0:T(8,128)(2,1)}) %all-gather.15.cloned.1.call-update) | async-done | bytes 4358160 | tf_op jit(solution)/shard_map/all_gather | solution.py:1277
  666.6 6.1 shard_map.261
  (216 shorter events, 33.8 us)
Async XLA Ops:
  7.2 4.2 copy-start
  7.2 132.0 %all-gather.7.cloned.1.call-start = ((), (), s32[]{:S(2)}) async-start(), calls=%async_computation.1 | async-start | bytes 6488064 | tf_op jit(solution)/shard_map/all_gather | solution.py:1073
  9.8 230.6 %all-gather.9.cloned.1.call-start = ((), (), s32[]{:S(2)}) async-start(), calls=%async_computation.2 | async-start | bytes 17301504 | tf_op jit(solution)/shard_map/all_gather | solution.py:1097
  11.4 1.6 copy-start.12
  12.6 3.8 copy-start.48
  12.6 3.8 copy-start.50
  12.6 3.8 copy-start.14
  12.6 420.3 %all-gather.11.cloned.1.call-start = ((), (), s32[]{:S(2)}) async-start(), calls=%async_computation.3 | async-start | bytes 10813440 | tf_op jit(solution)/shard_map/all_gather | solution.py:1073
  14.5 4.3 copy-start.44
  14.5 4.3 copy-start.49
  132.1 7.1 %copy-start.15 = (bf16[512,8,128]{0,2,1:T(8,128)(2,1)}, bf16[512,8,128]{0,2,1:T(8,128)(2,1)S(1)}, u32[]{:S(2)}) copy-start(bf16[512,8,128]{0,2,1:T(8,128)(2,1)S(1)} %copy.115) | copy-start | bytes 3145732
  132.1 4.8 copy-start.37
  138.2 4.6 copy-start.35
  142.4 1.3 copy-start.2
  142.4 1.3 copy-start.38
  142.8 4.8 copy-start.40
  198.8 123.2 %copy-start.20 = (bf16[512,8,128]{0,2,1:T(8,128)(2,1)}, bf16[512,8,128]{0,2,1:T(8,128)(2,1)S(1)}, u32[]{:S(2)}) copy-start(bf16[512,8,128]{0,2,1:T(8,128)(2,1)S(1)} %copy.118) | copy-start | bytes 3145732
  309.8 332.8 %all-gather.13.cloned.1.call-start = ((), (), s32[]{:S(2)}) async-start(), calls=%async_computation.4 | async-start | bytes 4718592 | tf_op jit(solution)/shard_map/all_gather | solution.py:1063
  309.9 3.2 copy-start.5
  310.0 3.2 copy-start.26
  320.6 1.3 copy-start.28
  323.6 99.3 %collective-permute-start = (bf16[1024,512]{1,0:T(8,128)(2,1)}, bf16[1024,512]{1,0:T(8,128)(2,1)}, u32[]{:S(2)}, u32[]{:S(2)}) collective-permute-start(bf16[1024,512]{1,0:T(8,128)(2,1)} %convolution_convert_fusion.2), channel_id=1, source_target_pairs={{0,4},{4,0},{8,12},{12,8},{16,20},{20,16},{24,28},{28,24},{1,5},{5... | collective-permute-start | bytes 3145736 | tf_op jit(solution)/shard_map/ppermute | solution.py:1038
  398.3 2.5 copy-start.18
  398.3 6.0 copy-start.3
  398.3 6.0 copy-start.36
  398.3 6.0 copy-start.39
  398.3 5.9 copy-start.41
  400.8 3.5 copy-start.22
  403.6 4.5 copy-start.6
  403.6 22.0 %collective-permute-start.1 = (bf16[1024,512]{1,0:T(8,128)(2,1)}, bf16[1024,512]{1,0:T(8,128)(2,1)}, u32[]{:S(2)}, u32[]{:S(2)}) collective-permute-start(bf16[1024,512]{1,0:T(8,128)(2,1)} %convolution_convert_fusion.1), channel_id=1, source_target_pairs={{0,4},{4,0},{8,12},{12,8},{16,20},{20,16},{24,28},{28,24},{1,5},{5... | collective-permute-start | bytes 3145736 | tf_op jit(solution)/shard_map/ppermute | solution.py:1038
  408.2 2.1 copy-start.16
  410.3 1.7 copy-start.30
  412.0 15.8 %collective-permute-start.2 = (bf16[1024,512]{1,0:T(8,128)(2,1)}, bf16[1024,512]{1,0:T(8,128)(2,1)}, u32[]{:S(2)}, u32[]{:S(2)}) collective-permute-start(bf16[1024,512]{1,0:T(8,128)(2,1)} %convolution_convert_fusion), channel_id=1, source_target_pairs={{0,4},{4,0},{8,12},{12,8},{16,20},{20,16},{24,28},{28,24},{1,5},{5... | collective-permute-start | bytes 3145736 | tf_op jit(solution)/shard_map/ppermute | solution.py:1038
  415.8 2.9 copy-start.25
  418.7 1.8 copy-start.24
  418.7 2.2 copy-start.32
  421.4 1.5 copy-start.21
  421.4 2.3 copy-start.29
  422.9 2.8 copy-start.19
  422.9 2.8 copy-start.23
  425.6 2.1 copy-start.31
  543.6 1.2 copy-start.9
  544.6 1.7 copy-start.7
  544.6 1.9 copy-start.46
  544.6 1.9 copy-start.45
  544.6 1.9 copy-start.43
  544.6 1.9 copy-start.42
  544.6 2.9 copy-start.33
  544.8 2.8 copy-start.11
  549.1 29.3 %all-to-all-start = ((bf16[8,256,256]{1,2,0:T(8,128)(2,1)}), bf16[8,256,256]{1,2,0:T(8,128)(2,1)}, u32[]{:S(2)}, u32[]{:S(2)}) async-start(bf16[8,256,256]{1,2,0:T(8,128)(2,1)} %copy.146), calls=%async_computation | async-start | bytes 2097152 | tf_op jit(solution)/shard_map/all_to_all | solution.py:1271
  553.4 113.3 %all-gather.15.cloned.1.call-start = ((), (), s32[]{:S(2)}) async-start(), calls=%async_computation.5 | async-start | bytes 4902912 | tf_op jit(solution)/shard_map/all_gather | solution.py:1277
  553.7 3.7 copy-start.8
  557.4 1.4 copy-start.13
  557.4 1.4 copy-start.47
  575.7 2.6 copy-start.10
  576.5 9.9 %collective-permute-start.6 = (bf16[3,64,512]{2,1,0:T(8,128)(2,1)}, bf16[3,64,512]{2,1,0:T(8,128)(2,1)S(1)}, u32[]{:S(2)}, u32[]{:S(2)}) collective-permute-start(bf16[3,64,512]{2,1,0:T(8,128)(2,1)} %get-tuple-element.124), channel_id=1, source_target_pairs={{0,1},{1,2},{2,3},{3,0},{4,5},{5,6},{6,7},{7,4},{8,9},{9,10},{10,1... | collective-permute-start | bytes 589832 | tf_op jit(solution)/shard_map/ppermute | solution.py:1047
  578.4 16.5 %collective-permute-start.7 = (bf16[3,64,512]{2,1,0:T(8,128)(2,1)}, bf16[3,64,512]{2,1,0:T(8,128)(2,1)S(1)}, u32[]{:S(2)}, u32[]{:S(2)}) collective-permute-start(bf16[3,64,512]{2,1,0:T(8,128)(2,1)} %get-tuple-element.126), channel_id=1, source_target_pairs={{0,2},{1,3},{2,0},{3,1},{4,6},{5,7},{6,4},{7,5},{8,10},{9,11},{10,... | collective-permute-start | bytes 589832 | tf_op jit(solution)/shard_map/ppermute | solution.py:1047
  580.8 14.0 %collective-permute-start.8 = (bf16[3,64,512]{2,1,0:T(8,128)(2,1)S(1)}, bf16[3,64,512]{2,1,0:T(8,128)(2,1)S(1)}, u32[]{:S(2)}, u32[]{:S(2)}) collective-permute-start(bf16[3,64,512]{2,1,0:T(8,128)(2,1)S(1)} %get-tuple-element.125), channel_id=1, source_target_pairs={{0,3},{1,0},{2,1},{3,2},{4,7},{5,4},{6,5},{7,6},{8,11},{9,8},{10,9... | collective-permute-start | bytes 589832 | tf_op jit(solution)/shard_map/ppermute | solution.py:1047
  583.2 19.1 %collective-permute-start.3 = (bf16[5,272,128]{2,1,0:T(8,128)(2,1)}, bf16[5,272,128]{2,1,0:T(8,128)(2,1)S(1)}, u32[]{:S(2)}, u32[]{:S(2)}) collective-permute-start(bf16[5,272,128]{2,1,0:T(8,128)(2,1)} %get-tuple-element.120), channel_id=1, source_target_pairs={{0,1},{1,2},{2,3},{3,0},{4,5},{5,6},{6,7},{7,4},{8,9},{9,10},{10,1... | collective-permute-start | bytes 1044488 | tf_op jit(solution)/shard_map/ppermute | solution.py:1047
  583.8 37.1 %collective-permute-start.4 = (bf16[5,272,128]{2,1,0:T(8,128)(2,1)}, bf16[5,272,128]{2,1,0:T(8,128)(2,1)S(1)}, u32[]{:S(2)}, u32[]{:S(2)}) collective-permute-start(bf16[5,272,128]{2,1,0:T(8,128)(2,1)} %get-tuple-element.122), channel_id=1, source_target_pairs={{0,2},{1,3},{2,0},{3,1},{4,6},{5,7},{6,4},{7,5},{8,10},{9,11},{10,... | collective-permute-start | bytes 1044488 | tf_op jit(solution)/shard_map/ppermute | solution.py:1047
  586.4 34.5 %collective-permute-start.5 = (bf16[5,272,128]{2,1,0:T(8,128)(2,1)S(1)}, bf16[5,272,128]{2,1,0:T(8,128)(2,1)S(1)}, u32[]{:S(2)}, u32[]{:S(2)}) collective-permute-start(bf16[5,272,128]{2,1,0:T(8,128)(2,1)S(1)} %get-tuple-element.121), channel_id=1, source_target_pairs={{0,3},{1,0},{2,1},{3,2},{4,7},{5,4},{6,5},{7,6},{8,11},{9,8},{10,9... | collective-permute-start | bytes 1044488 | tf_op jit(solution)/shard_map/ppermute | solution.py:1047
  622.0 4.2 slice-start
  666.6 6.1 copy-start.4
  666.6 8.7 %copy-start.1 = (bf16[1024,1024]{1,0:T(8,128)(2,1)S(1)}, bf16[1024,1024]{1,0:T(8,128)(2,1)}, u32[]{:S(2)}) copy-start(bf16[1024,1024]{1,0:T(8,128)(2,1)} %param.27) | copy-start | bytes 6291460
  (3 other events, 2.6 us)
Sparse Core Ops, SparseCore 0:
  11.5 97.1 all-gather.6
  112.1 128.2 all-gather.8
  309.9 107.4 all-gather.10
  544.8 45.4 all-gather.12
  622.1 44.5 all-gather.14

commit v3 on v2

--- a/solution.py
+++ b/solution.py
@@ -142,6 +142,72 @@
             copy((me + step) % count, me).wait_send()
 
     return send, arrived, sent
+
+
+def plane_gather(source, store, send, recv):
+    me = lax.axis_index("ctx")
+    chips = lax.axis_size("ctx") // 2
+    last = chips - 1
+    sibling = flipped_bits(me, 1)
+    near = [flipped_bits(me, 2 * other) for other in range(1, chips)]
+    relay = chips == 4
+    height = store.shape[1]
+    cut = height // 2 if height < 32 else height // 32 * 16
+
+    def own(index, there, block):
+        return remote(source, store.at[block], send.at[index], recv.at[index], {"ctx": there})
+
+    def passed(index, block):
+        return remote(
+            store.at[block], store.at[block], send.at[chips + index], recv.at[chips + index],
+            {"ctx": sibling},
+        )
+
+    def half(part, there, block):
+        rows = pl.ds(0, cut) if part == 0 else pl.ds(cut, height - cut)
+        at = 2 * chips - 1 + part
+        return remote(
+            store.at[block, rows], store.at[block, rows], send.at[at], recv.at[at], {"ctx": there}
+        )
+
+    firsts = range(2) if relay else range(last)
+
+    def start():
+        for index in firsts:
+            own(index, near[index], me).start()
+        own(last, sibling, me).start()
+
+    def land(index):
+        block = near[index]
+        if relay and index == 2:
+            half(0, near[0], block).wait_recv()
+            half(1, near[1], block).wait_recv()
+        else:
+            own(index, block, block).wait_recv()
+            if relay:
+                half(1 - index, near[1 - index], block).start()
+        passed(index, block).start()
+        return block
+
+    def rest(index):
+        if index == 0:
+            own(last, sibling, sibling).wait_recv()
+            return sibling
+        block = flipped_bits(near[index - 1], 1)
+        passed(index - 1, block).wait_recv()
+        return block
+
+    def done():
+        for index in firsts:
+            own(index, near[index], me).wait_send()
+        own(last, sibling, me).wait_send()
+        for index in range(last):
+            passed(index, near[index]).wait_send()
+        if relay:
+            half(0, near[0], near[1]).wait_send()
+            half(1, near[1], near[0]).wait_send()
+
+    return start, land, rest, done
 
 
 def attend_forward_kernel(cross, heads, conts, offs_ref, q_ref, k_ref, v_ref, *refs):
@@ -159,10 +225,16 @@
     greet(others("ctx") + ([] if cross else others("fsdp")))
     send, arrived, sent = exchange(stage, mixed_ref, send_sem, recv_sem, own_sem)
     if not cross:
-        gather_send, gather_recv, gather_own = refs
-        first, second, local = gather_copies(
-            enc_ref, kv_ref, enc_all, kv_all, gather_send, gather_recv, gather_own
-        )
+        gather_send, gather_recv, gather_own, kv_send, kv_recv = refs
+        enc_start, enc_land, enc_rest, enc_done = plane_gather(
+            enc_ref, enc_all, gather_send, gather_recv
+        )
+        enc_start()
+        first = group_spread(kv_ref, kv_all, kv_send, kv_recv, 0)
+        local = [
+            pltpu.make_async_copy(enc_ref, enc_all.at[me], gather_own.at[0]),
+            pltpu.make_async_copy(kv_ref, kv_all.at[lax.axis_index("fsdp")], gather_own.at[1]),
+        ]
         for copy in first + local:
             copy.start()
     if cross:
@@ -184,7 +256,7 @@
             q = q_all[i]
             q_out[i] = q
         else:
-            i = step
+            i = (me + 1 + step) % count
             q = q_ref[tile_rows(i), :]
         masked = [head_lanes(head, q) for head in range(heads)]
         total[...] = jnp.zeros_like(total)
@@ -259,13 +331,10 @@
         send(i)
         if not cross:
 
-            @pl.when(step == tiles - 2)
+            @pl.when(step == tiles - 3)
             def _():
-                for copy in local:
-                    copy.wait()
-                for copy in first:
-                    copy.wait_recv()
-                second.start()
+                for index in range(min(2, count // 2 - 1)):
+                    enc_land(index)
 
         return carry
 
@@ -278,38 +347,27 @@
     if cross:
         put_done()
     else:
+        for index in range(2, count // 2 - 1):
+            enc_land(index)
+        for index in range(count // 2):
+            enc_rest(index)
         for copy in first:
             copy.wait_send()
-        second.wait()
-
-
-def gather_copies(enc_ref, kv_ref, enc_all, kv_all, send_sem, recv_sem, own_sem):
-    me, zone = lax.axis_index("ctx"), lax.axis_index("fsdp")
-    chip, core = me // 2, me % 2
-    chips, groups = lax.axis_size("ctx") // 2, lax.axis_size("fsdp")
-    first = []
-    for other in range(1, chips):
-        sem = len(first)
-        first.append(
-            remote(enc_ref, enc_all.at[chip, core], send_sem.at[sem], recv_sem.at[sem],
-                   {"ctx": flipped_bits(me, 2 * other)})
-        )
-    for shift in range(1, groups):
-        sem = len(first)
-        first.append(
-            remote(kv_ref, kv_all.at[zone], send_sem.at[sem], recv_sem.at[sem],
-                   {"fsdp": (zone + shift) % groups})
-        )
-    sem = len(first)
-    second = remote(
-        enc_all.at[:, core], enc_all.at[:, core], send_sem.at[sem], recv_sem.at[sem],
-        {"ctx": flipped_bits(me, 1)},
-    )
-    local = [
-        pltpu.make_async_copy(enc_ref, enc_all.at[chip, core], own_sem.at[0]),
-        pltpu.make_async_copy(kv_ref, kv_all.at[zone], own_sem.at[1]),
+            copy.wait_recv()
+        for copy in local:
+            copy.wait()
+        enc_done()
+
+
+def group_spread(source, target, send_sem, recv_sem, sem):
+    zone, groups = lax.axis_index("fsdp"), lax.axis_size("fsdp")
+    return [
+        remote(
+            source, target.at[zone], send_sem.at[sem + shift - 1], recv_sem.at[sem + shift - 1],
+            {"fsdp": (zone + shift) % groups},
+        )
+        for shift in range(1, groups)
     ]
-    return first, second, local
 
 
 def attend_forward(cross, heads, offsets, q, k, v, extra=()):
@@ -340,10 +398,10 @@
     else:
         enc, kv = extra
         groups = lax.axis_size("fsdp")
-        outs.append(jax.ShapeDtypeStruct((count // 2, 2) + enc.shape, BF))
+        outs.append(jax.ShapeDtypeStruct((count,) + enc.shape, BF))
         outs.append(jax.ShapeDtypeStruct((groups,) + kv.shape, BF))
-        copies = count // 2 + groups - 1
-        scratch += [dma((copies,)), dma((copies,)), dma((2,))]
+        scratch += [dma((count + 1,)), dma((count + 1,)), dma((2,))]
+        scratch += [dma((groups - 1,)), dma((groups - 1,))]
         places = [hbm, hbm]
     return pl.pallas_call(
         functools.partial(attend_forward_kernel, cross, heads, offsets.shape[1]),
@@ -363,7 +421,8 @@
 
 def rest_copies(sources, targets, send_sem, recv_sem):
     me = lax.axis_index("ctx")
-    half = lax.axis_size("ctx") // 4
+    chips = lax.axis_size("ctx") // 2
+    half = chips // 2
     out = []
     for other in range(1, half):
         for part in range(2):
@@ -377,128 +436,175 @@
                     {"ctx": flipped_bits(me, (4 if part == 0 else 2) * other)},
                 )
             )
+    out = out + chip_copies(sources[2], targets[2], send_sem, recv_sem, len(out))
+    return out + group_spread(sources[3], targets[3], send_sem, recv_sem, len(out))
+
+
+def chip_copies(source, target, send_sem, recv_sem, sem):
+    me = lax.axis_index("ctx")
+    return [
+        remote(
+            source.at[flipped_bits(me // 2, other)], target.at[other - 1],
+            send_sem.at[sem + other - 1], recv_sem.at[sem + other - 1],
+            {"ctx": flipped_bits(me, 2 * other)},
+        )
+        for other in range(1, lax.axis_size("ctx") // 2)
+    ]
+
+
+def group_copies(source, target, send_sem, recv_sem, sem):
+    zone, groups = lax.axis_index("fsdp"), lax.axis_size("fsdp")
+    return [
+        remote(
+            source.at[(zone + shift) % groups], target.at[shift - 1],
+            send_sem.at[sem + shift - 1], recv_sem.at[sem + shift - 1],
+            {"fsdp": (zone + shift) % groups},
+        )
+        for shift in range(1, groups)
+    ]
+
+
+def last_copies(sources, targets, send_sem, recv_sem):
+    out = chip_copies(sources[0], targets[0], send_sem, recv_sem, 0)
+    for source, target in zip(sources[1:4], targets[1:4]):
+        out = out + group_copies(source, target, send_sem, recv_sem, len(out))
+    for source, target in zip(sources[4:], targets[4:]):
+        sem = len(out)
+        there = {"ctx": flipped_bits(lax.axis_index("ctx"), 1)}
+        out.append(remote(source, target, send_sem.at[sem], recv_sem.at[sem], there))
     return out
 
 
-def last_copies(sources, targets, send_sem, recv_sem):
-    me, zone = lax.axis_index("ctx"), lax.axis_index("fsdp")
-    chips, groups = lax.axis_size("ctx") // 2, lax.axis_size("fsdp")
-    out = []
-    for other in range(1, chips):
-        sem = len(out)
-        out.append(
-            remote(
-                sources[0].at[flipped_bits(me // 2, other)], targets[0].at[other - 1],
-                send_sem.at[sem], recv_sem.at[sem], {"ctx": flipped_bits(me, 2 * other)},
-            )
-        )
-    for shift in range(1, groups):
-        sem = len(out)
-        there = (zone + shift) % groups
-        out.append(
-            remote(
-                sources[1].at[there], targets[1].at[shift - 1],
-                send_sem.at[sem], recv_sem.at[sem], {"fsdp": there},
-            )
-        )
-    return out
-
-
 def attend_backward_kernel(
-    cross, heads, conts, scale, carried, offs_ref, q_ref, k_ref, v_ref, do_ref, att_ref,
+    cross, heads, conts, scale, carried, number, offs_ref, q_ref, k_ref, v_ref, do_ref, att_ref,
     lse_ref, *refs,
 ):
-    sources, refs = refs[:2], refs[2:]
+    sources, refs = refs[:number], refs[number:]
+    if not cross:
+        normed_ref, *refs = refs
     if cross:
         moved_ref, dk_ref, dv_ref, *refs = refs
     else:
-        moved_ref, stage, *refs = refs
-    targets, refs = refs[:2], refs[2:]
+        moved_ref, stage, product_ref, column_ref, *refs = refs
+    targets, refs = refs[:number], refs[number:]
     if cross:
         stage, *refs = refs
     (
         do_all, key_t, delta, dq_sum, dk_sum, dv_sum,
-        send_sem, recv_sem, own_sem, do_send, do_recv, do_own, carry_send, carry_recv,
+        send_sem, recv_sem, own_sem, do_send, do_recv, do_own, carry_send, carry_recv, *refs,
     ) = refs
+    if cross:
+        (keep_sem,) = refs
+        keep_own = pltpu.make_async_copy(
+            sources[3], targets[3].at[lax.axis_index("fsdp")], keep_sem
+        )
+    else:
+        normed, normed_sem = refs
+        product_ref[...] = jnp.zeros_like(product_ref)
+        column_ref[...] = jnp.zeros_like(column_ref)
     me, count = lax.axis_index("ctx"), lax.axis_size("ctx")
     tiles = count
     key_tiles = k_ref.shape[0] // TILE
     prompt = tiles * TILE - conts * CONT
-    prompt_tiles = prompt // TILE
-    greet(others("ctx") + ([] if cross else others("fsdp")))
+    greet(others("ctx") + others("fsdp"))
     put, got, put_done = exchange(do_ref, do_all, do_send, do_recv, do_own)
     for step in range(count):
         put((me + step) % count)
     carry_copies = carried(sources, targets, carry_send, carry_recv)
     for copy in carry_copies:
         copy.start()
+    if cross:
+        keep_own.start()
     send, arrived, sent = exchange(stage, moved_ref, send_sem, recv_sem, own_sem)
+    dq_sum[...] = jnp.zeros_like(dq_sum)
     dk_sum[...] = jnp.zeros_like(dk_sum)
     dv_sum[...] = jnp.zeros_like(dv_sum)
     for tile in range(key_tiles):
         at = pl.ds(tile * TILE, TILE)
         key_t[:, at] = transposed(k_ref[at, :])
 
-    def query_tile(step, carry):
-        i = (me + step) % count if cross else tiles - 1 - step
-        q = q_ref[tile_rows(i), :]
+    def ready(i):
         got(i)
-        do = do_all[i]
-        q_masked = [head_lanes(head, q) for head in range(heads)]
-        do_masked = [head_lanes(head, do) for head in range(heads)]
-        both = do.astype(F32).T * att_ref[:, tile_rows(i)]
+        both = do_all[i].astype(F32).T * att_ref[:, tile_rows(i)]
         for head in range(heads):
-            delta[head : head + 1, :] = jnp.sum(
+            delta[head : head + 1, tile_rows(i)] = jnp.sum(
                 both[64 * head : 64 * head + 64], axis=0, keepdims=True
             )
-        dq_sum[...] = jnp.zeros_like(dq_sum)
-
-        def key_step(j, shown):
-            at = tile_rows(j)
-            k, v = k_ref[at, :], v_ref[at, :]
-            for head in range(heads):
-                scores = nt(k, q_masked[head])
-                weights = jnp.exp(scores - lse_ref[head : head + 1, tile_rows(i)])
-                if shown is not None:
-                    weights = jnp.where(shown, weights, 0.0)
-                weight_grad = nt(v, do_masked[head])
-                score_grad = (weights * (weight_grad - delta[head : head + 1, :])).astype(BF)
-                dv_sum[at, :] += nn(weights.astype(BF), do_masked[head])
-                dk_sum[at, :] += nn(score_grad, q_masked[head])
-                own = slice(64 * head, 64 * head + 64)
-                dq_sum[own, :] += nn(key_t[own, at], score_grad)
+
+    def pair(i, j, shown):
+        row, at = tile_rows(i), tile_rows(j)
+        q, do, k, v = q_ref[row, :], do_all[i], k_ref[at, :], v_ref[at, :]
+        for head in range(heads):
+            q_own, do_own = head_lanes(head, q), head_lanes(head, do)
+            weights = jnp.exp(nt(k, q_own) - lse_ref[head : head + 1, row])
+            if shown is not None:
+                weights = jnp.where(shown, weights, 0.0)
+            weight_grad = nt(v, do_own)
+            score_grad = (weights * (weight_grad - delta[head : head + 1, row])).astype(BF)
+            dv_sum[at, :] += nn(weights.astype(BF), do_own)
+            dk_sum[at, :] += nn(score_grad, q_own)
+            own = slice(64 * head, 64 * head + 64)
+            dq_sum[own, row] += nn(key_t[own, at], score_grad)
+
+    def shown_of(i, j):
+        if conts == 1:
+            return None
+        cont = jnp.maximum(i * TILE - prompt, 0) // CONT
+        own = jnp.where(i * TILE < prompt, 0, prompt + cont * CONT)
+        return visible(j * TILE, i * TILE, TILE, TILE, own, offs_ref[0, cont])
+
+    def queries_back(i):
+        return (dq_sum[:, tile_rows(i)].T.astype(BF).astype(F32) * scale).astype(BF)
+
+    def cross_tile(step, carry):
+        i = (me + step) % count
+        ready(i)
 
         def plain(j, carry):
-            key_step(j, None)
+            pair(i, j, None)
             return carry
 
-        if cross:
-            lax.fori_loop(0, key_tiles, plain, 0)
-        elif conts == 1:
-            key_step(i, visible(0, 0, TILE, TILE, 0, None))
-            lax.fori_loop(0, i, plain, 0)
-        else:
-            cont = jnp.maximum(i * TILE - prompt, 0) // CONT
-            inside = i * TILE < prompt
-            own = jnp.where(inside, 0, prompt + cont * CONT)
-            limit = offs_ref[0, cont]
-
-            def one(j, carry):
-                key_step(j, visible(j * TILE, i * TILE, TILE, TILE, own, limit))
-                return carry
-
-            lax.fori_loop(jnp.where(inside, 0, own // TILE), i + 1, one, 0)
-            lax.fori_loop(0, jnp.where(inside, 0, prompt_tiles), one, 0)
-
-        dq = dq_sum[...].T.astype(BF).astype(F32)
-        stage[i, :, :128] = (dq * scale).astype(BF)
-        if not cross:
-            stage[i, :, 128:256] = dk_sum[tile_rows(i), :].astype(BF)
-            stage[i, :, 256:] = dv_sum[tile_rows(i), :].astype(BF)
+        lax.fori_loop(0, key_tiles, plain, 0)
+        stage[i] = queries_back(i)
         send(i)
         return carry
 
-    lax.fori_loop(0, tiles, query_tile, 0)
+    def self_tile(step, carry):
+        i = (me + 1 + step) % count
+        fetch = pltpu.make_async_copy(normed_ref.at[i], normed, normed_sem)
+        fetch.start()
+
+        @pl.when(step == 0)
+        def _():
+            ready(i)
+
+        pair(i, i, visible(0, 0, TILE, TILE, 0, None) if conts == 1 else shown_of(i, i))
+
+        def other(turn, carry):
+            p = (i + turn) % count
+
+            @pl.when(step == 0)
+            def _():
+                ready(p)
+
+            high, low = jnp.maximum(i, p), jnp.minimum(i, p)
+            pair(high, low, shown_of(high, low))
+            return carry
+
+        lax.fori_loop(1, count - step, other, 0)
+        stage[i, :, :128] = queries_back(i)
+        stage[i, :, 128:256] = dk_sum[tile_rows(i), :].astype(BF)
+        stage[i, :, 256:] = dv_sum[tile_rows(i), :].astype(BF)
+        send(i)
+        fetch.wait()
+        grads = stage[i]
+        product_ref[...] += tn(normed[...], grads)
+        column_ref[...] += jnp.broadcast_to(
+            jnp.sum(grads.astype(F32), axis=0, keepdims=True), column_ref.shape
+        )
+        return carry
+
+    lax.fori_loop(0, tiles, cross_tile if cross else self_tile, 0)
     if cross:
         dk_ref[...] = dk_sum[...].astype(BF)
         dv_ref[...] = dv_sum[...].astype(BF)
@@ -506,12 +612,16 @@
         arrived((me + step) % count)
     sent()
     put_done()
+    if cross:
+        keep_own.wait()
     for copy in carry_copies:
         copy.wait_send()
         copy.wait_recv()
 
 
-def attend_backward(cross, heads, scale, offsets, q, k, v, do, att, lse, sources, target_shapes):
+def attend_backward(
+    cross, heads, scale, offsets, q, k, v, do, att, lse, sources, target_shapes, normed=()
+):
     count = lax.axis_size("ctx")
     vmem = pl.BlockSpec(memory_space=pltpu.VMEM)
     hbm = pl.BlockSpec(memory_space=pl.ANY)
@@ -521,31 +631,37 @@
     moved = jax.ShapeDtypeStruct((count, TILE, wide), BF)
     if cross:
         local = [jax.ShapeDtypeStruct((keys, 128), BF)] * 2
-        carries = 2 * max(count // 4 - 1, 1)
+        carries = 2 * (count // 4 - 1) + count // 2 - 1 + lax.axis_size("fsdp") - 1
     else:
-        local = [jax.ShapeDtypeStruct((count, TILE, wide), BF)]
-        carries = count // 2 - 1 + lax.axis_size("fsdp") - 1
+        local = [
+            jax.ShapeDtypeStruct((count, TILE, wide), BF),
+            jax.ShapeDtypeStruct((normed[0].shape[2], wide), F32),
+            jax.ShapeDtypeStruct((8, wide), F32),
+        ]
+        carries = count // 2 - 1 + (lax.axis_size("fsdp") - 1) * 3 + 2
     targets = [jax.ShapeDtypeStruct(shape, BF) for shape in target_shapes]
     return pl.pallas_call(
         functools.partial(
             attend_backward_kernel, cross, heads, offsets.shape[1], scale,
-            rest_copies if cross else last_copies,
+            rest_copies if cross else last_copies, len(sources),
         ),
         out_shape=[moved] + local + targets,
-        in_specs=[pl.BlockSpec(memory_space=pltpu.SMEM)] + [vmem] * 6 + [hbm] * 2,
-        out_specs=[hbm] + [vmem] * len(local) + [hbm] * 2,
+        in_specs=[pl.BlockSpec(memory_space=pltpu.SMEM)] + [vmem] * 6
+        + [hbm] * (len(sources) + len(normed)),
+        out_specs=[hbm] + [vmem] * len(local) + [hbm] * len(sources),
         scratch_shapes=([pltpu.VMEM((count, TILE, wide), BF)] if cross else [])
         + [
             pltpu.VMEM((count, TILE, 128), BF),
             pltpu.VMEM((128, keys), BF),
-            pltpu.VMEM((8, TILE), F32),
-            pltpu.VMEM((128, TILE), F32),
+            pltpu.VMEM((8, count * TILE), F32),
+            pltpu.VMEM((128, count * TILE), F32),
             pltpu.VMEM((keys, 128), F32),
             pltpu.VMEM((keys, 128), F32),
             dma((count,)), dma((count,)), dma,
             dma((count,)), dma((count,)), dma,
             dma((carries,)), dma((carries,)),
-        ],
+        ]
+        + ([dma] if cross else [pltpu.VMEM(normed[0].shape[1:], BF), dma]),
         compiler_params=pltpu.CompilerParams(
             vmem_limit_bytes=VMEM_BYTES, collective_id=3 if cross else 4,
             has_side_effects=True,
@@ -553,7 +669,7 @@
         cost_estimate=pl.CostEstimate(
             flops=60 * 10**9, bytes_accessed=2**23, transcendentals=2**24
         ),
-    )(offsets, q, k, v, do, att, lse, *sources)
+    )(offsets, q, k, v, do, att, lse, *sources, *normed)
 
 
 def project_kernel(
@@ -587,18 +703,8 @@
     for copy in parts:
         copy.start()
 
-    def direct(there, block):
-        return remote(tokens_ref, all_tokens.at[block], token_send.at[there],
-                      token_recv.at[block], {"ctx": there})
-
-    def passed(block):
-        return remote(
-            all_tokens.at[block], all_tokens.at[block], token_send.at[flipped_bits(block, 1)],
-            token_recv.at[block], sibling,
-        )
-
-    for there in near + [flipped_bits(me, 1)]:
-        direct(there, me).start()
+    start, land, rest, done = plane_gather(tokens_ref, all_tokens, token_send, token_recv)
+    start()
     for copy in local:
         copy.wait()
     for copy in parts:
@@ -619,17 +725,28 @@
     def save(block, place):
         return pltpu.make_async_copy(staged.at[place], normed_ref.at[block], stage_sem.at[place])
 
-    order = [me, flipped_bits(me, 1)] + near + [flipped_bits(there, 1) for there in near]
-    for step, block in enumerate(order):
+    order, ready = [], []
+    for step in range(count):
         place = step % 2
-        if step == 1:
-            direct(block, block).wait_recv()
-        elif step >= 2:
-            if step <= chips:
-                direct(block, block).wait_recv()
-                passed(block).start()
+        if step == 0:
+            ready.append(me)
+        elif step == 1:
+            ready.append(rest(0))
+        elif step == 2:
+            for index in range(min(2, chips - 1)):
+                ready.append(land(index))
+        elif len(ready) == step:
+            index = step - chips - 1
+            if step == 4 and chips == 4:
+                ready += [rest(1), rest(2)]
+            elif step == 6 and chips == 4:
+                ready.append(land(2))
+            elif chips == 4:
+                ready.append(rest(3))
             else:
-                passed(block).wait_recv()
+                ready.append(land(step - 2) if step <= chips else rest(index + 1))
+        block = ready[step]
+        order.append(block)
         if step >= 2:
             save(order[step - 2], place).wait()
         unit, _ = normalize(all_tokens[block].astype(F32))
@@ -645,10 +762,7 @@
         save(order[step], step % 2).wait()
     for copy in parts:
         copy.wait_send()
-    for there in near + [flipped_bits(me, 1)]:
-        direct(there, me).wait_send()
-    for there in near:
-        passed(there).wait_send()
+    done()
 
 
 def project(own, scale, tokens, small, head_in):
@@ -671,7 +785,7 @@
         scratch_shapes=[
             pltpu.VMEM((count, rows, width), BF),
             pltpu.VMEM((2, rows, width), BF),
-            dma((count,)), dma((count,)),
+            dma((count + 1,)), dma((count + 1,)),
             dma((2, groups - 1)), dma((2, groups - 1)),
             dma((3,)), dma((2,)),
         ],
@@ -685,13 +799,17 @@
 
 
 def ffn_kernel(
-    steps, groups, n_ref, dy_ref, base_ref, bias_ref, win_ref, wout_ref,
-    out_ref, gn_ref, gb_ref, in_ref, sum_ref,
+    steps, groups, n_ref, dy_ref, base_ref, bias_ref, win_ref, wout_ref, rows_ref,
+    out_ref, gn_ref, gb_ref, in_ref, sum_ref, rows_all,
     n_t, own_in, own_out, post_in, post_out, got_in, got_out,
     keep_in, keep_out, flow_in, flow_out, near_in, near_out,
-    send_sem, recv_sem, flow_send, flow_recv, save_sem,
+    send_sem, recv_sem, flow_send, flow_recv, save_sem, rows_send, rows_recv, rows_own,
 ):
     f = pl.program_id(0)
+    spread = group_spread(rows_ref, rows_all, rows_send, rows_recv, 0)
+    keep_rows = pltpu.make_async_copy(
+        rows_ref, rows_all.at[lax.axis_index("fsdp")], rows_own
+    )
     me = lax.axis_index("ctx")
     count = lax.axis_size("ctx")
     chips = count // 2
@@ -722,7 +840,10 @@
 
     @pl.when(f == 0)
     def _():
-        greet([sibling, low, high])
+        greet([sibling, low, high] + others("fsdp"))
+        for copy in spread:
+            copy.start()
+        keep_rows.start()
         n_t[...] = transposed(n_ref[...])
         gn_ref[...] = jnp.zeros_like(gn_ref)
         out_ref[...] = base_ref[...]
@@ -837,9 +958,13 @@
 
         lax.fori_loop(0, steps, join, 0)
         lax.fori_loop(0, steps, saved, 0)
-
-
-def ffn(normed, dy, base, bias, weights):
+        keep_rows.wait()
+        for copy in spread:
+            copy.wait_send()
+            copy.wait_recv()
+
+
+def ffn(normed, dy, base, bias, weights, rows_part):
     rows, width = normed.shape
     hidden = weights.shape[1] // 2
     groups = lax.axis_size("fsdp")
@@ -865,6 +990,7 @@
             jax.ShapeDtypeStruct((steps, 8, step), F32),
             jax.ShapeDtypeStruct((steps, width // 2, cols), BF),
             jax.ShapeDtypeStruct((hidden // width, 2, width // 2, cols), BF),
+            jax.ShapeDtypeStruct((groups,) + rows_part.shape, BF),
         ),
         in_specs=[
             once, once, once,
@@ -873,12 +999,13 @@
             pl.BlockSpec(
                 (step, width), lambda f: (now(f) % per, hidden // width + now(f) // per)
             ),
+            hbm,
         ],
         out_specs=(
             pl.BlockSpec((rows, width), whole),
             pl.BlockSpec((rows, width), whole),
             pl.BlockSpec((1, 8, step), lambda f: (now(f), 0, 0)),
-            hbm, hbm,
+            hbm, hbm, hbm,
         ),
         scratch_shapes=[
             pltpu.VMEM((width, rows), BF),
@@ -895,6 +1022,7 @@
             pltpu.VMEM((steps, width // 2, cols), BF),
             pltpu.VMEM((steps, 2, step // 2, cols), BF),
             dma((2, 2)), dma((2, steps)), dma((2, 2)), dma((2, steps)), dma((2, steps)),
+            dma((groups - 1,)), dma((groups - 1,)), dma,
         ],
         compiler_params=pltpu.CompilerParams(
             vmem_limit_bytes=60 * 2**20, collective_id=0, has_side_effects=True
@@ -902,151 +1030,273 @@
         cost_estimate=pl.CostEstimate(
             flops=30 * 10**9, bytes_accessed=2**26, transcendentals=2**22
         ),
-    )(normed, dy, base, bias, weights, weights)
-
-
-def token_grad_kernel(
-    own, moved_ref, wq_ref, wk_ref, wv_ref, tokens_ref, gain_ref, first_ref, out_ref
-):
-    step = pl.program_id(0)
-
-    @pl.when(step == 0)
-    def _():
-        out_ref[...] = jnp.zeros_like(out_ref)
-
-    grads = moved_ref[0]
-    total = out_ref[...]
-    for part, weight in enumerate((wq_ref, wk_ref, wv_ref)):
-        total = total + nt(grads[:, part * 128 : part * 128 + own], weight[...])
-    out_ref[...] = total
-
-    @pl.when(step == pl.num_programs(0) - 1)
-    def _():
-        unit, scale = normalize(tokens_ref[...].astype(F32))
-        q = gain_ref[...] * out_ref[...]
-        mean = jnp.mean(q, axis=-1, keepdims=True)
-        slant = jnp.mean(q * unit, axis=-1, keepdims=True)
-        out_ref[...] = first_ref[...] + scale * (q - mean - unit * slant)
-
-
-def token_grad(moved, weights, tokens, gain, first):
-    ctx, rows, wide = moved.shape
-    width = tokens.shape[1]
-    own = width // ctx
-    if own < 128:
-        cut = moved.reshape(ctx, rows, 3, 128)[:, :, :, :own]
-        grads = jnp.transpose(cut, (1, 2, 0, 3)).reshape(rows, 3 * width)
-        unit, scale = normalize(tokens.astype(F32))
-        return first + normalize_back(unit, scale, gain, nt(grads, weights))[0]
-    whole = pl.BlockSpec((rows, width), lambda s: (0, 0))
+    )(normed, dy, base, bias, weights, weights, rows_part)
+
+
+def finish_kernel(more, late_ref, done_ref, ffn_ref, *refs):
+    if more:
+        moved_ref, enc_ref, self_mine, self_other, kv_mine, kv_other, *refs = refs
+    all_ffn, all_done, all_late, *refs = refs
+    if more:
+        token_ref, enc_grad_ref, *refs = refs
+    late_own, got, send_sem, recv_sem, zone_send, zone_recv, own_sem, *refs = refs
+    me, zone = lax.axis_index("ctx"), lax.axis_index("fsdp")
+    count, groups = lax.axis_size("ctx"), lax.axis_size("fsdp")
+    chips = count // 2
+    greet(others("ctx") + others("fsdp"))
+    zones = group_copies(late_ref, got, zone_send, zone_recv, 0)
+    for copy in zones:
+        copy.start()
+    if more:
+        all_moved, weights, all_enc, enc_send, enc_recv, enc_own, moved_sem, weight_sem = refs
+        put, arrived, put_done = exchange(enc_ref, all_enc, enc_send, enc_recv, enc_own)
+        for step in range(count):
+            put((me + step) % count)
+        fetch_moved = pltpu.make_async_copy(moved_ref, all_moved, moved_sem)
+        fetch_moved.start()
+    gathers = [
+        plane_gather(source, store, send_sem.at[kind], recv_sem.at[kind])
+        for kind, (source, store) in enumerate(
+            ((ffn_ref, all_ffn), (done_ref, all_done), (late_own, all_late))
+        )
+    ]
+    local = [
+        pltpu.make_async_copy(source, store.at[me], own_sem.at[kind])
+        for kind, (source, store) in enumerate(
+            ((ffn_ref, all_ffn), (done_ref, all_done), (late_own, all_late))
+        )
+    ]
+    for kind in range(2):
+        gathers[kind][0]()
+        local[kind].start()
+    if more:
+        width = token_ref.shape[1]
+        core = me % 2
+
+        def fetch(step):
+            source = (me + step) % count
+            out = []
+            for k in range(5):
+                at = (k if k < 3 else k - 3) * width + source * 128
+                columns = pl.ds(pl.multiple_of(at, 128), 128)
+                pair = (self_mine, self_other) if k < 3 else (kv_mine, kv_other)
+                for index, array in enumerate(pair):
+                    side = core if index == 0 else 1 - core
+                    out.append(
+                        pltpu.make_async_copy(
+                            array.at[:, :, columns], weights.at[step % 2, k, :, side],
+                            weight_sem.at[step % 2, k, index],
+                        )
+                    )
+            return out
+
+        for copy in fetch(0):
+            copy.start()
+        token_ref[...] = jnp.zeros_like(token_ref)
+        enc_grad_ref[...] = jnp.zeros_like(enc_grad_ref)
+        fetch_moved.wait()
+
+        def one_source(step, carry):
+            source = (me + step) % count
+
+            @pl.when(step + 1 < count)
+            def _():
+                for copy in fetch(step + 1):
+                    copy.start()
+
+            for copy in fetch(step):
+                copy.wait()
+            grads = all_moved[source]
+
+            def part(index):
+                return weights[step % 2, index].reshape(width, 128)
+
+            token_ref[...] += (
+                nt(grads[:, :128], part(0))
+                + nt(grads[:, 128:256], part(1))
+                + nt(grads[:, 256:], part(2))
+            )
+            arrived(source)
+            rows = all_enc[source]
+            enc_grad_ref[...] += nt(rows[:, :128], part(3)) + nt(rows[:, 128:], part(4))
+            return carry
+
+        lax.fori_loop(0, count, one_source, 0)
+    total = late_ref[zone].astype(F32)
+    for shift in range(groups - 1):
+        zones[shift].wait_recv()
+        total = total + got[shift].astype(F32)
+    late_own[...] = total.astype(BF)
+    gathers[2][0]()
+    local[2].start()
+    for index in range(chips - 1):
+        for gather in gathers:
+            gather[1](index)
+    for index in range(chips):
+        for gather in gathers:
+            gather[2](index)
+    for copy in local:
+        copy.wait()
+    for gather in gathers:
+        gather[3]()
+    for copy in zones:
+        copy.wait_send()
+    if more:
+        put_done()
+
+
+def finish(late, done, ffn_sums, width, more=()):
+    count, groups = lax.axis_size("ctx"), lax.axis_size("fsdp")
+    vmem = pl.BlockSpec(memory_space=pltpu.VMEM)
+    hbm = pl.BlockSpec(memory_space=pl.ANY)
+    dma = pltpu.SemaphoreType.DMA
+    outs = [
+        jax.ShapeDtypeStruct((count,) + shape, BF)
+        for shape in (ffn_sums.shape, done.shape, late.shape[1:])
+    ]
+    places = [hbm] * 3
+    scratch = [
+        pltpu.VMEM(late.shape[1:], BF),
+        pltpu.VMEM((groups - 1,) + late.shape[1:], BF),
+        dma((3, count + 1)), dma((3, count + 1)),
+        dma((groups - 1,)), dma((groups - 1,)), dma((3,)),
+    ]
+    if more:
+        moved, enc, weights = more[:3]
+        outs.append(jax.ShapeDtypeStruct((moved.shape[1], width), F32))
+        outs.append(jax.ShapeDtypeStruct((enc.shape[1], width), F32))
+        places += [vmem, vmem]
+        scratch += [
+            pltpu.VMEM(moved.shape, BF),
+            pltpu.VMEM((2, 5, groups, 2, weights.shape[1], 128), BF),
+            pltpu.VMEM(enc.shape, BF),
+            dma((count,)), dma((count,)), dma, dma, dma((2, 5, 2)),
+        ]
     return pl.pallas_call(
-        functools.partial(token_grad_kernel, own),
-        grid=(ctx,),
-        out_shape=jax.ShapeDtypeStruct((rows, width), F32),
-        in_specs=[
-            pl.BlockSpec((1, rows, wide), lambda s: (s, 0, 0)),
-            pl.BlockSpec((width, own), lambda s: (0, s)),
-            pl.BlockSpec((width, own), lambda s: (0, ctx + s)),
-            pl.BlockSpec((width, own), lambda s: (0, 2 * ctx + s)),
-            whole,
-            pl.BlockSpec((1, width), lambda s: (0, 0)),
-            whole,
-        ],
-        out_specs=whole,
-        compiler_params=pltpu.CompilerParams(vmem_limit_bytes=VMEM_BYTES),
-        cost_estimate=pl.CostEstimate(flops=10**10, bytes_accessed=2**24, transcendentals=0),
-    )(moved, weights, weights, weights, tokens, gain, first)
-
-
-def place_ffn_kernel(groups, sum_ref, in_ref, out_ref):
-    chips, _, lead, part, cols = sum_ref.shape
-    steps = lead // 2
-    depth, hidden = in_ref.shape
-    blocks = hidden // (depth * groups)
+        functools.partial(finish_kernel, bool(more)),
+        out_shape=outs,
+        in_specs=[vmem] + [hbm] * (2 + len(more)),
+        out_specs=places,
+        scratch_shapes=scratch,
+        compiler_params=pltpu.CompilerParams(
+            vmem_limit_bytes=VMEM_BYTES, collective_id=6, has_side_effects=True
+        ),
+        cost_estimate=pl.CostEstimate(
+            flops=50 * 10**9, bytes_accessed=2**25, transcendentals=0
+        ),
+    )(late, done, ffn_sums, *more)
+
+
+def place_kernel(groups, more, ffn_ref, self_refs, kv_refs, mixed_refs, out_refs, extra):
+    in_ref, out_ref, self_ref, kv_ref, *weight_refs = out_refs
+    cols = ffn_ref.shape[3]
+    steps = ffn_ref.shape[1] // 2
+    hidden = in_ref.shape[1]
+    blocks = out_ref.shape[0]
+    width = out_ref.shape[3]
+    depth = width // groups
     per = steps // blocks
     span = min(depth, cols)
-    for chip in range(chips):
-        rows = slice(chip * part, chip * part + part)
-        for core in range(2):
-            for f in range(steps):
-                value = sum_ref[chip, core, f].astype(F32)
-                for piece in range(cols // span):
-                    unit = (f % per) * 2 * cols + core * cols + piece * span
-                    at = (unit // depth * blocks + f // per) * depth + unit % depth
-                    in_ref[rows, at : at + span] = value[:, piece * span : piece * span + span]
-            for slab in range(steps):
-                block, half = slab // 2, slab % 2
-                top = block * depth + chip * part
-                at = (core * 2 + half) * cols
-                out_ref[top : top + part, at : at + cols] = sum_ref[
-                    chip, core, steps + slab
-                ].astype(F32)
-
-
-def place_ffn(sums, depth, hidden, rows, width):
-    vmem = pl.BlockSpec(memory_space=pltpu.VMEM)
+    for core in range(2):
+        for f in range(steps):
+            value = ffn_ref[core, f].astype(F32)
+            for piece in range(cols // span):
+                unit = (f % per) * 2 * cols + core * cols + piece * span
+                at = (unit // depth * blocks + f // per) * depth + unit % depth
+                in_ref[:, at : at + span] = value[:, piece * span : piece * span + span]
+        for slab in range(steps):
+            at = (core * 2 + slab % 2) * cols
+            out_ref[slab // 2, 0, :, at : at + cols] = ffn_ref[core, steps + slab].astype(F32)
+    for refs, target in ((self_refs, self_ref), (kv_refs, kv_ref)):
+        for k, ref in enumerate(refs):
+            own = ref.shape[2]
+            for source in range(ref.shape[0]):
+                at = k * width + source * own
+                target[:, at : at + own] = ref[source].astype(F32)
+    part = in_ref.shape[0]
+    for (ref, count), targets in zip(mixed_refs, (weight_refs[:1], weight_refs[1:])):
+        own = ref.shape[2]
+        for w, target in enumerate(targets):
+            for core in range(2):
+                for index in range(count):
+                    top = (w * count + index) * part
+                    at = core * (width // 2) + index * own
+                    target[:, at : at + own] = ref[core, top : top + part, :].astype(F32)
+    if more:
+        total_ref, tokens_ref, gain_ref, base_ref, enc_ref, token_ref, enc_out = extra
+        unit, scale = normalize(tokens_ref[...].astype(F32))
+        token_ref[...] = (
+            base_ref[...] + normalize_back(unit, scale, gain_ref[...], total_ref[...])[0]
+        )
+        enc_out[...] = enc_ref[...]
+
+
+def place(ffn_sums, done, late, hidden, width, more=()):
+    count, groups = lax.axis_size("ctx"), lax.axis_size("fsdp")
+    chips, own = count // 2, late.shape[2]
+    depth = width // groups
+    part = depth // chips
+    blocks = hidden // width
+    wide = width // 2 // own
+
+    def lane_blocks(start, k):
+        return pl.BlockSpec((count, part, own), lambda c: (0, (start + k * depth) // part + c, 0))
+
+    in_specs = [pl.BlockSpec((2,) + ffn_sums.shape[1:], lambda c: (c, 0, 0, 0))]
+    in_specs += [lane_blocks(2 * wide * part, k) for k in range(3)]
+    in_specs += [lane_blocks(wide * part, k) for k in range(2)]
+    in_specs += [
+        pl.BlockSpec((2, wide * part, own), lambda c: (c, 0, 0)),
+        pl.BlockSpec((2, 2 * wide * part, own), lambda c: (c, 0, 0)),
+    ]
+    row = lambda n: pl.BlockSpec((part, n), lambda c: (c, 0))
+    out_specs = [
+        row(hidden), pl.BlockSpec((blocks, 1, part, width), lambda c: (0, c, 0, 0)),
+        row(3 * width), row(2 * width), row(width), row(width), row(width),
+    ]
+    out_shape = [
+        jax.ShapeDtypeStruct((depth, hidden), F32),
+        jax.ShapeDtypeStruct((blocks, chips, part, width), F32),
+        jax.ShapeDtypeStruct((depth, 3 * width), F32),
+        jax.ShapeDtypeStruct((depth, 2 * width), F32),
+    ] + [jax.ShapeDtypeStruct((depth, width), F32)] * 3
+    if more:
+        total, _, _, _, enc = more
+        tall, short = total.shape[0] // chips, enc.shape[0] // chips
+        tokens_rows = pl.BlockSpec((tall, width), lambda c: (c, 0))
+        enc_rows = pl.BlockSpec((short, width), lambda c: (c, 0))
+        in_specs += [
+            tokens_rows, tokens_rows, pl.BlockSpec((1, width), lambda c: (0, 0)), tokens_rows,
+            enc_rows,
+        ]
+        out_specs += [tokens_rows, enc_rows]
+        out_shape += [
+            jax.ShapeDtypeStruct(total.shape, F32), jax.ShapeDtypeStruct(enc.shape, F32)
+        ]
+
+    def kernel(*refs):
+        ffn_ref, refs = refs[0], refs[1:]
+        self_refs, kv_refs, mixed, refs = refs[:3], refs[3:5], refs[5:7], refs[7:]
+        extra_in, refs = refs[: len(more)], refs[len(more) :]
+        place_kernel(
+            groups, bool(more), ffn_ref, self_refs, kv_refs,
+            ((mixed[0], wide), (mixed[1], wide)), refs[:7], extra_in + refs[7:],
+        )
+
     return pl.pallas_call(
-        functools.partial(place_ffn_kernel, width // depth),
-        out_shape=(
-            jax.ShapeDtypeStruct((depth, hidden), F32),
-            jax.ShapeDtypeStruct((rows, width), F32),
-        ),
-        in_specs=[vmem],
-        out_specs=(vmem, vmem),
+        kernel,
+        grid=(chips,),
+        out_shape=out_shape,
+        in_specs=in_specs,
+        out_specs=out_specs,
         compiler_params=pltpu.CompilerParams(vmem_limit_bytes=VMEM_BYTES),
-        cost_estimate=pl.CostEstimate(flops=0, bytes_accessed=2**24, transcendentals=0),
-    )(sums)
-
-
-def place_late_kernel(tall, sum_ref, self_ref, kv_ref, *refs):
-    ctx, _, own = sum_ref.shape
-    depth, width = refs[0].shape
-    part = depth // (ctx // 2)
-    for src in range(ctx):
-        for k in range(5):
-            target = self_ref if k < 3 else kv_ref
-            at = (k if k < 3 else k - 3) * width + src * own
-            top = k * tall
-            target[:, at : at + own] = sum_ref[src, top : top + depth, :].astype(F32)
-        for w, target in enumerate(refs):
-            for block in range(width // 2 // own):
-                top = 5 * tall + (w * (width // 2 // own) + block) * part
-                at = (src % 2) * (width // 2) + block * own
-                rows = slice(src // 2 * part, src // 2 * part + part)
-                target[rows, at : at + own] = sum_ref[src, top : top + part, :].astype(F32)
-
-
-def place_late(sums, tall, depth, width):
-    vmem = pl.BlockSpec(memory_space=pltpu.VMEM)
-    small = jax.ShapeDtypeStruct((depth, width), F32)
-    return pl.pallas_call(
-        functools.partial(place_late_kernel, tall),
-        out_shape=(
-            jax.ShapeDtypeStruct((depth, 3 * width), F32),
-            jax.ShapeDtypeStruct((depth, 2 * width), F32),
-            small, small, small,
-        ),
-        in_specs=[vmem],
-        out_specs=(vmem,) * 5,
-        compiler_params=pltpu.CompilerParams(vmem_limit_bytes=VMEM_BYTES),
-        cost_estimate=pl.CostEstimate(flops=0, bytes_accessed=2**24, transcendentals=0),
-    )(sums)
+        cost_estimate=pl.CostEstimate(flops=0, bytes_accessed=2**25, transcendentals=0),
+    )(ffn_sums, late, late, late, done, done, done, late, *more)
 
 
 def swap(value, bit):
     count = lax.axis_size("ctx")
     return lax.ppermute(value, "ctx", [(i, i ^ bit) for i in range(count)])
-
-
-def across_groups(value):
-    count = lax.axis_size("fsdp")
-    me = lax.axis_index("fsdp")
-    total = lax.dynamic_index_in_dim(value, me, 0, keepdims=False).astype(F32)
-    for shift in range(1, count):
-        send = lax.dynamic_index_in_dim(value, (me + shift) % count, 0, keepdims=False)
-        got = lax.ppermute(send, "fsdp", [(i, (i + shift) % count) for i in range(count)])
-        total = total + got.astype(F32)
-    return total
 
 
 def pair_product(left, right):
@@ -1058,19 +1308,17 @@
     return (kept + got).astype(BF)
 
 
-def ctx_gather(value):
-    count = lax.axis_size("ctx")
-    full = lax.all_gather(value, "ctx", axis=0)
-    return full.reshape((count // 2, 2) + value.shape)
-
-
-def gather_all(pieces):
+def gather_joined(pieces):
     count = lax.axis_size("ctx")
     me = lax.axis_index("ctx")
     rows = pieces[0].shape[0] // count
     cut = [lax.dynamic_slice_in_dim(p, me * rows, rows, 0) for p in pieces]
     joined = jnp.concatenate(cut, axis=1)
-    full = lax.all_gather(joined, ("fsdp", "ctx"), axis=0, tiled=True)
+    return lax.all_gather(joined, ("fsdp", "ctx"), axis=0, tiled=True)
+
+
+def gather_all(pieces):
+    full = gather_joined(pieces)
     out, at = [], 0
     for p in pieces:
         out.append(full[:, at : at + p.shape[1]])
@@ -1172,13 +1420,15 @@
     blocks = ffn_in.shape[1] // width
     order = full_ffn_bias.reshape(groups, blocks, depth)
     order = jnp.moveaxis(order, 0, 1).reshape(-1, 1, 512)
-    layer_sum, grad_three, bias_parts, in_sum, out_sum = ffn(
+    half_rows = depth // 2
+    core = me % 2
+    self_rows = lax.dynamic_slice_in_dim(self_in, core * half_rows, half_rows, 0)
+    kv_rows = lax.dynamic_slice_in_dim(cross_kv, core * half_rows, half_rows, 0)
+    layer_sum, grad_three, bias_parts, in_sum, out_sum, kv_mine = ffn(
         normed_three, cotangent, second + full_out_bias,
-        jnp.broadcast_to(order, (order.shape[0], 8, 512)), ffn_weights,
+        jnp.broadcast_to(order, (order.shape[0], 8, 512)), ffn_weights, kv_rows,
     )
     layer_out = layer_sum.astype(BF)
-    late_in, late_kv, grad_three = lax.optimization_barrier((self_in, cross_kv, grad_three))
-    full_self_in, full_cross_kv = gather_all([late_in, late_kv])
     chips = ctx // 2
     part = depth // chips
     in_sum = in_sum.reshape(-1, groups, chips // 2, part, 256)
@@ -1188,13 +1438,15 @@
     back_three = normalize_back(unit_three, scale_three, gain[2], grad_three)
     grad_second = dy + back_three[0]
     branch_two = grad_second.astype(BF)
-    middle = [pair_product(cross_mixed, branch_two)]
+    chip_first = lambda value: jnp.moveaxis(value.reshape(groups, chips, part, -1), 1, 0)
+    cross_part = chip_first(pair_product(cross_mixed, branch_two))
     grad_cross_mixed = nt(branch_two, full_cross_out).astype(BF)
     got_shape = (max(chips // 2 - 1, 1),) + in_sum.shape[:2] + in_sum.shape[3:]
-    cross_moved, cross_dk, cross_dv, in_got, out_got = attend_backward(
+    cross_moved, cross_dk, cross_dv, in_got, out_got, cross_got, self_mine = attend_backward(
         True, heads, scale, prompt_offsets, all_cross_q.reshape(-1, 128), enc_keys, enc_values,
-        to_heads(grad_cross_mixed), att_cross, lse_cross, (in_sum, out_sum),
-        (got_shape, got_shape),
+        to_heads(grad_cross_mixed), att_cross, lse_cross,
+        (in_sum, out_sum, cross_part, self_rows),
+        (got_shape, got_shape, (chips - 1,) + cross_part.shape[1:], (groups,) + self_rows.shape),
     )
 
     def joined(value, mine, dim, got):
@@ -1206,10 +1458,16 @@
     grad_first = grad_second + back_two[0]
     branch_one = grad_first.astype(BF)
     grad_mixed = nt(branch_one, full_self_out).astype(BF)
-    middle.append(pair_product(normed_two, cross_dq))
-    middle.append(pair_product(mixed, branch_one))
-    middle = jnp.stack([m.reshape(groups, chips, part, -1) for m in middle])
-    middle = jnp.moveaxis(middle, 2, 0)
+    middle = jnp.stack(
+        [
+            chip_first(pair_product(normed_two, cross_dq)),
+            chip_first(pair_product(mixed, branch_one)),
+        ],
+        axis=1,
+    )
+    cross_part = joined(cross_part, me // 2, 0, cross_got).astype(BF)
+    enc_heads = jnp.concatenate([cross_dk[:, :own], cross_dv[:, :own]], axis=1)
+    kv_part = tn(all_encoder, enc_heads).astype(BF).reshape(groups, depth, 2 * own)
     ffn_sums = jnp.concatenate(
         [
             joined(in_sum, me // 4, 2, in_got),
@@ -1218,28 +1476,23 @@
         axis=0,
     )
     ffn_sums = jnp.moveaxis(ffn_sums.astype(BF), 1, 0)
-    grad_rows, full_self_in, full_cross_kv = lax.optimization_barrier(
-        (to_heads(grad_mixed), full_self_in, full_cross_kv)
+    carried = (middle, ffn_sums, cross_part, kv_part, self_mine, kv_mine)
+    moved, _, grad_head_in, column, *got = attend_backward(
+        False, heads, scale, prompt_offsets, queries, keys, values, to_heads(grad_mixed),
+        att_self, lse_self, carried,
+        [(value.shape[0] - 1,) + value.shape[1:] for value in carried[:4]]
+        + [value.shape for value in carried[4:]],
+        (all_normed.reshape(ctx, row_count, width),),
     )
-    moved, grad_heads, middle_got, ffn_got = attend_backward(
-        False, heads, scale, prompt_offsets, queries, keys, values, grad_rows,
-        att_self, lse_self, (middle, ffn_sums),
-        ((chips - 1,) + middle.shape[1:], (groups - 1,) + ffn_sums.shape[1:]),
-    )
+    grad_head_in = grad_head_in.reshape(width, 3, 128)[:, :, :own].reshape(width, 3 * own)
+    column = column[0].reshape(3, 128)[:, :own].reshape(-1)
     zone = lax.axis_index("fsdp")
-    ffn_sums = joined(ffn_sums, zone, 0, ffn_got).astype(BF)
-    middle = joined(middle, me // 2, 0, middle_got).astype(BF)
-    input_grad = token_grad(moved, full_self_in, tokens, gain[:1], grad_first)
-    grad_heads = grad_heads.reshape(-1, 3, 128)[:, :, :own].reshape(-1, 3 * own)
-
-    grad_ffn_in, grad_ffn_out = place_ffn(
-        ctx_gather(ffn_sums), depth, ffn_in.shape[1], ffn_out.shape[0], width
-    )
-
-    grad_head_in = tn(all_normed, grad_heads)
-    enc_heads = jnp.concatenate([cross_dk[:, :own], cross_dv[:, :own]], axis=1)
-    grad_head_kv = tn(all_encoder, enc_heads)
-    column = jnp.sum(grad_heads.astype(F32), axis=0)
+    middle = joined(middle, me // 2, 0, got[0]).astype(BF)
+    ffn_sums, cross_part, kv_part = [
+        joined(value, zone, 0, part_got).astype(BF)
+        for value, part_got in zip(carried[1:4], got[1:4])
+    ]
+    self_other, kv_other = got[4:]
     weight = head_in.reshape(width, 3 * own).astype(F32)
     grad_shift_one = jnp.sum(weight * column, axis=1)
     grad_gain_one = jnp.sum(weight * (grad_head_in - shift[0][:, None] * column), axis=1) / gain[0]
@@ -1263,28 +1516,47 @@
     bias = jnp.moveaxis(bias_parts[:, 0].reshape(blocks, groups, depth), 0, 1)
     totals = jnp.concatenate([totals, bias.reshape(groups, -1)], axis=1)
     count = totals.shape[1]
-    totals = jnp.pad(totals, ((0, 0), (0, 80 * own - count))).reshape(groups, 5, 16, own)
-    late = jnp.concatenate([grad_head_in, grad_head_kv], axis=1)
-    late = jnp.moveaxis(late.reshape(groups, depth, 5, own), 2, 1)
-    late = jnp.concatenate([late, totals], axis=2).astype(BF)
+    totals = jnp.pad(totals, ((0, 0), (0, 48 * own - count))).reshape(groups, 48, own)
+
+    def by_lanes(value, rows):
+        lead = value.shape[:-2]
+        value = jnp.moveaxis(value.reshape(lead + (rows, -1, own)), -2, -3)
+        return value.reshape(lead + (-1, own))
+
+    middle = jnp.moveaxis(by_lanes(middle, part), 1, 0).reshape(groups, -1, own)
+    late = by_lanes(grad_head_in.reshape(groups, depth, 3 * own), depth)
+    late = jnp.concatenate([middle, late.astype(BF), totals.astype(BF)], axis=1)
+    done = jnp.concatenate([by_lanes(cross_part, part), by_lanes(kv_part, depth)], axis=0)
     enc_sum = enc_heads.reshape(ctx, -1, 2 * own)
-    enc_sum = lax.all_to_all(enc_sum, "ctx", split_axis=0, concat_axis=0, tiled=True)
-    late, enc_sum = lax.optimization_barrier((late, enc_sum))
-    late = across_groups(late).astype(BF)
-    middle = across_groups(jnp.moveaxis(middle, 1, 0)).astype(BF)
-    middle = jnp.moveaxis(middle.reshape(3, part, -1, own), 2, 1)
-    packed = jnp.concatenate([late.reshape(-1, own), middle.reshape(-1, own)], axis=0)
-    packed = lax.all_gather(packed, "ctx", axis=0)
-    tall = depth + 16
-    grad_self_in, grad_cross_kv, grad_cross_out, grad_cross_q, grad_self_out = place_late(
-        packed, tall, depth, width
-    )
-    sums = packed[:, : 5 * tall].reshape(ctx, 5, tall, own)[:, :, depth:]
-    sums = jnp.sum(sums.astype(F32), axis=0).reshape(-1)[:count]
+    more = ()
+    if own == 128:
+        more = (moved, enc_sum, self_mine, self_other, kv_mine, kv_other)
+    all_ffn, all_done, all_late, *more_sums = finish(late, done, ffn_sums, width, more)
+    if more:
+        more = (more_sums[0], tokens, gain[:1], grad_first, more_sums[1])
+    (
+        grad_ffn_in, grad_ffn_out, grad_self_in, grad_cross_kv, grad_cross_out, grad_cross_q,
+        grad_self_out, *more_grads,
+    ) = place(all_ffn, all_done, all_late, ffn_in.shape[1], width, more)
+    grad_ffn_out = grad_ffn_out.reshape(-1, width)
+    sums = jnp.sum(all_late[:, -48:].astype(F32), axis=0).reshape(-1)[:count]
     mine, grad_ffn_bias = sums[: 13 * shard].reshape(13, shard), sums[13 * shard :]
-
-    enc_sum = jnp.transpose(enc_sum.reshape(ctx, -1, 2, own), (1, 2, 0, 3))
-    grad_encoder = nt(enc_sum.reshape(-1, 2 * width), full_cross_kv)
+    if more:
+        input_grad, grad_encoder = more_grads
+    else:
+
+        def whole(kept, other):
+            pair = jnp.where(core == 0, jnp.stack([kept, other]), jnp.stack([other, kept]))
+            return jnp.moveaxis(pair, 0, 1).reshape(width, -1)
+
+        cut = moved.reshape(ctx, row_count, 3, 128)[:, :, :, :own]
+        grads = jnp.transpose(cut, (1, 2, 0, 3)).reshape(row_count, 3 * width)
+        unit_one, scale_one = normalize(token_values)
+        grad_normed = nt(grads, whole(self_mine, self_other))
+        input_grad = grad_first + normalize_back(unit_one, scale_one, gain[0], grad_normed)[0]
+        enc_sum = lax.all_to_all(enc_sum, "ctx", split_axis=0, concat_axis=0, tiled=True)
+        enc_sum = jnp.transpose(enc_sum.reshape(ctx, -1, 2, own), (1, 2, 0, 3))
+        grad_encoder = nt(enc_sum.reshape(-1, 2 * width), whole(kv_mine, kv_other))
     return (
         layer_out, input_grad, grad_encoder, mine[:3], mine[3:12], grad_self_in, grad_self_out,
         grad_cross_q, grad_cross_kv, grad_cross_out, grad_ffn_in, grad_ffn_bias, grad_ffn_out, mine[12],

time: 693 us -> 639 us (0.922)
  waiting for transfers between devices: 86.4 us -> 40.6 us
  Pallas kernels: 429 us -> 448 us
  starting transfers between devices: 14 us -> 1.91 us
  matrix products: 49.7 us -> 38.9 us
    pallas_call x3 -> x2, Pallas kernels: 26.3 us -> 72.9 us  [the longest x1 60.3 us: finish(): pl.pallas_call(functools.partial(finish_kernel, bool(more)), out_shape=ou...]
    ppermute x6 -> x0, waiting for transfers between devices: 33.3 us -> none  [across_groups(): lax.ppermute(send, 'fsdp', [(i, (i + shift) % count) for i in range(count)])]
    all_gather x4 -> x1, waiting for transfers between devices: 17.9 us -> 0.01 us  [gather_joined(): return lax.all_gather(joined, ('fsdp', 'ctx'), axis=0, tiled=True)]
    pallas_call x2, Pallas kernels: 178 us -> 161 us  [attend_backward(): pl.pallas_call(functools.partial(attend_backward_kernel, cross, heads, of...]
    pallas_call x1, Pallas kernels: 68.7 us -> 53.5 us  [project(): pl.pallas_call(functools.partial(project_kernel, own, scale), out_shape=(...]
    ppermute x6 -> x0, starting transfers between devices: 8.93 us -> none  [across_groups(): lax.ppermute(send, 'fsdp', [(i, (i + shift) % count) for i in range(count)])]
    dot_general x8 -> x7, matrix products: 22.7 us -> 14.6 us  [tn(): lax.dot_general(left, right, (((0,), (0,)), ((), ())), preferred_element_...]
  transfers between devices with their start and end apart: 15 -> 5, of which waited for: 6 -> 1; matrix products, arithmetic and copies ran while one was open for 17% -> 11% of each run, Pallas kernels for 37% -> 24%
where the time goes in v3:
time: 639 us; the launch traced here: 628 us
  Pallas kernels  448 us (70%)
  local copies, waits for them, and re-layouts  45 us (7%)
  waiting for transfers between devices  40.6 us (6%)
  matrix products  38.9 us (6%)
  other arithmetic  37.7 us (6%)
  between operations  16.1 us (3%)
    pallas_call x2, Pallas kernels, attend_backward(): pl.pallas_call(functools.partial(attend_backward_kernel, cross, heads, of...  161 us
    pallas_call x2, Pallas kernels, attend_forward(): pl.pallas_call(functools.partial(attend_forward_kernel, cross, heads, off...  96.5 us
    pallas_call x1, Pallas kernels, ffn(): pl.pallas_call(functools.partial(ffn_kernel, steps, groups), grid=(steps...  63.5 us
    pallas_call x1, Pallas kernels, finish(): pl.pallas_call(functools.partial(finish_kernel, bool(more)), out_shape=ou...  60.3 us
    pallas_call x1, Pallas kernels, project(): pl.pallas_call(functools.partial(project_kernel, own, scale), out_shape=(...  53.5 us
    all_gather x1, waiting for transfers between devices, gather_ffn(): return lax.all_gather(joined, ('fsdp', 'ctx'), axis=0, tiled=True)  40.5 us
    dot_general x7, matrix products, tn(): lax.dot_general(left, right, (((0,), (0,)), ((), ())), preferred_element_...  14.6 us
    dot_general x4, matrix products, nn(): lax.dot_general(left, right, (((1,), (0,)), ((), ())), preferred_element_...  13.6 us
  transfers between devices with their start and end apart: 5, of which 1 were waited for; matrix products, arithmetic and copies ran while one was open for 11% of the time, Pallas kernels for 24%

profile of v3, /device:TPU:0, one launch (start us, length us, event | category | flops | bytes accessed | tf_op | source)
XLA Modules:
  0.0 627.7 jit_solution(6724134684919810913)
XLA Ops:
  7.2 1.0 constant_dynamic-slice_fusion.8
  9.9 1.0 constant_dynamic-slice_fusion.5
  13.0 1.6 copy.115
  14.5 1.0 constant_dynamic-slice_fusion.9
  16.6 0.9 dynamic-slice_reduce_fusion
  19.5 53.5 %shard_map.254 = (bf16[8,512,1024]{2,1,0:T(8,128)(2,1)}, bf16[8,512,128]{2,1,0:T(8,128)(2,1)}, bf16[8,512,128]{2,1,0:T(8,128)(2,1)}, bf16[8,512,128]{2,1,0:T(8,1...) custom-call(bf16[512,1024]{1,0:T(8,128)(2,1)} %refs_9_.1, bf16[32,256]{1,0:T(8,128)(2,1)} %fusion.63.small_ref, ...), custom_call_target="tpu_custom_call" | custom-call | flops 49999998976 | bytes 33554432 | tf_op jit(solution)/shard_map/pallas_call | solution.py:775
  73.0 45.9 %shard_map.255 = (bf16[8,512,128]{2,1,0:T(8,128)(2,1)}, f32[128,4096]{1,0:T(8,128)}, f32[8,4096]{1,0:T(8,128)}, bf16[8,256,1024]{2,1,0:T(8,128)(2,1)}, bf16[4,256,256]{2,1,0:T(8,128)(2,1)}) custom-call(s32[1,1]{1,0:T(1,128)S(6)} %copy.186.offs_ref, bf16[4096,128]{1,0:T(8,128)(2,1)} %bitcast.240, bf16[4096,128]{1,0:T(8,128)(2,1)} %bitcast.242, ...), custom_call_target="tpu_custom_call" | custom-call | flops 40000000000 | bytes 8388608 | tf_op jit(solution)/shard_map/pallas_call | solution.py:406
  118.9 2.3 copy.118
  121.2 3.6 fusion.79
  127.9 0.9 fusion.28.v_ref
  128.8 3.6 fusion.77
  133.7 1.0 copy-done.15
  134.7 2.9 multiply_convert_fusion
  138.1 1.3 copy.120
  139.4 50.7 %shard_map.256 = (bf16[8,512,128]{2,1,0:T(8,128)(2,1)}, f32[128,4096]{1,0:T(8,128)}, f32[8,4096]{1,0:T(8,128)}, bf16[8,512,128]{2,1,0:T(8,128)(2,1)}) custom-call(s32[1,1]{1,0:T(1,128)S(6)} %copy.186.offs_ref, bf16[8,512,128]{2,1,0:T(8,128)(2,1)} %bitcast.191, bf16[2048,128]{1,0:T(8,128)(2,1)} %slice.233.k_ref, bf16[2048,128]{1,0:T(8,128)(2,1)} %fusion.28.v_ref), custom_call_target="tpu_custom_call" | custom-call | flops 40000000000 | bytes 8388608 | tf_op jit(solution)/shard_map/pallas_call | solution.py:406
  190.1 1.5 copy.121
  191.6 3.6 fusion.78
  195.5 2.2 broadcast_add_fusion
  197.7 40.5 %all-gather.5.cloned.1.call-done.win_ref.wout_ref = bf16[1024,8192]{1,0:T(8,128)(2,1)} async-done(((bf16[32,8192]{1,0:T(8,128)(2,1)}), bf16[1024,8192]{1,0:T(8,128)(2,1)}) %all-gather.5.cloned.1.call-update) | async-done | bytes 16777232 | tf_op jit(solution)/shard_map/all_gather | solution.py:1345
  238.9 63.5 %shard_map.257 = (f32[512,1024]{1,0:T(8,128)}, f32[512,1024]{1,0:T(8,128)}, f32[8,8,512]{2,1,0:T(8,128)}, bf16[8,512,256]{2,1,0:T(8,128)(2,1)}, bf16[4,2,512,256...) custom-call(bf16[512,1024]{1,0:T(8,128)(2,1)} %get-tuple-element.131.n_ref, bf16[512,1024]{1,0:T(8,128)(2,1)} %dy_ref.1, ...), custom_call_target="tpu_custom_call" | custom-call | flops 30000001024 | bytes 67108864 | tf_op jit(solution)/shard_map/pallas_call | solution.py:984
  302.4 2.6 multiply_reduce_fusion
  305.1 2.2 fusion.71
  307.3 1.0 copy-done.20
  308.2 1.7 convolution_convert_fusion.2
  309.9 0.9 constant_dynamic-slice_fusion.2.refs_3_
  310.9 3.2 fusion.19
  314.6 1.3 copy.126
  318.3 0.9 fusion.64
  319.9 2.7 convert_element_type.199
  322.6 1.9 add_convert_fusion.2
  324.6 1.1 copy.181
  325.6 63.0 %shard_map.258 = (bf16[8,512,128]{2,1,0:T(8,128)(2,1)}, bf16[2048,128]{1,0:T(8,128)(2,1)}, bf16[2048,128]{1,0:T(8,128)(2,1)}, bf16[1,8,4,64,256]{4,3,2,1,0:T(8,1...) custom-call(s32[1,1]{1,0:T(1,128)S(6)} %copy.186.offs_ref, ...), custom_call_target="tpu_custom_call" | custom-call | flops 60000002048 | bytes 8388608 | tf_op jit(solution)/shard_map/pallas_call | solution.py:643
  388.7 1.1 constant_dynamic-update-slice_fusion.4
  389.8 1.2 constant_dynamic-update-slice_fusion.3
  391.0 2.1 convolution_convert_fusion.3
  393.2 0.9 convert_reduce_fusion.2
  394.8 1.3 copy.128
  396.1 3.2 convolution_convert_fusion.1
  399.3 1.7 collective-permute-start.1
  400.9 3.7 multiply_reduce_fusion.1
  404.6 2.1 fusion.72
  406.7 1.7 convolution_convert_fusion
  408.6 3.9 fusion.16
  412.5 1.6 copy.131
  414.0 1.3 copy.132
  415.3 1.0 fusion.35.refs_2_
  417.1 1.0 dynamic-slice_convert_fusion
  418.3 2.1 fusion.2
  420.7 1.6 fusion.1
  422.3 1.5 fusion.refs_1_
  424.6 2.1 add_convert_fusion.1
  426.8 1.9 add_convert_fusion
  428.8 1.5 pad_maximum_fusion.refs_0_
  430.4 98.1 %shard_map.259 = (bf16[8,512,384]{2,1,0:T(8,128)(2,1)}, bf16[8,512,384]{2,1,0:T(8,128)(2,1)}, f32[1024,384]{1,0:T(8,128)}, f32[8,384]{1,0:T(8,128)}, bf16[3,2,4,...) custom-call(s32[1,1]{1,0:T(1,128)S(6)} %copy.186.offs_ref, ...), custom_call_target="tpu_custom_call" | custom-call | flops 60000002048 | bytes 8388608 | tf_op jit(solution)/shard_map/pallas_call | solution.py:643
  528.5 1.8 convert_reduce_fusion
  530.3 1.0 fusion.29.ffn_ref
  531.5 1.1 convert_reduce_fusion.4
  533.2 1.8 convert_reduce_fusion.1
  535.8 0.9 slice_reduce_fusion
  539.5 1.4 fusion.75
  543.1 1.2 pad_maximum_fusion.2.late_ref
  544.3 60.3 %shard_map.260 = (bf16[8,16,64,256]{3,2,1,0:T(8,128)(2,1)}, bf16[8,768,128]{2,1,0:T(8,128)(2,1)}, bf16[8,1328,128]{2,1,0:T(8,128)(2,1)}, f32[512,1024]{1,0:T(8,128)}, f32[256,1024]{1,0:T(8,128)}) custom-call(bf16[4,1328,128]{2,1,0:T(8,128)(2,1)} %pad_maximum_fusion.2.late_ref, bf16[768,128]{1,0:T(8,128)(2,1)} %pad_maximum_fusion.5.done_ref, ...), custom_call_target="tpu_custom_call" | custom-call | flops 49999998976 | bytes 33554432 | tf_op jit(solution)/shard_map/pallas_call | solution.py:1175
  604.6 0.9 convert_reduce_fusion.6
  607.9 12.6 %shard_map.261 = (f32[256,4096]{1,0:T(8,128)}, f32[4,4,64,1024]{3,2,1,0:T(8,128)}, f32[256,3072]{1,0:T(8,128)}, f32[256,2048]{1,0:T(8,128)}, f32[256,1024]{1,0:T...) custom-call(bf16[8,16,64,256]{3,2,1,0:T(8,128)(2,1)} %get-tuple-element.102.refs, ...), custom_call_target="tpu_custom_call" | custom-call | bytes 33554432 | tf_op jit(solution)/shard_map/pallas_call | solution.py:1286
  (199 shorter events, 27.4 us)
Async XLA Ops:
  7.2 4.2 copy-start
  7.2 121.6 %all-gather.3.cloned.1.call-start = ((), (), s32[]{:S(2)}) async-start(), calls=%async_computation | async-start | bytes 6488064 | tf_op jit(solution)/shard_map/all_gather | solution.py:1317
  9.8 228.4 %all-gather.5.cloned.1.call-start = ((), (), s32[]{:S(2)}) async-start(), calls=%async_computation.1 | async-start | bytes 17301504 | tf_op jit(solution)/shard_map/all_gather | solution.py:1345
  11.4 1.6 copy-start.7
  12.6 3.8 copy-start.47
  12.6 3.8 copy-start.49
  12.6 3.8 copy-start.10
  14.5 4.3 copy-start.46
  14.5 4.3 copy-start.48
  121.2 4.5 copy-start.32
  125.8 0.6 copy-start.29
  127.0 5.8 copy-start.30
  132.4 1.3 copy-start.2
  132.4 1.3 copy-start.34
  132.7 4.8 copy-start.36
  133.7 1.0 copy-start.15
  302.4 2.7 copy-start.4
  302.4 2.7 copy-start.19
  307.3 1.0 copy-start.20
  307.3 2.7 copy-start.8
  309.9 12.7 %collective-permute-start = (bf16[1024,512]{1,0:T(8,128)(2,1)}, bf16[1024,512]{1,0:T(8,128)(2,1)}, u32[]{:S(2)}, u32[]{:S(2)}) collective-permute-start(bf16[1024,512]{1,0:T(8,128)(2,1)} %convolution_convert_fusion.2), channel_id=1, source_target_pairs={{0,4},{4,0},{8,12},{12,8},{16,20},{20,16},{24,28},{28,24},{1,5},{5... | collective-permute-start | bytes 3145736 | tf_op jit(solution)/shard_map/ppermute | solution.py:1299
  315.9 6.7 %copy-start.21 = (bf16[512,1024]{1,0:T(8,128)(2,1)S(1)}, bf16[512,1024]{1,0:T(8,128)(2,1)}, u32[]{:S(2)}) copy-start(bf16[512,1024]{1,0:T(8,128)(2,1)} %copy-done.20) | copy-start | bytes 3145732
  325.6 65.4 %copy-start.50 = (bf16[8,256,1024]{2,1,0:T(8,128)(2,1)S(1)}, bf16[8,256,1024]{2,1,0:T(8,128)(2,1)}, u32[]{:S(2)}) copy-start(bf16[8,256,1024]{2,1,0:T(8,128)(2,1)} %get-tuple-element.70) | copy-start | bytes 12582916
  391.0 2.1 copy-start.27
  391.0 2.1 copy-start.24
  391.0 3.0 copy-start.6
  394.8 6.2 copy-start.3
  394.8 6.2 copy-start.31
  394.8 6.2 copy-start.35
  394.8 6.2 copy-start.37
  396.1 4.9 copy-start.17
  399.3 5.4 copy-start.5
  399.3 25.2 %collective-permute-start.1 = (bf16[1024,512]{1,0:T(8,128)(2,1)}, bf16[1024,512]{1,0:T(8,128)(2,1)}, u32[]{:S(2)}, u32[]{:S(2)}) collective-permute-start(bf16[1024,512]{1,0:T(8,128)(2,1)} %convolution_convert_fusion.1), channel_id=1, source_target_pairs={{0,4},{4,0},{8,12},{12,8},{16,20},{20,16},{24,28},{28,24},{1,5},{5... | collective-permute-start | bytes 3145736 | tf_op jit(solution)/shard_map/ppermute | solution.py:1299
  404.6 2.1 copy-start.14
  406.7 1.9 copy-start.22
  408.4 18.3 %collective-permute-start.2 = (bf16[1024,512]{1,0:T(8,128)(2,1)}, bf16[1024,512]{1,0:T(8,128)(2,1)}, u32[]{:S(2)}, u32[]{:S(2)}) collective-permute-start(bf16[1024,512]{1,0:T(8,128)(2,1)} %convolution_convert_fusion), channel_id=1, source_target_pairs={{0,4},{4,0},{8,12},{12,8},{16,20},{20,16},{24,28},{28,24},{1,5},{5... | collective-permute-start | bytes 3145736 | tf_op jit(solution)/shard_map/ppermute | solution.py:1299
  412.5 2.9 copy-start.12
  414.0 4.2 copy-start.45
  416.4 0.7 copy-start.26
  417.1 3.3 copy-start.11
  418.3 2.4 copy-start.25
  422.3 2.1 copy-start.16
  422.3 2.3 copy-start.18
  423.8 0.6 copy-start.43
  424.4 2.4 copy-start.23
  530.3 1.0 copy-start.28
  535.4 1.4 copy-start.9
  535.4 1.7 copy-start.13
  535.4 1.7 copy-start.38
  537.7 4.5 copy-start.39
  537.7 4.5 copy-start.40
  537.7 4.5 copy-start.41
  537.7 4.5 copy-start.42
  537.7 4.5 copy-start.44
  537.7 4.7 copy-start.33
  607.9 12.6 %copy-start.1 = (bf16[1024,1024]{1,0:T(8,128)(2,1)S(1)}, bf16[1024,1024]{1,0:T(8,128)(2,1)}, u32[]{:S(2)}) copy-start(bf16[1024,1024]{1,0:T(8,128)(2,1)} %param.27) | copy-start | bytes 6291460
Sparse Core Ops, SparseCore 0:
  11.5 95.2 all-gather.2
  110.2 128.0 all-gather.4

commit v4 on v3

--- a/solution.py
+++ b/solution.py
@@ -212,18 +212,21 @@
 
 def attend_forward_kernel(cross, heads, conts, offs_ref, q_ref, k_ref, v_ref, *refs):
     if cross:
-        mixed_ref, att_ref, lse_ref, q_out, *refs = refs
+        rows_ref, mixed_ref, att_ref, lse_ref, q_out, rows_all, pair_all, *refs = refs
     else:
-        enc_ref, kv_ref, mixed_ref, att_ref, lse_ref, enc_all, kv_all, *refs = refs
-    total, peak, value_t, score_a, score_b, stage, send_sem, recv_sem, own_sem, *refs = refs
+        pair_ref, enc_ref, kv_ref, *refs = refs
+        mixed_ref, att_ref, lse_ref, pair_all, enc_all, kv_all, *refs = refs
+    total, peak, value_t, score_a, score_b, stage, send_sem, recv_sem, own_sem, pair_sem, *refs = refs
     me, count = lax.axis_index("ctx"), lax.axis_size("ctx")
     rows = att_ref.shape[1]
     tiles = rows // TILE
     key_tiles = k_ref.shape[0] // TILE
     prompt = rows - conts * CONT
     prompt_tiles = prompt // TILE
-    greet(others("ctx") + ([] if cross else others("fsdp")))
+    greet(others("ctx") + others("fsdp"))
     send, arrived, sent = exchange(stage, mixed_ref, send_sem, recv_sem, own_sem)
+    zone = lax.axis_index("fsdp")
+    pair_copy = core_swap(rows_all if cross else pair_ref, pair_all, pair_sem)
     if not cross:
         gather_send, gather_recv, gather_own, kv_send, kv_recv = refs
         enc_start, enc_land, enc_rest, enc_done = plane_gather(
@@ -233,15 +236,21 @@
         first = group_spread(kv_ref, kv_all, kv_send, kv_recv, 0)
         local = [
             pltpu.make_async_copy(enc_ref, enc_all.at[me], gather_own.at[0]),
-            pltpu.make_async_copy(kv_ref, kv_all.at[lax.axis_index("fsdp")], gather_own.at[1]),
+            pltpu.make_async_copy(kv_ref, kv_all.at[zone], gather_own.at[1]),
         ]
         for copy in first + local:
             copy.start()
     if cross:
-        q_all, q_send, q_recv, q_own = refs
+        q_all, q_send, q_recv, q_own, rows_send, rows_recv = refs
         put, got, put_done = exchange(q_ref, q_all, q_send, q_recv, q_own)
         for step in range(count):
             put((me + step) % count)
+        spread = group_spread(rows_ref, rows_all, rows_send, rows_recv, 0)
+        keep_rows = pltpu.make_async_copy(rows_ref, rows_all.at[zone], pair_sem.at[2])
+        for copy in spread + [keep_rows]:
+            copy.start()
+    else:
+        pair_copy.start()
 
     for tile in range(key_tiles):
         at = pl.ds(tile * TILE, TILE)
@@ -329,7 +338,16 @@
             lse_ref[head : head + 1, tile_rows(i)] = peak[head][:1] + jnp.log(part[64:65])
         stage[i] = att_ref[:, tile_rows(i)].T.astype(BF)
         send(i)
-        if not cross:
+        if cross:
+
+            @pl.when(step == tiles - 2)
+            def _():
+                keep_rows.wait()
+                for copy in spread:
+                    copy.wait_recv()
+                pair_copy.start()
+
+        else:
 
             @pl.when(step == tiles - 3)
             def _():
@@ -344,8 +362,11 @@
     for step in range(count):
         arrived((me + step) % count)
     sent()
+    pair_copy.wait()
     if cross:
         put_done()
+        for copy in spread:
+            copy.wait_send()
     else:
         for index in range(2, count // 2 - 1):
             enc_land(index)
@@ -357,6 +378,11 @@
         for copy in local:
             copy.wait()
         enc_done()
+
+
+def core_swap(source, target, sems):
+    there = {"ctx": flipped_bits(lax.axis_index("ctx"), 1)}
+    return remote(source, target, sems.at[0], sems.at[1], there)
 
 
 def group_spread(source, target, send_sem, recv_sem, sem):
@@ -389,20 +415,23 @@
         pltpu.VMEM((heads, TILE, TILE), F32),
         pltpu.VMEM((heads, TILE, TILE), F32),
         pltpu.VMEM((count, TILE, 128), BF),
-        dma((count,)), dma((count,)), dma,
+        dma((count,)), dma((count,)), dma, dma((3,)),
     ]
+    groups = lax.axis_size("fsdp")
     if cross:
-        outs.append(tiles)
+        spread = jax.ShapeDtypeStruct((groups,) + extra[0].shape, BF)
+        outs += [tiles, spread, spread]
         scratch += [pltpu.VMEM((count, TILE, 128), BF), dma((count,)), dma((count,)), dma]
-        places = [vmem]
+        scratch += [dma((groups - 1,)), dma((groups - 1,))]
+        places = [vmem, hbm, hbm]
     else:
-        enc, kv = extra
-        groups = lax.axis_size("fsdp")
+        near, enc, kv = extra
+        outs.append(jax.ShapeDtypeStruct(near.shape, BF))
         outs.append(jax.ShapeDtypeStruct((count,) + enc.shape, BF))
         outs.append(jax.ShapeDtypeStruct((groups,) + kv.shape, BF))
         scratch += [dma((count + 1,)), dma((count + 1,)), dma((2,))]
         scratch += [dma((groups - 1,)), dma((groups - 1,))]
-        places = [hbm, hbm]
+        places = [hbm] * 3
     return pl.pallas_call(
         functools.partial(attend_forward_kernel, cross, heads, offsets.shape[1]),
         out_shape=outs,
@@ -468,10 +497,6 @@
     out = chip_copies(sources[0], targets[0], send_sem, recv_sem, 0)
     for source, target in zip(sources[1:4], targets[1:4]):
         out = out + group_copies(source, target, send_sem, recv_sem, len(out))
-    for source, target in zip(sources[4:], targets[4:]):
-        sem = len(out)
-        there = {"ctx": flipped_bits(lax.axis_index("ctx"), 1)}
-        out.append(remote(source, target, send_sem.at[sem], recv_sem.at[sem], there))
     return out
 
 
@@ -490,7 +515,7 @@
     if cross:
         stage, *refs = refs
     (
-        do_all, key_t, delta, dq_sum, dk_sum, dv_sum,
+        do_all, key_t, delta, dq_sum, dk_sum, dv_sum, score_a, score_b, grad_a, grad_b,
         send_sem, recv_sem, own_sem, do_send, do_recv, do_own, carry_send, carry_recv, *refs,
     ) = refs
     if cross:
@@ -499,7 +524,11 @@
             sources[3], targets[3].at[lax.axis_index("fsdp")], keep_sem
         )
     else:
-        normed, normed_sem = refs
+        normed, normed_sem, *pair_sems = refs
+        pair_copies = [
+            core_swap(sources[4 + index], targets[4 + index], pair_sems[index])
+            for index in range(2)
+        ]
         product_ref[...] = jnp.zeros_like(product_ref)
         column_ref[...] = jnp.zeros_like(column_ref)
     me, count = lax.axis_index("ctx"), lax.axis_size("ctx")
@@ -515,6 +544,9 @@
         copy.start()
     if cross:
         keep_own.start()
+    else:
+        for copy in pair_copies:
+            copy.start()
     send, arrived, sent = exchange(stage, moved_ref, send_sem, recv_sem, own_sem)
     dq_sum[...] = jnp.zeros_like(dq_sum)
     dk_sum[...] = jnp.zeros_like(dk_sum)
@@ -531,20 +563,28 @@
                 both[64 * head : 64 * head + 64], axis=0, keepdims=True
             )
 
-    def pair(i, j, shown):
+    def score(i, j, kept):
         row, at = tile_rows(i), tile_rows(j)
         q, do, k, v = q_ref[row, :], do_all[i], k_ref[at, :], v_ref[at, :]
         for head in range(heads):
-            q_own, do_own = head_lanes(head, q), head_lanes(head, do)
-            weights = jnp.exp(nt(k, q_own) - lse_ref[head : head + 1, row])
+            kept[0][head] = nt(k, head_lanes(head, q))
+            kept[1][head] = nt(v, head_lanes(head, do))
+
+    def settle(i, j, kept, shown=None):
+        row, at = tile_rows(i), tile_rows(j)
+        q, do = q_ref[row, :], do_all[i]
+        for head in range(heads):
+            weights = jnp.exp(kept[0][head] - lse_ref[head : head + 1, row])
             if shown is not None:
                 weights = jnp.where(shown, weights, 0.0)
-            weight_grad = nt(v, do_own)
-            score_grad = (weights * (weight_grad - delta[head : head + 1, row])).astype(BF)
-            dv_sum[at, :] += nn(weights.astype(BF), do_own)
-            dk_sum[at, :] += nn(score_grad, q_own)
+            score_grad = weights * (kept[1][head] - delta[head : head + 1, row])
+            score_grad = score_grad.astype(BF)
+            dv_sum[at, :] += nn(weights.astype(BF), head_lanes(head, do))
+            dk_sum[at, :] += nn(score_grad, head_lanes(head, q))
             own = slice(64 * head, 64 * head + 64)
             dq_sum[own, row] += nn(key_t[own, at], score_grad)
+
+    even, odd = (score_a, grad_a), (score_b, grad_b)
 
     def shown_of(i, j):
         if conts == 1:
@@ -560,11 +600,12 @@
         i = (me + step) % count
         ready(i)
 
-        def plain(j, carry):
-            pair(i, j, None)
-            return carry
-
-        lax.fori_loop(0, key_tiles, plain, 0)
+        both = (even, odd)
+        score(i, 0, even)
+        for j in range(key_tiles):
+            if j + 1 < key_tiles:
+                score(i, j + 1, both[(j + 1) % 2])
+            settle(i, j, both[j % 2])
         stage[i] = queries_back(i)
         send(i)
         return carry
@@ -574,24 +615,68 @@
         fetch = pltpu.make_async_copy(normed_ref.at[i], normed, normed_sem)
         fetch.start()
 
+        def tiles_of(turn):
+            p = (i + turn) % count
+            return jnp.maximum(i, p), jnp.minimum(i, p)
+
+        def score_turn(turn, kept):
+            high, low = tiles_of(turn)
+            score(high, low, kept)
+
+        def settle_turn(turn, kept):
+            high, low = tiles_of(turn)
+            settle(high, low, kept, shown_of(high, low))
+
+        diagonal = visible(0, 0, TILE, TILE, 0, None) if conts == 1 else shown_of(i, i)
+        left = count - 1 - step
+
         @pl.when(step == 0)
         def _():
             ready(i)
-
-        pair(i, i, visible(0, 0, TILE, TILE, 0, None) if conts == 1 else shown_of(i, i))
-
-        def other(turn, carry):
-            p = (i + turn) % count
-
-            @pl.when(step == 0)
+            score(i, i, even)
+            settle(i, i, even, diagonal)
+
+            def fresh(turn, carry):
+                ready((i + turn) % count)
+                score_turn(turn, even)
+                settle_turn(turn, even)
+                return carry
+
+            lax.fori_loop(1, count, fresh, 0)
+
+        @pl.when(step > 0)
+        def _():
+            score(i, i, even)
+
+            @pl.when(left > 0)
             def _():
-                ready(p)
-
-            high, low = jnp.maximum(i, p), jnp.minimum(i, p)
-            pair(high, low, shown_of(high, low))
-            return carry
-
-        lax.fori_loop(1, count - step, other, 0)
+                score_turn(1, odd)
+                settle(i, i, even, diagonal)
+
+            @pl.when(left == 0)
+            def _():
+                settle(i, i, even, diagonal)
+
+            def two(turn, carry):
+                at = 1 + 2 * turn
+                score_turn(at + 1, even)
+                settle_turn(at, odd)
+                score_turn(at + 2, odd)
+                settle_turn(at + 1, even)
+                return carry
+
+            lax.fori_loop(0, jnp.maximum(left - 1, 0) // 2, two, 0)
+
+            @pl.when(left % 2 == 1)
+            def _():
+                settle_turn(left, odd)
+
+            @pl.when((left > 0) & (left % 2 == 0))
+            def _():
+                score_turn(left, even)
+                settle_turn(left - 1, odd)
+                settle_turn(left, even)
+
         stage[i, :, :128] = queries_back(i)
         stage[i, :, 128:256] = dk_sum[tile_rows(i), :].astype(BF)
         stage[i, :, 256:] = dv_sum[tile_rows(i), :].astype(BF)
@@ -614,6 +699,9 @@
     put_done()
     if cross:
         keep_own.wait()
+    else:
+        for copy in pair_copies:
+            copy.wait()
     for copy in carry_copies:
         copy.wait_send()
         copy.wait_recv()
@@ -638,7 +726,7 @@
             jax.ShapeDtypeStruct((normed[0].shape[2], wide), F32),
             jax.ShapeDtypeStruct((8, wide), F32),
         ]
-        carries = count // 2 - 1 + (lax.axis_size("fsdp") - 1) * 3 + 2
+        carries = count // 2 - 1 + (lax.axis_size("fsdp") - 1) * 3
     targets = [jax.ShapeDtypeStruct(shape, BF) for shape in target_shapes]
     return pl.pallas_call(
         functools.partial(
@@ -657,11 +745,14 @@
             pltpu.VMEM((128, count * TILE), F32),
             pltpu.VMEM((keys, 128), F32),
             pltpu.VMEM((keys, 128), F32),
+        ]
+        + [pltpu.VMEM((heads, TILE, TILE), F32)] * 4
+        + [
             dma((count,)), dma((count,)), dma,
             dma((count,)), dma((count,)), dma,
             dma((carries,)), dma((carries,)),
         ]
-        + ([dma] if cross else [pltpu.VMEM(normed[0].shape[1:], BF), dma]),
+        + ([dma] if cross else [pltpu.VMEM(normed[0].shape[1:], BF), dma, dma((2,)), dma((2,))]),
         compiler_params=pltpu.CompilerParams(
             vmem_limit_bytes=VMEM_BYTES, collective_id=3 if cross else 4,
             has_side_effects=True,
@@ -673,13 +764,15 @@
 
 
 def project_kernel(
-    own, scale, tokens_ref, small_ref, head_ref, normed_ref, q_ref, k_ref, v_ref,
-    small_all, head_all, all_tokens, staged, token_send, token_recv, part_send, part_recv,
-    own_sem, stage_sem,
+    own, scale, tokens_ref, small_ref, head_ref, rows_ref, normed_ref, q_ref, k_ref, v_ref,
+    small_all, head_all, rows_all, all_tokens, staged, token_send, token_recv, part_send, part_recv,
+    own_sem, stage_sem, rows_send, rows_recv,
 ):
     me, zone = lax.axis_index("ctx"), lax.axis_index("fsdp")
     count, groups = lax.axis_size("ctx"), lax.axis_size("fsdp")
     chips = count // 2
+    spread = group_spread(rows_ref, rows_all, rows_send, rows_recv, 0)
+    keep_rows = pltpu.make_async_copy(rows_ref, rows_all.at[zone], own_sem.at[3])
     shard = small_ref.shape[1]
     sibling = {"ctx": flipped_bits(me, 1)}
     near = [flipped_bits(me, 2 * other) for other in range(1, chips)]
@@ -705,6 +798,8 @@
 
     start, land, rest, done = plane_gather(tokens_ref, all_tokens, token_send, token_recv)
     start()
+    for copy in spread + [keep_rows]:
+        copy.start()
     for copy in local:
         copy.wait()
     for copy in parts:
@@ -762,10 +857,14 @@
         save(order[step], step % 2).wait()
     for copy in parts:
         copy.wait_send()
+    keep_rows.wait()
+    for copy in spread:
+        copy.wait_send()
+        copy.wait_recv()
     done()
 
 
-def project(own, scale, tokens, small, head_in):
+def project(own, scale, tokens, small, head_in, rows_part):
     count, groups = lax.axis_size("ctx"), lax.axis_size("fsdp")
     rows, width = tokens.shape
     vmem = pl.BlockSpec(memory_space=pltpu.VMEM)
@@ -779,15 +878,16 @@
             lanes, lanes, lanes,
             jax.ShapeDtypeStruct((groups,) + small.shape, BF),
             jax.ShapeDtypeStruct((groups,) + head_in.shape, BF),
+            jax.ShapeDtypeStruct((groups,) + rows_part.shape, BF),
         ),
-        in_specs=[hbm, hbm, hbm],
-        out_specs=(hbm,) + (vmem,) * 5,
+        in_specs=[hbm, hbm, hbm, hbm],
+        out_specs=(hbm,) + (vmem,) * 5 + (hbm,),
         scratch_shapes=[
             pltpu.VMEM((count, rows, width), BF),
             pltpu.VMEM((2, rows, width), BF),
             dma((count + 1,)), dma((count + 1,)),
             dma((2, groups - 1)), dma((2, groups - 1)),
-            dma((3,)), dma((2,)),
+            dma((4,)), dma((2,)), dma((groups - 1,)), dma((groups - 1,)),
         ],
         compiler_params=pltpu.CompilerParams(
             vmem_limit_bytes=VMEM_BYTES, collective_id=5, has_side_effects=True
@@ -795,7 +895,7 @@
         cost_estimate=pl.CostEstimate(
             flops=50 * 10**9, bytes_accessed=2**25, transcendentals=0
         ),
-    )(tokens, small, head_in)
+    )(tokens, small, head_in, rows_part)
 
 
 def ffn_kernel(
@@ -1035,7 +1135,7 @@
 
 def finish_kernel(more, late_ref, done_ref, ffn_ref, *refs):
     if more:
-        moved_ref, enc_ref, self_mine, self_other, kv_mine, kv_other, *refs = refs
+        moved_ref, enc_ref, *late, refs = (*refs[:6], refs[6:])
     all_ffn, all_done, all_late, *refs = refs
     if more:
         token_ref, enc_grad_ref, *refs = refs
@@ -1071,20 +1171,17 @@
         local[kind].start()
     if more:
         width = token_ref.shape[1]
-        core = me % 2
 
         def fetch(step):
             source = (me + step) % count
             out = []
             for k in range(5):
-                at = (k if k < 3 else k - 3) * width + source * 128
-                columns = pl.ds(pl.multiple_of(at, 128), 128)
-                pair = (self_mine, self_other) if k < 3 else (kv_mine, kv_other)
-                for index, array in enumerate(pair):
-                    side = core if index == 0 else 1 - core
+                columns = pl.ds(pl.multiple_of(k * width + source * 128, 128), 128)
+                for index, array in enumerate(late):
+                    side = me % 2 if index < 2 else 1 - me % 2
                     out.append(
                         pltpu.make_async_copy(
-                            array.at[:, :, columns], weights.at[step % 2, k, :, side],
+                            array.at[:, :, columns], weights.at[step % 2, k, :, side, index % 2],
                             weight_sem.at[step % 2, k, index],
                         )
                     )
@@ -1168,9 +1265,9 @@
         places += [vmem, vmem]
         scratch += [
             pltpu.VMEM(moved.shape, BF),
-            pltpu.VMEM((2, 5, groups, 2, weights.shape[1], 128), BF),
+            pltpu.VMEM((2, 5, groups, 2, 2, weights.shape[1], 128), BF),
             pltpu.VMEM(enc.shape, BF),
-            dma((count,)), dma((count,)), dma, dma, dma((2, 5, 2)),
+            dma((count,)), dma((count,)), dma, dma, dma((2, 5, 4)),
         ]
     return pl.pallas_call(
         functools.partial(finish_kernel, bool(more)),
@@ -1308,24 +1405,6 @@
     return (kept + got).astype(BF)
 
 
-def gather_joined(pieces):
-    count = lax.axis_size("ctx")
-    me = lax.axis_index("ctx")
-    rows = pieces[0].shape[0] // count
-    cut = [lax.dynamic_slice_in_dim(p, me * rows, rows, 0) for p in pieces]
-    joined = jnp.concatenate(cut, axis=1)
-    return lax.all_gather(joined, ("fsdp", "ctx"), axis=0, tiled=True)
-
-
-def gather_all(pieces):
-    full = gather_joined(pieces)
-    out, at = [], 0
-    for p in pieces:
-        out.append(full[:, at : at + p.shape[1]])
-        at += p.shape[1]
-    return out
-
-
 def gather_ffn(ffn_in, ffn_out):
     count = lax.axis_size("ctx")
     groups = lax.axis_size("fsdp")
@@ -1368,8 +1447,15 @@
     head_in = lax.dynamic_index_in_dim(
         self_in.reshape(self_in.shape[0], 3, ctx, own), me, 2, keepdims=False
     ).reshape(-1, 3 * own)
-    all_normed, queries, keys, values, small, head_in = project(
-        own, scale, tokens, small, head_in
+    half_rows = self_in.shape[0] // 2
+    core = me % 2
+
+    def half_of(*weights):
+        cut = [lax.dynamic_slice_in_dim(w, core * half_rows, half_rows, 0) for w in weights]
+        return jnp.concatenate(cut, axis=1)
+
+    all_normed, queries, keys, values, small, head_in, near_rows = project(
+        own, scale, tokens, small, head_in, half_of(self_out, cross_q)
     )
     all_normed = all_normed.reshape(-1, width)
     queries, keys, values = [x.reshape(-1, 128) for x in (queries, keys, values)]
@@ -1378,8 +1464,6 @@
     gain, shift, full_out_bias = vectors[:3], vectors[3:12], vectors[12]
     full_ffn_bias = small[:, 13:].reshape(-1)
 
-    full_self_out, full_cross_q, full_cross_out = gather_all([self_out, cross_q, cross_out])
-    ffn_weights = gather_ffn(ffn_in, ffn_out)
     def lanes(value):
         gap = [(0, 0)] * (value.ndim - 1) + [(0, 128 - own)]
         return value if own == 128 else jnp.pad(value, gap)
@@ -1387,9 +1471,20 @@
     head_kv = lax.dynamic_index_in_dim(
         cross_kv.reshape(-1, 2, ctx, own), me, 2, keepdims=False
     ).reshape(-1, 2 * own)
-    mixed_heads, att_self, lse_self, all_encoder, head_kv = attend_forward(
-        False, heads, prompt_offsets, queries, keys, values, (encoder_out, head_kv)
+    (queries, ffn_in, ffn_out) = lax.optimization_barrier((queries, ffn_in, ffn_out))
+    ffn_weights = gather_ffn(ffn_in, ffn_out)
+    mixed_heads, att_self, lse_self, near_other, all_encoder, head_kv = attend_forward(
+        False, heads, prompt_offsets, queries, keys, values, (near_rows, encoder_out, head_kv),
     )
+
+    def both_cores(mine, other):
+        shape = (mine.shape[0], 2) + mine.shape[1:]
+        full = lax.dynamic_update_index_in_dim(jnp.zeros(shape, BF), mine, core, 1)
+        full = lax.dynamic_update_index_in_dim(full, other, 1 - core, 1)
+        return full.reshape(width, -1)
+
+    near_weights = both_cores(near_rows, near_other)
+    full_self_out, full_cross_q = near_weights[:, :width], near_weights[:, width:]
     all_encoder = all_encoder.reshape(-1, width)
     head_kv = head_kv.reshape(width, 2 * own)
 
@@ -1409,9 +1504,11 @@
     enc_projected = nn(all_encoder, head_kv)
     enc_keys = lanes(enc_projected[:, :own].astype(BF))
     enc_values = lanes((enc_projected[:, own:] + enc_shift).astype(BF))
-    cross_heads, att_cross, lse_cross, all_cross_q = attend_forward(
-        True, heads, prompt_offsets, to_heads(cross_queries), enc_keys, enc_values
+    cross_heads, att_cross, lse_cross, all_cross_q, far_rows, far_other = attend_forward(
+        True, heads, prompt_offsets, to_heads(cross_queries), enc_keys, enc_values,
+        (half_of(cross_out),),
     )
+    full_cross_out = both_cores(far_rows, far_other)
     cross_mixed = to_rows(cross_heads)
     second = first + nn(cross_mixed, full_cross_out) + shift[8]
     unit_three, scale_three = normalize(second)
@@ -1420,13 +1517,11 @@
     blocks = ffn_in.shape[1] // width
     order = full_ffn_bias.reshape(groups, blocks, depth)
     order = jnp.moveaxis(order, 0, 1).reshape(-1, 1, 512)
-    half_rows = depth // 2
-    core = me % 2
-    self_rows = lax.dynamic_slice_in_dim(self_in, core * half_rows, half_rows, 0)
-    kv_rows = lax.dynamic_slice_in_dim(cross_kv, core * half_rows, half_rows, 0)
-    layer_sum, grad_three, bias_parts, in_sum, out_sum, kv_mine = ffn(
+    late_rows = half_of(self_in, cross_kv)
+    quarter = half_rows // 2
+    layer_sum, grad_three, bias_parts, in_sum, out_sum, late_first = ffn(
         normed_three, cotangent, second + full_out_bias,
-        jnp.broadcast_to(order, (order.shape[0], 8, 512)), ffn_weights, kv_rows,
+        jnp.broadcast_to(order, (order.shape[0], 8, 512)), ffn_weights, late_rows[:quarter],
     )
     layer_out = layer_sum.astype(BF)
     chips = ctx // 2
@@ -1442,11 +1537,11 @@
     cross_part = chip_first(pair_product(cross_mixed, branch_two))
     grad_cross_mixed = nt(branch_two, full_cross_out).astype(BF)
     got_shape = (max(chips // 2 - 1, 1),) + in_sum.shape[:2] + in_sum.shape[3:]
-    cross_moved, cross_dk, cross_dv, in_got, out_got, cross_got, self_mine = attend_backward(
+    cross_moved, cross_dk, cross_dv, in_got, out_got, cross_got, late_second = attend_backward(
         True, heads, scale, prompt_offsets, all_cross_q.reshape(-1, 128), enc_keys, enc_values,
         to_heads(grad_cross_mixed), att_cross, lse_cross,
-        (in_sum, out_sum, cross_part, self_rows),
-        (got_shape, got_shape, (chips - 1,) + cross_part.shape[1:], (groups,) + self_rows.shape),
+        (in_sum, out_sum, cross_part, late_rows[quarter:]),
+        (got_shape, got_shape, (chips - 1,) + cross_part.shape[1:], late_first.shape),
     )
 
     def joined(value, mine, dim, got):
@@ -1476,7 +1571,7 @@
         axis=0,
     )
     ffn_sums = jnp.moveaxis(ffn_sums.astype(BF), 1, 0)
-    carried = (middle, ffn_sums, cross_part, kv_part, self_mine, kv_mine)
+    carried = (middle, ffn_sums, cross_part, kv_part, late_first, late_second)
     moved, _, grad_head_in, column, *got = attend_backward(
         False, heads, scale, prompt_offsets, queries, keys, values, to_heads(grad_mixed),
         att_self, lse_self, carried,
@@ -1492,7 +1587,7 @@
         joined(value, zone, 0, part_got).astype(BF)
         for value, part_got in zip(carried[1:4], got[1:4])
     ]
-    self_other, kv_other = got[4:]
+    other_first, other_second = got[4:]
     weight = head_in.reshape(width, 3 * own).astype(F32)
     grad_shift_one = jnp.sum(weight * column, axis=1)
     grad_gain_one = jnp.sum(weight * (grad_head_in - shift[0][:, None] * column), axis=1) / gain[0]
@@ -1530,7 +1625,7 @@
     enc_sum = enc_heads.reshape(ctx, -1, 2 * own)
     more = ()
     if own == 128:
-        more = (moved, enc_sum, self_mine, self_other, kv_mine, kv_other)
+        more = (moved, enc_sum, late_first, late_second, other_first, other_second)
     all_ffn, all_done, all_late, *more_sums = finish(late, done, ffn_sums, width, more)
     if more:
         more = (more_sums[0], tokens, gain[:1], grad_first, more_sums[1])
@@ -1545,18 +1640,17 @@
         input_grad, grad_encoder = more_grads
     else:
 
-        def whole(kept, other):
-            pair = jnp.where(core == 0, jnp.stack([kept, other]), jnp.stack([other, kept]))
-            return jnp.moveaxis(pair, 0, 1).reshape(width, -1)
-
+        late_mine = jnp.concatenate([late_first, late_second], axis=1)
+        late_other = jnp.concatenate([other_first, other_second], axis=1)
+        late_weights = both_cores(late_mine, late_other)
         cut = moved.reshape(ctx, row_count, 3, 128)[:, :, :, :own]
         grads = jnp.transpose(cut, (1, 2, 0, 3)).reshape(row_count, 3 * width)
         unit_one, scale_one = normalize(token_values)
-        grad_normed = nt(grads, whole(self_mine, self_other))
+        grad_normed = nt(grads, late_weights[:, : 3 * width])
         input_grad = grad_first + normalize_back(unit_one, scale_one, gain[0], grad_normed)[0]
         enc_sum = lax.all_to_all(enc_sum, "ctx", split_axis=0, concat_axis=0, tiled=True)
         enc_sum = jnp.transpose(enc_sum.reshape(ctx, -1, 2, own), (1, 2, 0, 3))
-        grad_encoder = nt(enc_sum.reshape(-1, 2 * width), whole(kv_mine, kv_other))
+        grad_encoder = nt(enc_sum.reshape(-1, 2 * width), late_weights[:, 3 * width :])
     return (
         layer_out, input_grad, grad_encoder, mine[:3], mine[3:12], grad_self_in, grad_self_out,
         grad_cross_q, grad_cross_kv, grad_cross_out, grad_ffn_in, grad_ffn_bias, grad_ffn_out, mine[12],

time: 639 us -> 626 us (0.980)
  waiting for transfers between devices: 40.6 us -> 10.5 us
  Pallas kernels: 448 us -> 460 us
  local copies, waits for them, and re-layouts: 45 us -> 54.8 us
  matrix products: 38.9 us -> 31.4 us
    all_gather x1, waiting for transfers between devices: 40.5 us -> 10.5 us  [gather_ffn(): return lax.all_gather(joined, ('fsdp', 'ctx'), axis=0, tiled=True)]
    pallas_call x2, Pallas kernels: 96.5 us -> 109 us  [attend_forward(): pl.pallas_call(functools.partial(attend_forward_kernel, cross, heads, off...]
    pallas_call x1, Pallas kernels: 53.5 us -> 62.7 us  [project(): pl.pallas_call(functools.partial(project_kernel, own, scale), out_shape=(...]
    pallas_call x2, Pallas kernels: 161 us -> 152 us  [attend_backward(): pl.pallas_call(functools.partial(attend_backward_kernel, cross, heads, of...]
    unnamed x109 -> x141, local copies, waits for them, and re-layouts: 8.74 us -> 15.4 us
  transfers between devices with their start and end apart: 5 -> 4, of which waited for: 1 -> 1; matrix products, arithmetic and copies ran while one was open for 11% -> 8% of each run, Pallas kernels for 24% -> 18%
where the time goes in v4:
time: 626 us; the launch traced here: 615 us
  Pallas kernels  460 us (73%)
  local copies, waits for them, and re-layouts  54.8 us (9%)
  other arithmetic  39.3 us (6%)
  matrix products  31.4 us (5%)
  between operations  16.4 us (3%)
  waiting for transfers between devices  10.5 us (2%)
    pallas_call x2, Pallas kernels, attend_backward(): pl.pallas_call(functools.partial(attend_backward_kernel, cross, heads, of...  152 us
    pallas_call x2, Pallas kernels, attend_forward(): pl.pallas_call(functools.partial(attend_forward_kernel, cross, heads, off...  109 us
    pallas_call x1, Pallas kernels, ffn(): pl.pallas_call(functools.partial(ffn_kernel, steps, groups), grid=(steps...  63.7 us
    pallas_call x1, Pallas kernels, project(): pl.pallas_call(functools.partial(project_kernel, own, scale), out_shape=(...  62.7 us
    pallas_call x1, Pallas kernels, finish(): pl.pallas_call(functools.partial(finish_kernel, bool(more)), out_shape=ou...  60.4 us
    unnamed x141, local copies, waits for them, and re-layouts  15.4 us
    dot_general x7, matrix products, tn(): lax.dot_general(left, right, (((0,), (0,)), ((), ())), preferred_element_...  14.3 us
    pallas_call x1, Pallas kernels, place(): pl.pallas_call(kernel, grid=(chips,), out_shape=out_shape, in_specs=in_sp...  12.6 us
  transfers between devices with their start and end apart: 4, of which 1 were waited for; matrix products, arithmetic and copies ran while one was open for 8% of the time, Pallas kernels for 18%

profile of v4, /device:TPU:0, one launch (start us, length us, event | category | flops | bytes accessed | tf_op | source)
XLA Modules:
  0.0 614.7 jit_solution(15852920531005068330)
XLA Ops:
  7.3 2.7 copy.123
  10.0 1.0 constant_dynamic-slice_fusion.9
  11.9 1.7 constant_dynamic-slice_fusion.6
  15.1 62.7 %shard_map.254 = (bf16[8,512,1024]{2,1,0:T(8,128)(2,1)}, bf16[8,512,128]{2,1,0:T(8,128)(2,1)}, bf16[8,512,128]{2,1,0:T(8,128)(2,1)}, bf16[8,512,128]{2,1,0:T(8,1...) custom-call(bf16[512,1024]{1,0:T(8,128)(2,1)} %refs_9_.1, ...), custom_call_target="tpu_custom_call" | custom-call | flops 49999998976 | bytes 33554432 | tf_op jit(solution)/shard_map/pallas_call | solution.py:874
  77.8 1.0 constant_dynamic-slice_fusion.5
  79.8 1.1 reshape.334
  84.6 53.4 %shard_map.255 = (bf16[8,512,128]{2,1,0:T(8,128)(2,1)}, f32[128,4096]{1,0:T(8,128)}, f32[8,4096]{1,0:T(8,128)}, bf16[4,128,2048]{2,1,0:T(8,128)(2,1)}, bf16[8,25...) custom-call(s32[1,1]{1,0:T(1,128)S(6)} %copy.202.offs_ref, bf16[4096,128]{1,0:T(8,128)(2,1)} %bitcast.266, ...), custom_call_target="tpu_custom_call" | custom-call | flops 40000000000 | bytes 8388608 | tf_op jit(solution)/shard_map/pallas_call | solution.py:435
  138.0 3.6 fusion.71
  142.5 2.3 copy.126
  146.6 1.1 copy-done.15
  147.9 1.3 copy-done.16
  149.5 1.0 copy-done.20
  150.5 1.1 copy-done.23
  151.6 1.4 fusion.69
  154.3 1.0 copy-done.25
  155.3 1.3 multiply_convert_fusion
  157.1 1.3 copy.130
  158.5 2.1 fusion.19.v_ref
  160.6 55.3 %shard_map.256 = (bf16[8,512,128]{2,1,0:T(8,128)(2,1)}, f32[128,4096]{1,0:T(8,128)}, f32[8,4096]{1,0:T(8,128)}, bf16[8,512,128]{2,1,0:T(8,128)(2,1)}, bf16[4,128...) custom-call(s32[1,1]{1,0:T(1,128)S(6)} %copy.202.offs_ref, bf16[8,512,128]{2,1,0:T(8,128)(2,1)} %bitcast.216, ...), custom_call_target="tpu_custom_call" | custom-call | flops 40000000000 | bytes 8388608 | tf_op jit(solution)/shard_map/pallas_call | solution.py:435
  215.9 2.4 copy.131
  220.5 1.4 fusion.70
  222.3 1.0 copy-done.10
  223.4 2.2 broadcast_add_fusion
  225.5 1.1 pad_maximum_fusion.3
  226.7 10.5 %all-gather.2.cloned.1.call-done.win_ref.wout_ref = bf16[1024,8192]{1,0:T(8,128)(2,1)} async-done(((bf16[32,8192]{1,0:T(8,128)(2,1)}), bf16[1024,8192]{1,0:T(8,128)(2,1)}) %all-gather.2.cloned.1.call-update) | async-done | bytes 16777232 | tf_op jit(solution)/shard_map/all_gather | solution.py:1424
  237.8 63.7 %shard_map.257 = (f32[512,1024]{1,0:T(8,128)}, f32[512,1024]{1,0:T(8,128)}, f32[8,8,512]{2,1,0:T(8,128)}, bf16[8,512,256]{2,1,0:T(8,128)(2,1)}, bf16[4,2,512,256...) custom-call(bf16[512,1024]{1,0:T(8,128)(2,1)} %get-tuple-element.145.n_ref, bf16[512,1024]{1,0:T(8,128)(2,1)} %dy_ref.1, ...), custom_call_target="tpu_custom_call" | custom-call | flops 30000001024 | bytes 67108864 | tf_op jit(solution)/shard_map/pallas_call | solution.py:1084
  301.6 2.6 multiply_reduce_fusion
  304.2 2.2 fusion.63
  306.4 1.0 copy-done.33
  307.4 1.7 convolution_convert_fusion.3
  309.1 3.5 convolution_convert_fusion
  312.5 1.5 copy.137
  314.0 1.3 copy.138
  317.7 0.9 fusion.56
  319.3 2.7 convert_element_type.199
  322.0 1.9 add_convert_fusion.2
  324.0 1.1 copy.193
  325.0 65.2 %shard_map.258 = (bf16[8,512,128]{2,1,0:T(8,128)(2,1)}, bf16[2048,128]{1,0:T(8,128)(2,1)}, bf16[2048,128]{1,0:T(8,128)(2,1)}, bf16[1,8,4,64,256]{4,3,2,1,0:T(8,1...) custom-call(s32[1,1]{1,0:T(1,128)S(6)} %copy.202.offs_ref, ...), custom_call_target="tpu_custom_call" | custom-call | flops 60000002048 | bytes 8388608 | tf_op jit(solution)/shard_map/pallas_call | solution.py:731
  390.3 2.6 copy.140
  392.9 2.9 convolution_convert_fusion.2
  395.8 3.8 multiply_reduce_fusion.1
  399.7 2.1 fusion.64
  401.8 1.7 convolution_convert_fusion.1
  403.5 2.3 fusion.12
  407.0 2.1 convolution_convert_fusion.4
  409.2 1.7 collective-permute-start.1
  411.0 1.5 copy.143
  412.5 1.3 copy.144
  413.8 1.0 fusion.27.refs_2_
  416.1 2.1 fusion.2
  418.5 1.6 fusion.1
  420.1 1.5 fusion.refs_1_
  422.4 2.1 add_convert_fusion.1
  424.6 1.9 add_convert_fusion
  426.6 1.5 pad_maximum_fusion.refs_0_
  428.2 87.0 %shard_map.259 = (bf16[8,512,384]{2,1,0:T(8,128)(2,1)}, bf16[8,512,384]{2,1,0:T(8,128)(2,1)}, f32[1024,384]{1,0:T(8,128)}, f32[8,384]{1,0:T(8,128)}, bf16[3,2,4,...) custom-call(s32[1,1]{1,0:T(1,128)S(6)} %copy.202.offs_ref, ...), custom_call_target="tpu_custom_call" | custom-call | flops 60000002048 | bytes 8388608 | tf_op jit(solution)/shard_map/pallas_call | solution.py:731
  515.2 1.8 convert_reduce_fusion
  517.1 1.0 fusion.20.ffn_ref
  518.2 1.1 convert_reduce_fusion.4
  520.0 1.8 convert_reduce_fusion.1
  526.2 1.4 fusion.67
  529.8 1.2 pad_maximum_fusion.2.late_ref
  531.0 60.4 %shard_map.260 = (bf16[8,16,64,256]{3,2,1,0:T(8,128)(2,1)}, bf16[8,768,128]{2,1,0:T(8,128)(2,1)}, bf16[8,1328,128]{2,1,0:T(8,128)(2,1)}, f32[512,1024]{1,0:T(8,128)}, f32[256,1024]{1,0:T(8,128)}) custom-call(bf16[4,1328,128]{2,1,0:T(8,128)(2,1)} %pad_maximum_fusion.2.late_ref, bf16[768,128]{1,0:T(8,128)(2,1)} %pad_maximum_fusion.6.done_ref, ...), custom_call_target="tpu_custom_call" | custom-call | flops 49999998976 | bytes 33554432 | tf_op jit(solution)/shard_map/pallas_call | solution.py:1272
  594.8 12.6 %shard_map.261 = (f32[256,4096]{1,0:T(8,128)}, f32[4,4,64,1024]{3,2,1,0:T(8,128)}, f32[256,3072]{1,0:T(8,128)}, f32[256,2048]{1,0:T(8,128)}, f32[256,1024]{1,0:T...) custom-call(bf16[8,16,64,256]{3,2,1,0:T(8,128)(2,1)} %get-tuple-element.116.refs, ...), custom_call_target="tpu_custom_call" | custom-call | bytes 33554432 | tf_op jit(solution)/shard_map/pallas_call | solution.py:1383
  (235 shorter events, 32.4 us)
Async XLA Ops:
  7.2 73.7 %copy-start = (bf16[1024,1024]{1,0:T(8,128)(2,1)S(1)}, bf16[1024,1024]{1,0:T(8,128)(2,1)}, u32[]{:S(2)}) copy-start(bf16[1024,1024]{1,0:T(8,128)(2,1)} %param.27) | copy-start | bytes 6291460
  7.2 4.6 copy-start.63
  7.2 4.6 copy-start.65
  7.2 4.6 copy-start.44
  7.2 229.9 %all-gather.2.cloned.1.call-start = ((), (), s32[]{:S(2)}) async-start(), calls=%async_computation | async-start | bytes 17301504 | tf_op jit(solution)/shard_map/all_gather | solution.py:1424
  7.3 4.6 copy-start.45
  10.0 4.4 copy-start.62
  10.0 4.4 copy-start.64
  79.0 3.2 copy-start.12
  141.6 3.2 copy-start.19
  141.6 3.2 copy-start.48
  146.0 7.3 %copy-start.46 = (f32[1,4,256]{2,0,1:T(1,128)}, f32[1,4,256]{2,0,1:T(1,128)S(1)}, u32[]{:S(2)}) copy-start(f32[1,4,256]{2,0,1:T(1,128)S(1)} %get-tuple-element.163) | copy-start | bytes 12292
  146.0 1.6 copy-start.15
  147.6 1.6 copy-start.16
  149.2 1.3 copy-start.20
  149.2 2.4 copy-start.23
  149.5 4.8 copy-start.7
  153.0 1.3 copy-start.2
  153.0 1.3 copy-start.50
  215.9 2.7 copy-start.22
  218.3 1.2 copy-start.21
  218.6 1.7 copy-start.3
  218.6 2.0 copy-start.28
  219.6 2.3 copy-start.13
  221.9 1.4 copy-start.10
  301.5 2.7 copy-start.5
  301.5 2.7 copy-start.32
  304.2 3.2 copy-start.29
  306.4 2.7 copy-start.14
  309.1 13.0 %collective-permute-start = (bf16[1024,512]{1,0:T(8,128)(2,1)}, bf16[1024,512]{1,0:T(8,128)(2,1)}, u32[]{:S(2)}, u32[]{:S(2)}) collective-permute-start(bf16[1024,512]{1,0:T(8,128)(2,1)} %convolution_convert_fusion.3), channel_id=1, source_target_pairs={{0,4},{4,0},{8,12},{12,8},{16,20},{20,16},{24,28},{28,24},{1,5},{5... | collective-permute-start | bytes 3145736 | tf_op jit(solution)/shard_map/ppermute | solution.py:1396
  315.4 6.7 %copy-start.34 = (bf16[512,1024]{1,0:T(8,128)(2,1)S(1)}, bf16[512,1024]{1,0:T(8,128)(2,1)}, u32[]{:S(2)}) copy-start(bf16[512,1024]{1,0:T(8,128)(2,1)} %copy-done.33) | copy-start | bytes 3145732
  390.3 2.6 copy-start.26
  390.3 5.5 copy-start.4
  390.3 5.5 copy-start.47
  390.3 5.5 copy-start.51
  390.3 5.5 copy-start.53
  392.9 2.9 copy-start.30
  395.8 3.8 copy-start.6
  399.7 2.1 copy-start.24
  399.7 3.8 copy-start.8
  401.8 4.0 copy-start.35
  403.5 2.3 copy-start.9
  403.5 3.0 copy-start.39
  403.5 3.5 copy-start.66
  407.0 2.1 copy-start.41
  407.0 2.1 copy-start.37
  409.2 13.0 %collective-permute-start.1 = (bf16[1024,512]{1,0:T(8,128)(2,1)}, bf16[1024,512]{1,0:T(8,128)(2,1)}, u32[]{:S(2)}, u32[]{:S(2)}) collective-permute-start(bf16[1024,512]{1,0:T(8,128)(2,1)} %convolution_convert_fusion.2), channel_id=1, source_target_pairs={{0,4},{4,0},{8,12},{12,8},{16,20},{20,16},{24,28},{28,24},{1,5},{5... | collective-permute-start | bytes 3145736 | tf_op jit(solution)/shard_map/ppermute | solution.py:1396
  410.9 13.7 %collective-permute-start.2 = (bf16[1024,512]{1,0:T(8,128)(2,1)}, bf16[1024,512]{1,0:T(8,128)(2,1)}, u32[]{:S(2)}, u32[]{:S(2)}) collective-permute-start(bf16[1024,512]{1,0:T(8,128)(2,1)} %convolution_convert_fusion.1), channel_id=1, source_target_pairs={{0,4},{4,0},{8,12},{12,8},{16,20},{20,16},{24,28},{28,24},{1,5},{5... | collective-permute-start | bytes 3145736 | tf_op jit(solution)/shard_map/ppermute | solution.py:1396
  413.8 2.3 copy-start.61
  414.8 1.2 copy-start.40
  416.1 2.4 copy-start.38
  420.1 2.1 copy-start.27
  420.1 2.3 copy-start.31
  422.2 2.4 copy-start.36
  522.1 1.4 copy-start.11
  522.1 1.7 copy-start.18
  522.1 1.7 copy-start.54
  524.4 4.5 copy-start.55
  524.4 4.5 copy-start.56
  524.4 4.5 copy-start.57
  524.4 4.5 copy-start.58
  524.4 4.5 copy-start.60
  524.5 4.7 copy-start.49
  594.8 12.6 %copy-start.1 = (bf16[1024,1024]{1,0:T(8,128)(2,1)S(1)}, bf16[1024,1024]{1,0:T(8,128)(2,1)}, u32[]{:S(2)}) copy-start(bf16[1024,1024]{1,0:T(8,128)(2,1)} %param.27) | copy-start | bytes 6291460
  (7 other events, 6.1 us)
Sparse Core Ops, SparseCore 0:
  82.2 154.8 all-gather.1

commit v5 on v4

--- a/solution.py
+++ b/solution.py
@@ -378,6 +378,68 @@
         for copy in local:
             copy.wait()
         enc_done()
+
+
+def chain_spread(source, target, send, recv):
+    zone, groups = lax.axis_index("fsdp"), lax.axis_size("fsdp")
+
+    def copy(way, stage):
+        step = 1 - 2 * way
+        block = jnp.clip(zone - step * stage, 0, groups - 1)
+        at = way * groups + stage
+        return remote(
+            source if stage == 0 else target.at[block], target.at[block],
+            send.at[at], recv.at[at], {"fsdp": jnp.clip(zone + step, 0, groups - 1)},
+        )
+
+    def arrival(way, stage):
+        step = 1 - 2 * way
+        block = jnp.clip(zone - step * (stage + 1), 0, groups - 1)
+        at = way * groups + stage
+        return remote(
+            target.at[block], target.at[block], send.at[at], recv.at[at],
+            {"fsdp": jnp.clip(zone + step, 0, groups - 1)},
+        )
+
+    def sends(way, stage):
+        return (zone + 1 < groups) & (zone >= stage) if way == 0 else (
+            (zone > 0) & (zone + stage < groups)
+        )
+
+    def comes(way, stage):
+        return zone >= stage + 1 if way == 0 else zone + stage + 1 < groups
+
+    def send_all(stage):
+        for way in range(2):
+
+            @pl.when(sends(way, stage))
+            def _():
+                copy(way, stage).start()
+
+    def wait_all(stage):
+        for way in range(2):
+
+            @pl.when(comes(way, stage))
+            def _():
+                arrival(way, stage).wait_recv()
+
+    def start():
+        send_all(0)
+
+    def advance(stage):
+        wait_all(stage - 1)
+        send_all(stage)
+
+    def finish():
+        wait_all(groups - 2)
+        for stage in range(groups - 1):
+            for way in range(2):
+
+                @pl.when(sends(way, stage))
+                def _():
+                    copy(way, stage).wait_send()
+
+    return start, advance, finish
 
 
 def core_swap(source, target, sems):
@@ -465,8 +527,7 @@
                     {"ctx": flipped_bits(me, (4 if part == 0 else 2) * other)},
                 )
             )
-    out = out + chip_copies(sources[2], targets[2], send_sem, recv_sem, len(out))
-    return out + group_spread(sources[3], targets[3], send_sem, recv_sem, len(out))
+    return out + chip_copies(sources[2], targets[2], send_sem, recv_sem, len(out))
 
 
 def chip_copies(source, target, send_sem, recv_sem, sem):
@@ -519,7 +580,10 @@
         send_sem, recv_sem, own_sem, do_send, do_recv, do_own, carry_send, carry_recv, *refs,
     ) = refs
     if cross:
-        (keep_sem,) = refs
+        keep_sem, chain_send, chain_recv = refs
+        chain_start, chain_advance, chain_finish = chain_spread(
+            sources[3], targets[3], chain_send, chain_recv
+        )
         keep_own = pltpu.make_async_copy(
             sources[3], targets[3].at[lax.axis_index("fsdp")], keep_sem
         )
@@ -543,6 +607,7 @@
     for copy in carry_copies:
         copy.start()
     if cross:
+        chain_start()
         keep_own.start()
     else:
         for copy in pair_copies:
@@ -600,6 +665,12 @@
         i = (me + step) % count
         ready(i)
 
+        for hop in range(1, min(3, lax.axis_size("fsdp") - 1)):
+
+            @pl.when(step == 2 * hop + 1)
+            def _():
+                chain_advance(hop)
+
         both = (even, odd)
         score(i, 0, even)
         for j in range(key_tiles):
@@ -699,6 +770,9 @@
     put_done()
     if cross:
         keep_own.wait()
+        for hop in range(3, lax.axis_size("fsdp") - 1):
+            chain_advance(hop)
+        chain_finish()
     else:
         for copy in pair_copies:
             copy.wait()
@@ -719,7 +793,7 @@
     moved = jax.ShapeDtypeStruct((count, TILE, wide), BF)
     if cross:
         local = [jax.ShapeDtypeStruct((keys, 128), BF)] * 2
-        carries = 2 * (count // 4 - 1) + count // 2 - 1 + lax.axis_size("fsdp") - 1
+        carries = 2 * (count // 4 - 1) + count // 2 - 1
     else:
         local = [
             jax.ShapeDtypeStruct((count, TILE, wide), BF),
@@ -752,7 +826,7 @@
             dma((count,)), dma((count,)), dma,
             dma((carries,)), dma((carries,)),
         ]
-        + ([dma] if cross else [pltpu.VMEM(normed[0].shape[1:], BF), dma, dma((2,)), dma((2,))]),
+        + ([dma] + [dma((2 * lax.axis_size("fsdp"),))] * 2 if cross else [pltpu.VMEM(normed[0].shape[1:], BF), dma, dma((2,)), dma((2,))]),
         compiler_params=pltpu.CompilerParams(
             vmem_limit_bytes=VMEM_BYTES, collective_id=3 if cross else 4,
             has_side_effects=True,
@@ -771,7 +845,9 @@
     me, zone = lax.axis_index("ctx"), lax.axis_index("fsdp")
     count, groups = lax.axis_size("ctx"), lax.axis_size("fsdp")
     chips = count // 2
-    spread = group_spread(rows_ref, rows_all, rows_send, rows_recv, 0)
+    chain_start, chain_advance, chain_finish = chain_spread(
+        rows_ref, rows_all, rows_send, rows_recv
+    )
     keep_rows = pltpu.make_async_copy(rows_ref, rows_all.at[zone], own_sem.at[3])
     shard = small_ref.shape[1]
     sibling = {"ctx": flipped_bits(me, 1)}
@@ -798,8 +874,8 @@
 
     start, land, rest, done = plane_gather(tokens_ref, all_tokens, token_send, token_recv)
     start()
-    for copy in spread + [keep_rows]:
-        copy.start()
+    chain_start()
+    keep_rows.start()
     for copy in local:
         copy.wait()
     for copy in parts:
@@ -823,6 +899,8 @@
     order, ready = [], []
     for step in range(count):
         place = step % 2
+        if step in (2, 4) and step // 2 <= groups - 2:
+            chain_advance(step // 2)
         if step == 0:
             ready.append(me)
         elif step == 1:
@@ -858,9 +936,9 @@
     for copy in parts:
         copy.wait_send()
     keep_rows.wait()
-    for copy in spread:
-        copy.wait_send()
-        copy.wait_recv()
+    for stage in range(3, groups - 1):
+        chain_advance(stage)
+    chain_finish()
     done()
 
 
@@ -887,7 +965,7 @@
             pltpu.VMEM((2, rows, width), BF),
             dma((count + 1,)), dma((count + 1,)),
             dma((2, groups - 1)), dma((2, groups - 1)),
-            dma((4,)), dma((2,)), dma((groups - 1,)), dma((groups - 1,)),
+            dma((4,)), dma((2,)), dma((2 * groups,)), dma((2 * groups,)),
         ],
         compiler_params=pltpu.CompilerParams(
             vmem_limit_bytes=VMEM_BYTES, collective_id=5, has_side_effects=True
@@ -1133,6 +1211,79 @@
     )(normed, dy, base, bias, weights, weights, rows_part)
 
 
+def branch_kernel(query, *refs):
+    if query:
+        moved_ref, query_ref, normed_ref, *refs = refs
+    else:
+        grad_ref, *refs = refs
+    (
+        values_ref, gain_ref, base_ref, mixed_ref, weight_ref,
+        total_ref, do_ref, sums_ref, send_ref, keep_ref,
+    ) = refs
+    core = lax.axis_index("ctx") % 2
+
+    def rows_of(ref):
+        pieces = [ref[index] for index in range(ref.shape[0])]
+        return pieces[0] if len(pieces) == 1 else jnp.concatenate(pieces, axis=1)
+
+    def column_sum(row, value):
+        sums_ref[row : row + 1, :] = jnp.sum(value, axis=0, keepdims=True)
+
+    sums_ref[...] = jnp.zeros_like(sums_ref)
+    products = []
+    if query:
+        cq = rows_of(moved_ref)
+        grad = nt(cq, query_ref[...])
+        column_sum(3, cq.astype(F32))
+        products.append((normed_ref[...], cq))
+    else:
+        grad = grad_ref[...]
+    unit, scale = normalize(values_ref[...])
+    q = gain_ref[...] * grad
+    back = scale * (
+        q - jnp.mean(q, axis=-1, keepdims=True) - unit * jnp.mean(q * unit, axis=-1, keepdims=True)
+    )
+    column_sum(0, grad * unit)
+    column_sum(1, grad)
+    total = base_ref[...].astype(F32) + back
+    total_ref[...] = total
+    branch = total.astype(BF)
+    column_sum(2, branch.astype(F32))
+    do = nt(branch, weight_ref[...]).astype(BF)
+    own = do_ref.shape[2]
+    for index in range(do_ref.shape[0]):
+        do_ref[index] = do[:, index * own : index * own + own]
+    products.append((rows_of(mixed_ref), branch))
+    half = keep_ref.shape[2]
+    for index, (left, right) in enumerate(products):
+        low, high = tn(left, right[:, :half]), tn(left, right[:, half:])
+        keep_ref[index] = jnp.where(core == 0, low, high).astype(BF)
+        send_ref[index] = jnp.where(core == 0, high, low).astype(BF)
+
+
+def branch(grad, values, gain, base, mixed, weight, query=()):
+    rows, width = values.shape
+    number = 2 if query else 1
+    vmem = pl.BlockSpec(memory_space=pltpu.VMEM)
+    half = jax.ShapeDtypeStruct((number, width, width // 2), BF)
+    operands = (grad, *query, values, gain, base, mixed, weight)
+    return pl.pallas_call(
+        functools.partial(branch_kernel, bool(query)),
+        out_shape=(
+            jax.ShapeDtypeStruct((rows, width), F32),
+            jax.ShapeDtypeStruct(mixed.shape, BF),
+            jax.ShapeDtypeStruct((8, width), F32),
+            half, half,
+        ),
+        in_specs=[vmem] * len(operands),
+        out_specs=(vmem,) * 5,
+        compiler_params=pltpu.CompilerParams(vmem_limit_bytes=VMEM_BYTES),
+        cost_estimate=pl.CostEstimate(
+            flops=10**10, bytes_accessed=2**24, transcendentals=0
+        ),
+    )(*operands)
+
+
 def finish_kernel(more, late_ref, done_ref, ffn_ref, *refs):
     if more:
         moved_ref, enc_ref, *late, refs = (*refs[:6], refs[6:])
@@ -1396,13 +1547,8 @@
     return lax.ppermute(value, "ctx", [(i, i ^ bit) for i in range(count)])
 
 
-def pair_product(left, right):
-    core = lax.axis_index("ctx") % 2
-    half = right.shape[1] // 2
-    send = tn(left, lax.dynamic_slice_in_dim(right, (1 - core) * half, half, 1)).astype(BF)
-    got = swap(send, 1).astype(F32)
-    kept = tn(left, lax.dynamic_slice_in_dim(right, core * half, half, 1))
-    return (kept + got).astype(BF)
+def pair_sum(send, keep):
+    return (keep.astype(F32) + swap(send, 1).astype(F32)).astype(BF)
 
 
 def gather_ffn(ffn_in, ffn_out):
@@ -1497,8 +1643,7 @@
     mixed = to_rows(mixed_heads)
     token_values = tokens.astype(F32)
     first = token_values + nn(mixed, full_self_out) + shift[5]
-    unit_two, scale_two = normalize(first)
-    normed_two = (unit_two * gain[1] + shift[1]).astype(BF)
+    normed_two = (normalize(first)[0] * gain[1] + shift[1]).astype(BF)
     cross_queries = (scale * (nn(normed_two, full_cross_q) + shift[6])).astype(BF)
     enc_shift = lax.dynamic_slice_in_dim(shift[7], me * own, own, 0)
     enc_projected = nn(all_encoder, head_kv)
@@ -1511,8 +1656,7 @@
     full_cross_out = both_cores(far_rows, far_other)
     cross_mixed = to_rows(cross_heads)
     second = first + nn(cross_mixed, full_cross_out) + shift[8]
-    unit_three, scale_three = normalize(second)
-    normed_three = (unit_three * gain[2] + shift[2]).astype(BF)
+    normed_three = (normalize(second)[0] * gain[2] + shift[2]).astype(BF)
     depth = ffn_in.shape[0]
     blocks = ffn_in.shape[1] // width
     order = full_ffn_bias.reshape(groups, blocks, depth)
@@ -1530,16 +1674,22 @@
     out_sum = out_sum.reshape(-1, groups, chips // 2, part, 256)
 
     dy = cotangent.astype(F32)
-    back_three = normalize_back(unit_three, scale_three, gain[2], grad_three)
-    grad_second = dy + back_three[0]
-    branch_two = grad_second.astype(BF)
     chip_first = lambda value: jnp.moveaxis(value.reshape(groups, chips, part, -1), 1, 0)
-    cross_part = chip_first(pair_product(cross_mixed, branch_two))
-    grad_cross_mixed = nt(branch_two, full_cross_out).astype(BF)
+
+    def stacked(value):
+        return value if own == 128 else to_rows(value)[None]
+
+    def tiles_of(value):
+        return value if own == 128 else to_heads(value[0])
+
+    grad_second, cross_do, sums_two, send, keep = branch(
+        grad_three, second, gain[2:3], cotangent, stacked(cross_heads), full_cross_out
+    )
+    cross_part = chip_first(pair_sum(send, keep)[0])
     got_shape = (max(chips // 2 - 1, 1),) + in_sum.shape[:2] + in_sum.shape[3:]
     cross_moved, cross_dk, cross_dv, in_got, out_got, cross_got, late_second = attend_backward(
         True, heads, scale, prompt_offsets, all_cross_q.reshape(-1, 128), enc_keys, enc_values,
-        to_heads(grad_cross_mixed), att_cross, lse_cross,
+        tiles_of(cross_do), att_cross, lse_cross,
         (in_sum, out_sum, cross_part, late_rows[quarter:]),
         (got_shape, got_shape, (chips - 1,) + cross_part.shape[1:], late_first.shape),
     )
@@ -1548,18 +1698,12 @@
         kept = lax.dynamic_index_in_dim(value, mine, dim, keepdims=False).astype(F32)
         return kept + jnp.sum(got.astype(F32), axis=0)
 
-    cross_dq = to_rows(cross_moved)
-    back_two = normalize_back(unit_two, scale_two, gain[1], nt(cross_dq, full_cross_q))
-    grad_first = grad_second + back_two[0]
-    branch_one = grad_first.astype(BF)
-    grad_mixed = nt(branch_one, full_self_out).astype(BF)
-    middle = jnp.stack(
-        [
-            chip_first(pair_product(normed_two, cross_dq)),
-            chip_first(pair_product(mixed, branch_one)),
-        ],
-        axis=1,
+    grad_first, self_do, sums_one, send, keep = branch(
+        stacked(cross_moved), first, gain[1:2], grad_second, stacked(mixed_heads), full_self_out,
+        (full_cross_q, normed_two),
     )
+    middle = pair_sum(send, keep)
+    middle = jnp.moveaxis(middle.reshape(2, groups, chips, part, -1), 2, 0)
     cross_part = joined(cross_part, me // 2, 0, cross_got).astype(BF)
     enc_heads = jnp.concatenate([cross_dk[:, :own], cross_dv[:, :own]], axis=1)
     kv_part = tn(all_encoder, enc_heads).astype(BF).reshape(groups, depth, 2 * own)
@@ -1573,7 +1717,7 @@
     ffn_sums = jnp.moveaxis(ffn_sums.astype(BF), 1, 0)
     carried = (middle, ffn_sums, cross_part, kv_part, late_first, late_second)
     moved, _, grad_head_in, column, *got = attend_backward(
-        False, heads, scale, prompt_offsets, queries, keys, values, to_heads(grad_mixed),
+        False, heads, scale, prompt_offsets, queries, keys, values, tiles_of(self_do),
         att_self, lse_self, carried,
         [(value.shape[0] - 1,) + value.shape[1:] for value in carried[:4]]
         + [value.shape for value in carried[4:]],
@@ -1597,13 +1741,13 @@
 
     totals = jnp.stack(
         [
-            grad_gain_one, back_two[1], back_three[1],
-            grad_shift_one, back_two[2], back_three[2],
+            grad_gain_one, sums_one[0], sums_two[0],
+            grad_shift_one, sums_one[1], sums_two[1],
             spread(column[:own]), spread(column[2 * own :]),
-            jnp.sum(branch_one.astype(F32), axis=0),
-            jnp.sum(cross_dq.astype(F32), axis=0),
+            sums_one[2],
+            sums_one[3],
             spread(jnp.sum(enc_heads[:, own:].astype(F32), axis=0)),
-            jnp.sum(branch_two.astype(F32), axis=0),
+            sums_two[2],
             jnp.sum(dy, axis=0),
         ]
     )

time: 626 us -> 606 us (0.968)
  matrix products: 31.4 us -> 12.5 us
  Pallas kernels: 460 us -> 470 us
  other arithmetic: 39.3 us -> 30.8 us
    pallas_call x0 -> x2, Pallas kernels: none -> 20.2 us  [branch(): pl.pallas_call(functools.partial(branch_kernel, bool(query)), out_shape=(...]
    dot_general x7 -> x1, matrix products: 14.3 us -> 3.87 us  [tn(): lax.dot_general(left, right, (((0,), (0,)), ((), ())), preferred_element_...]
    dot_general x3 -> x0, matrix products: 9.55 us -> none  [nt(): lax.dot_general(left, right, (((1,), (1,)), ((), ())), preferred_element_...]
    pallas_call x2, Pallas kernels: 109 us -> 99.7 us  [attend_forward(): pl.pallas_call(functools.partial(attend_forward_kernel, cross, heads, off...]
    reduce_sum x4 -> x1, other arithmetic: 7.62 us -> 0.19 us  [body(): jnp.sum(dy, axis=0)]
    unnamed x141 -> x119, local copies, waits for them, and re-layouts: 15.4 us -> 15.3 us
  transfers between devices with their start and end apart: 4 -> 3, of which waited for: 1 -> 1; matrix products, arithmetic and copies ran while one was open for 8% -> 8% of each run, Pallas kernels for 18% -> 17%
where the time goes in v5:
time: 606 us; the launch traced here: 594 us
  Pallas kernels  470 us (78%)
  local copies, waits for them, and re-layouts  52.9 us (9%)
  other arithmetic  30.8 us (5%)
  between operations  16.2 us (3%)
  matrix products  12.5 us (2%)
  waiting for transfers between devices  9.41 us (2%)
    pallas_call x2, Pallas kernels, attend_backward(): pl.pallas_call(functools.partial(attend_backward_kernel, cross, heads, of...  150 us
    pallas_call x2, Pallas kernels, attend_forward(): pl.pallas_call(functools.partial(attend_forward_kernel, cross, heads, off...  99.7 us
    pallas_call x1, Pallas kernels, ffn(): pl.pallas_call(functools.partial(ffn_kernel, steps, groups), grid=(steps...  65 us
    pallas_call x1, Pallas kernels, project(): pl.pallas_call(functools.partial(project_kernel, own, scale), out_shape=(...  62.6 us
    pallas_call x1, Pallas kernels, finish(): pl.pallas_call(functools.partial(finish_kernel, bool(more)), out_shape=ou...  60.2 us
    pallas_call x2, Pallas kernels, branch(): pl.pallas_call(functools.partial(branch_kernel, bool(query)), out_shape=(...  20.2 us
    unnamed x119, local copies, waits for them, and re-layouts  15.3 us
    pallas_call x1, Pallas kernels, place(): pl.pallas_call(kernel, grid=(chips,), out_shape=out_shape, in_specs=in_sp...  12.6 us
  transfers between devices with their start and end apart: 3, of which 1 were waited for; matrix products, arithmetic and copies ran while one was open for 8% of the time, Pallas kernels for 17%

profile of v5, /device:TPU:0, one launch (start us, length us, event | category | flops | bytes accessed | tf_op | source)
XLA Modules:
  0.0 593.8 jit_solution(16171403122061233638)
XLA Ops:
  7.3 2.7 copy.100
  10.0 1.0 constant_dynamic-slice_fusion.9
  11.0 0.8 copy.101.head_ref
  11.9 1.7 constant_dynamic-slice_fusion.6
  13.6 0.8 pad_maximum_fusion.3.rows_ref
  15.1 62.6 %shard_map.254 = (bf16[8,512,1024]{2,1,0:T(8,128)(2,1)}, bf16[8,512,128]{2,1,0:T(8,128)(2,1)}, bf16[8,512,128]{2,1,0:T(8,128)(2,1)}, bf16[8,512,128]{2,1,0:T(8,1...) custom-call(bf16[512,1024]{1,0:T(8,128)(2,1)} %refs_9_.1, ...), custom_call_target="tpu_custom_call" | custom-call | flops 49999998976 | bytes 33554432 | tf_op jit(solution)/shard_map/pallas_call | solution.py:952
  77.7 1.0 constant_dynamic-slice_fusion.5
  78.8 0.8 copy.112
  79.6 1.1 reshape.294
  81.1 0.8 pad_maximum_fusion.4
  82.2 0.9 dynamic-slice_reduce_fusion
  84.5 47.5 %shard_map.255 = (bf16[8,512,128]{2,1,0:T(8,128)(2,1)}, f32[128,4096]{1,0:T(8,128)}, f32[8,4096]{1,0:T(8,128)}, bf16[4,128,2048]{2,1,0:T(8,128)(2,1)}, bf16[8,25...) custom-call(s32[1,1]{1,0:T(1,128)S(6)} %copy.175.offs_ref, bf16[4096,128]{1,0:T(8,128)(2,1)} %bitcast.216, ...), custom_call_target="tpu_custom_call" | custom-call | flops 40000000000 | bytes 8388608 | tf_op jit(solution)/shard_map/pallas_call | solution.py:497
  132.0 3.6 fusion.34
  135.7 0.9 slice.275.k_ref
  136.6 1.3 copy.103
  139.7 1.1 copy-done.12
  141.0 1.3 copy-done.13
  142.6 1.0 copy-done.17
  143.6 1.1 copy-done.25
  144.7 1.4 fusion.32
  146.9 1.0 copy-done.23
  147.9 2.2 multiply_convert_fusion
  150.1 1.5 copy.106
  151.6 1.3 copy.107
  153.0 2.4 fusion.4.v_ref
  155.4 52.2 %shard_map.256 = (bf16[8,512,128]{2,1,0:T(8,128)(2,1)}, f32[128,4096]{1,0:T(8,128)}, f32[8,4096]{1,0:T(8,128)}, bf16[8,512,128]{2,1,0:T(8,128)(2,1)}, bf16[4,128...) custom-call(s32[1,1]{1,0:T(1,128)S(6)} %copy.175.offs_ref, bf16[8,512,128]{2,1,0:T(8,128)(2,1)} %bitcast.177, ...), custom_call_target="tpu_custom_call" | custom-call | flops 40000000000 | bytes 8388608 | tf_op jit(solution)/shard_map/pallas_call | solution.py:497
  207.6 2.4 copy.108
  210.4 0.8 copy-done.19
  211.6 1.4 fusion.33
  213.4 1.8 copy-done.5
  215.3 2.2 broadcast_add_fusion
  217.5 1.1 pad_maximum_fusion.2
  218.6 9.4 %all-gather.2.cloned.1.call-done.win_ref.wout_ref = bf16[1024,8192]{1,0:T(8,128)(2,1)} async-done(((bf16[32,8192]{1,0:T(8,128)(2,1)}), bf16[1024,8192]{1,0:T(8,128)(2,1)}) %all-gather.2.cloned.1.call-update) | async-done | bytes 16777232 | tf_op jit(solution)/shard_map/all_gather | solution.py:1570
  228.7 65.0 %shard_map.257 = (f32[512,1024]{1,0:T(8,128)}, f32[512,1024]{1,0:T(8,128)}, f32[8,8,512]{2,1,0:T(8,128)}, bf16[8,512,256]{2,1,0:T(8,128)(2,1)}, bf16[4,2,512,256...) custom-call(bf16[512,1024]{1,0:T(8,128)(2,1)} %get-tuple-element.158.n_ref, bf16[512,1024]{1,0:T(8,128)(2,1)} %refs_3_.1, ...), custom_call_target="tpu_custom_call" | custom-call | flops 30000001024 | bytes 67108864 | tf_op jit(solution)/shard_map/pallas_call | solution.py:1162
  293.7 8.5 %shard_map.258 = (f32[512,1024]{1,0:T(8,128)}, bf16[8,512,128]{2,1,0:T(8,128)(2,1)}, f32[8,1024]{1,0:T(8,128)}, bf16[1,1024,512]{2,1,0:T(8,128)(2,1)}, bf16[1,1024,512]{2,1,0:T(8,128)(2,1)}) custom-call(f32[512,1024]{1,0:T(8,128)} %get-tuple-element.99.refs_0_, f32[512,1024]{1,0:T(8,128)} %copy-done.4, f32[1,1024]{1,0:T(1,128)} %bitcast.203, ...), custom_call_target="tpu_custom_call" | custom-call | flops 10000000000 | bytes 16777216 | tf_op jit(solution)/shard_map/pallas_call | solution.py:1270
  302.1 0.9 collective-permute-start
  303.8 4.8 fusion.27
  310.5 0.9 fusion.24
  312.1 1.1 convert_element_type.168
  313.2 1.5 add_convert_fusion.1
  314.7 1.1 copy.154
  315.8 63.6 %shard_map.259 = (bf16[8,512,128]{2,1,0:T(8,128)(2,1)}, bf16[2048,128]{1,0:T(8,128)(2,1)}, bf16[2048,128]{1,0:T(8,128)(2,1)}, bf16[1,8,4,64,256]{4,3,2,1,0:T(8,1...) custom-call(s32[1,1]{1,0:T(1,128)S(6)} %copy.175.offs_ref, ...), custom_call_target="tpu_custom_call" | custom-call | flops 60000002048 | bytes 8388608 | tf_op jit(solution)/shard_map/pallas_call | solution.py:805
  379.4 1.1 constant_dynamic-update-slice_fusion.1
  380.5 1.3 convert_reduce_fusion.2
  381.8 11.7 %shard_map.260 = (f32[512,1024]{1,0:T(8,128)}, bf16[8,512,128]{2,1,0:T(8,128)(2,1)}, f32[8,1024]{1,0:T(8,128)}, bf16[2,1024,512]{2,1,0:T(8,128)(2,1)}, bf16[2,1024,512]{2,1,0:T(8,128)(2,1)}) custom-call(bf16[8,512,128]{2,1,0:T(8,128)(2,1)} %get-tuple-element.107.refs_0_, bf16[1024,1024]{1,0:T(8,128)(2,1)} %get-tuple-element.156.refs_1_, ...), custom_call_target="tpu_custom_call" | custom-call | flops 10000000000 | bytes 16777216 | tf_op jit(solution)/shard_map/pallas_call | solution.py:1270
  394.1 1.0 fusion.10.refs_2_
  395.4 3.9 convolution_convert_fusion
  400.1 2.1 fusion.2
  402.8 1.5 fusion.refs_1_
  404.3 0.8 copy-done.9
  405.1 2.2 add_convert_fusion
  407.3 1.5 copy.151
  408.9 86.7 %shard_map.261 = (bf16[8,512,384]{2,1,0:T(8,128)(2,1)}, bf16[8,512,384]{2,1,0:T(8,128)(2,1)}, f32[1024,384]{1,0:T(8,128)}, f32[8,384]{1,0:T(8,128)}, bf16[3,2,4,...) custom-call(s32[1,1]{1,0:T(1,128)S(6)} %copy.175.offs_ref, ...), custom_call_target="tpu_custom_call" | custom-call | flops 60000002048 | bytes 8388608 | tf_op jit(solution)/shard_map/pallas_call | solution.py:805
  495.6 1.8 convert_reduce_fusion
  497.4 1.0 fusion.5.ffn_ref
  498.9 1.8 convert_reduce_fusion.1
  501.9 0.9 slice_reduce_fusion.5
  504.6 0.9 copy.123
  505.5 1.4 fusion.30
  506.9 0.7 constant_dynamic-update-slice_fusion.16
  509.3 1.2 pad_maximum_fusion.1.late_ref
  510.4 60.2 %shard_map.262 = (bf16[8,16,64,256]{3,2,1,0:T(8,128)(2,1)}, bf16[8,768,128]{2,1,0:T(8,128)(2,1)}, bf16[8,1328,128]{2,1,0:T(8,128)(2,1)}, f32[512,1024]{1,0:T(8,128)}, f32[256,1024]{1,0:T(8,128)}) custom-call(bf16[4,1328,128]{2,1,0:T(8,128)(2,1)} %pad_maximum_fusion.1.late_ref, bf16[768,128]{1,0:T(8,128)(2,1)} %pad_maximum_fusion.5.done_ref, ...), custom_call_target="tpu_custom_call" | custom-call | flops 49999998976 | bytes 33554432 | tf_op jit(solution)/shard_map/pallas_call | solution.py:1423
  570.6 0.9 convert_reduce_fusion.6
  573.9 12.6 %shard_map.263 = (f32[256,4096]{1,0:T(8,128)}, f32[4,4,64,1024]{3,2,1,0:T(8,128)}, f32[256,3072]{1,0:T(8,128)}, f32[256,2048]{1,0:T(8,128)}, f32[256,1024]{1,0:T...) custom-call(bf16[8,16,64,256]{3,2,1,0:T(8,128)(2,1)} %get-tuple-element.135.refs, ...), custom_call_target="tpu_custom_call" | custom-call | bytes 33554432 | tf_op jit(solution)/shard_map/pallas_call | solution.py:1534
  (202 shorter events, 20.0 us)
Async XLA Ops:
  7.2 73.6 %copy-start = (bf16[1024,1024]{1,0:T(8,128)(2,1)S(1)}, bf16[1024,1024]{1,0:T(8,128)(2,1)}, u32[]{:S(2)}) copy-start(bf16[1024,1024]{1,0:T(8,128)(2,1)} %param.27) | copy-start | bytes 6291460
  7.2 4.6 copy-start.48
  7.2 4.6 copy-start.50
  7.2 4.6 copy-start.33
  7.2 220.8 %all-gather.2.cloned.1.call-start = ((), (), s32[]{:S(2)}) async-start(), calls=%async_computation | async-start | bytes 17301504 | tf_op jit(solution)/shard_map/all_gather | solution.py:1570
  7.3 4.6 copy-start.34
  10.0 4.4 copy-start.47
  10.0 4.4 copy-start.49
  78.8 3.2 copy-start.7
  132.0 4.6 copy-start.22
  135.6 2.3 copy-start.16
  135.7 2.2 copy-start.35
  137.9 0.6 copy-start.32
  139.2 7.3 %copy-start.41 = (f32[1,4,256]{2,0,1:T(1,128)}, f32[1,4,256]{2,0,1:T(1,128)S(1)}, u32[]{:S(2)}) copy-start(f32[1,4,256]{2,0,1:T(1,128)S(1)} %get-tuple-element.175) | copy-start | bytes 12292
  139.2 76.1 %copy-start.42 = (f32[1,4,256]{2,0,1:T(1,128)}, f32[1,4,256]{2,0,1:T(1,128)S(1)}, u32[]{:S(2)}) copy-start(f32[1,4,256]{2,0,1:T(1,128)S(1)} %get-tuple-element.170) | copy-start | bytes 12292
  139.2 1.6 copy-start.12
  140.8 1.6 copy-start.13
  142.3 1.3 copy-start.17
  142.4 2.4 copy-start.25
  142.6 4.3 copy-start.2
  146.1 65.3 %copy-start.3 = (f32[512,1024]{1,0:T(8,128)}, f32[512,1024]{1,0:T(8,128)S(1)}, u32[]{:S(2)}) copy-start(f32[512,1024]{1,0:T(8,128)S(1)} %get-tuple-element.178.refs_3_) | copy-start | bytes 6291460
  146.9 1.0 copy-start.23
  207.6 2.7 copy-start.20
  210.0 1.2 copy-start.19
  210.3 1.3 copy-start.26
  211.3 1.7 copy-start.11
  211.6 1.8 copy-start.8
  213.0 2.3 copy-start.4
  213.0 2.2 copy-start.5
  293.7 9.4 %copy-start.21 = (bf16[512,1024]{1,0:T(8,128)(2,1)S(1)}, bf16[512,1024]{1,0:T(8,128)(2,1)}, u32[]{:S(2)}) copy-start(bf16[512,1024]{1,0:T(8,128)(2,1)} %refs_3_.1) | copy-start | bytes 3145732
  302.1 11.1 %collective-permute-start = (bf16[1,1024,512]{2,1,0:T(8,128)(2,1)}, bf16[1,1024,512]{2,1,0:T(8,128)(2,1)}, u32[]{:S(2)}, u32[]{:S(2)}) collective-permute-start(bf16[1,1024,512]{2,1,0:T(8,128)(2,1)} %get-tuple-element.106), channel_id=1, source_target_pairs={{0,4},{4,0},{8,12},{12,8},{16,20},{20,16},{24,28},{28,24},{1,5},{5... | collective-permute-start | bytes 3145736 | tf_op jit(solution)/shard_map/ppermute | solution.py:1547
  303.8 4.8 copy-start.36
  303.8 8.2 %copy-start.10 = (f32[512,1024]{1,0:T(8,128)S(1)}, f32[512,1024]{1,0:T(8,128)}, u32[]{:S(2)}) copy-start(f32[512,1024]{1,0:T(8,128)} %get-tuple-element.97) | copy-start | bytes 6291460
  308.7 4.6 copy-start.18
  381.8 13.4 %copy-start.14 = (bf16[2048,128]{1,0:T(8,128)(2,1)S(1)}, bf16[2048,128]{1,0:T(8,128)(2,1)}, u32[]{:S(2)}) copy-start(bf16[2048,128]{1,0:T(8,128)(2,1)} %get-tuple-element.118) | copy-start | bytes 1572868
  393.5 10.7 %collective-permute-start.1 = (bf16[2,1024,512]{2,1,0:T(8,128)(2,1)}, bf16[2,1024,512]{2,1,0:T(8,128)(2,1)}, u32[]{:S(2)}, u32[]{:S(2)}) collective-permute-start(bf16[2,1024,512]{2,1,0:T(8,128)(2,1)} %get-tuple-element.110), channel_id=1, source_target_pairs={{0,4},{4,0},{8,12},{12,8},{16,20},{20,16},{24,28},{28,24},{1,5},{5... | collective-permute-start | bytes 6291464 | tf_op jit(solution)/shard_map/ppermute | solution.py:1547
  395.1 4.1 copy-start.28
  395.4 3.9 copy-start.30
  395.4 4.1 copy-start.37
  399.3 0.8 copy-start.38
  399.3 2.9 copy-start.24
  400.1 2.3 copy-start.27
  402.7 2.4 copy-start.9
  497.4 1.0 copy-start.31
  497.4 1.1 copy-start.29
  501.4 1.4 copy-start.6
  501.4 1.7 copy-start.15
  501.4 1.7 copy-start.40
  503.7 4.6 copy-start.46
  503.7 4.7 copy-start.45
  503.7 4.8 copy-start.44
  503.7 4.8 copy-start.43
  503.8 4.8 copy-start.39
  573.9 12.6 %copy-start.1 = (bf16[1024,1024]{1,0:T(8,128)(2,1)S(1)}, bf16[1024,1024]{1,0:T(8,128)(2,1)}, u32[]{:S(2)}) copy-start(bf16[1024,1024]{1,0:T(8,128)(2,1)} %param.27) | copy-start | bytes 6291460
Sparse Core Ops, SparseCore 0:
  82.1 145.8 all-gather.1

commit v6 on v5

--- a/solution.py
+++ b/solution.py
@@ -899,8 +899,8 @@
     order, ready = [], []
     for step in range(count):
         place = step % 2
-        if step in (2, 4) and step // 2 <= groups - 2:
-            chain_advance(step // 2)
+        if step in (4, 6) and step // 2 <= groups - 1:
+            chain_advance(step // 2 - 1)
         if step == 0:
             ready.append(me)
         elif step == 1:
@@ -1629,8 +1629,8 @@
         full = lax.dynamic_update_index_in_dim(full, other, 1 - core, 1)
         return full.reshape(width, -1)
 
-    near_weights = both_cores(near_rows, near_other)
-    full_self_out, full_cross_q = near_weights[:, :width], near_weights[:, width:]
+    full_self_out = both_cores(near_rows[:, :, :width], near_other[:, :, :width])
+    full_cross_q = both_cores(near_rows[:, :, width:], near_other[:, :, width:])
     all_encoder = all_encoder.reshape(-1, width)
     head_kv = head_kv.reshape(width, 2 * own)
 

time: 606 us -> 604 us (level)
    unnamed x119 -> x111, local copies, waits for them, and re-layouts: 15.3 us -> 12.9 us
where the time goes in v6:
time: 604 us; the launch traced here: 592 us
  Pallas kernels  471 us (78%)
  local copies, waits for them, and re-layouts  47.2 us (8%)
  other arithmetic  32.9 us (5%)
  between operations  16.3 us (3%)
  matrix products  13.7 us (2%)
  waiting for transfers between devices  8.93 us (1%)
    pallas_call x2, Pallas kernels, attend_backward(): pl.pallas_call(functools.partial(attend_backward_kernel, cross, heads, of...  150 us
    pallas_call x2, Pallas kernels, attend_forward(): pl.pallas_call(functools.partial(attend_forward_kernel, cross, heads, off...  99.6 us
    pallas_call x1, Pallas kernels, ffn(): pl.pallas_call(functools.partial(ffn_kernel, steps, groups), grid=(steps...  65.7 us
    pallas_call x1, Pallas kernels, project(): pl.pallas_call(functools.partial(project_kernel, own, scale), out_shape=(...  62.4 us
    pallas_call x1, Pallas kernels, finish(): pl.pallas_call(functools.partial(finish_kernel, bool(more)), out_shape=ou...  60.1 us
    pallas_call x2, Pallas kernels, branch(): pl.pallas_call(functools.partial(branch_kernel, bool(query)), out_shape=(...  20.2 us
    unnamed x111, local copies, waits for them, and re-layouts  12.9 us
    pallas_call x1, Pallas kernels, place(): pl.pallas_call(kernel, grid=(chips,), out_shape=out_shape, in_specs=in_sp...  12.6 us
  transfers between devices with their start and end apart: 3, of which 1 were waited for; matrix products, arithmetic and copies ran while one was open for 8% of the time, Pallas kernels for 17%

profile of v6, /device:TPU:0, one launch (start us, length us, event | category | flops | bytes accessed | tf_op | source)
XLA Modules:
  0.0 592.3 jit_solution(14278329961711577869)
XLA Ops:
  7.3 2.7 copy.106
  10.0 1.0 constant_dynamic-slice_fusion.9
  11.0 0.8 copy.107.head_ref
  11.9 1.7 constant_dynamic-slice_fusion.6
  13.6 0.8 pad_maximum_fusion.3.rows_ref
  15.1 62.4 %shard_map.254 = (bf16[8,512,1024]{2,1,0:T(8,128)(2,1)}, bf16[8,512,128]{2,1,0:T(8,128)(2,1)}, bf16[8,512,128]{2,1,0:T(8,128)(2,1)}, bf16[8,512,128]{2,1,0:T(8,1...) custom-call(bf16[512,1024]{1,0:T(8,128)(2,1)} %refs_9_.1, ...), custom_call_target="tpu_custom_call" | custom-call | flops 49999998976 | bytes 33554432 | tf_op jit(solution)/shard_map/pallas_call | solution.py:952
  77.5 1.0 constant_dynamic-slice_fusion.5
  78.7 0.8 copy.120
  79.5 1.1 reshape.298
  81.0 0.8 pad_maximum_fusion.4
  82.1 0.9 dynamic-slice_reduce_fusion
  84.3 47.5 %shard_map.255 = (bf16[8,512,128]{2,1,0:T(8,128)(2,1)}, f32[128,4096]{1,0:T(8,128)}, f32[8,4096]{1,0:T(8,128)}, bf16[4,128,2048]{2,1,0:T(8,128)(2,1)}, bf16[8,25...) custom-call(s32[1,1]{1,0:T(1,128)S(6)} %copy.185.offs_ref, bf16[4096,128]{1,0:T(8,128)(2,1)} %bitcast.228, ...), custom_call_target="tpu_custom_call" | custom-call | flops 40000000000 | bytes 8388608 | tf_op jit(solution)/shard_map/pallas_call | solution.py:497
  131.8 4.9 fusion.31
  136.7 2.1 slice.281.k_ref
  138.8 1.6 copy.109
  142.5 1.2 copy-done.15
  144.1 0.9 copy-done.5
  145.0 1.4 fusion.29
  147.1 1.0 copy-done.21
  148.1 2.2 multiply_convert_fusion
  150.3 1.5 copy.114
  151.8 1.3 copy.115
  153.2 2.4 fusion.4.v_ref
  155.6 52.1 %shard_map.256 = (bf16[8,512,128]{2,1,0:T(8,128)(2,1)}, f32[128,4096]{1,0:T(8,128)}, f32[8,4096]{1,0:T(8,128)}, bf16[8,512,128]{2,1,0:T(8,128)(2,1)}, bf16[4,128...) custom-call(s32[1,1]{1,0:T(1,128)S(6)} %copy.185.offs_ref, bf16[8,512,128]{2,1,0:T(8,128)(2,1)} %bitcast.189, ...), custom_call_target="tpu_custom_call" | custom-call | flops 40000000000 | bytes 8388608 | tf_op jit(solution)/shard_map/pallas_call | solution.py:497
  207.8 2.4 copy.116
  210.6 0.8 copy-done.19
  211.8 1.4 fusion.30
  213.6 1.8 copy-done.6
  215.5 2.2 broadcast_add_fusion
  217.6 1.1 pad_maximum_fusion.2
  218.8 8.9 %all-gather.2.cloned.1.call-done.win_ref.wout_ref = bf16[1024,8192]{1,0:T(8,128)(2,1)} async-done(((bf16[32,8192]{1,0:T(8,128)(2,1)}), bf16[1024,8192]{1,0:T(8,128)(2,1)}) %all-gather.2.cloned.1.call-update) | async-done | bytes 16777232 | tf_op jit(solution)/shard_map/all_gather | solution.py:1570
  228.4 65.7 %shard_map.257 = (f32[512,1024]{1,0:T(8,128)}, f32[512,1024]{1,0:T(8,128)}, f32[8,8,512]{2,1,0:T(8,128)}, bf16[8,512,256]{2,1,0:T(8,128)(2,1)}, bf16[4,2,512,256...) custom-call(bf16[512,1024]{1,0:T(8,128)(2,1)} %get-tuple-element.156.n_ref, bf16[512,1024]{1,0:T(8,128)(2,1)} %refs_3_.1, ...), custom_call_target="tpu_custom_call" | custom-call | flops 30000001024 | bytes 67108864 | tf_op jit(solution)/shard_map/pallas_call | solution.py:1162
  294.0 8.5 %shard_map.258 = (f32[512,1024]{1,0:T(8,128)}, bf16[8,512,128]{2,1,0:T(8,128)(2,1)}, f32[8,1024]{1,0:T(8,128)}, bf16[1,1024,512]{2,1,0:T(8,128)(2,1)}, bf16[1,1024,512]{2,1,0:T(8,128)(2,1)}) custom-call(f32[512,1024]{1,0:T(8,128)} %get-tuple-element.99.refs_0_, f32[512,1024]{1,0:T(8,128)} %copy-done.3, f32[1,1024]{1,0:T(1,128)} %bitcast.216, ...), custom_call_target="tpu_custom_call" | custom-call | flops 10000000000 | bytes 16777216 | tf_op jit(solution)/shard_map/pallas_call | solution.py:1270
  302.6 0.9 collective-permute-start
  303.5 1.5 reduce.1
  305.6 0.8 convert.81
  308.2 0.9 fusion.24
  309.7 1.1 convert_element_type.168
  310.9 1.5 add_convert_fusion.1
  312.4 1.1 copy.162
  313.4 63.5 %shard_map.259 = (bf16[8,512,128]{2,1,0:T(8,128)(2,1)}, bf16[2048,128]{1,0:T(8,128)(2,1)}, bf16[2048,128]{1,0:T(8,128)(2,1)}, bf16[1,8,4,64,256]{4,3,2,1,0:T(8,1...) custom-call(s32[1,1]{1,0:T(1,128)S(6)} %copy.185.offs_ref, ...), custom_call_target="tpu_custom_call" | custom-call | flops 60000002048 | bytes 8388608 | tf_op jit(solution)/shard_map/pallas_call | solution.py:805
  376.9 1.1 constant_dynamic-update-slice_fusion.1
  378.1 1.3 convert_reduce_fusion.2
  379.4 11.7 %shard_map.260 = (f32[512,1024]{1,0:T(8,128)}, bf16[8,512,128]{2,1,0:T(8,128)(2,1)}, f32[8,1024]{1,0:T(8,128)}, bf16[2,1024,512]{2,1,0:T(8,128)(2,1)}, bf16[2,1024,512]{2,1,0:T(8,128)(2,1)}) custom-call(bf16[8,512,128]{2,1,0:T(8,128)(2,1)} %get-tuple-element.107.refs_0_, bf16[1024,1024]{1,0:T(8,128)(2,1)} %bitcast.181, bf16[512,1024]{1,0:T(8,128)(2,1)} %copy-done.21, ...), custom_call_target="tpu_custom_call" | custom-call | flops 10000000000 | bytes 16777216 | tf_op jit(solution)/shard_map/pallas_call | solution.py:1270
  391.1 1.7 collective-permute-start.1
  392.7 1.0 fusion.10.refs_2_
  394.0 3.9 convolution_convert_fusion
  398.7 2.1 fusion.2
  401.4 1.5 fusion.refs_1_
  402.9 0.8 copy-done.10
  403.7 2.2 add_convert_fusion
  405.9 1.5 copy.159
  407.5 86.5 %shard_map.261 = (bf16[8,512,384]{2,1,0:T(8,128)(2,1)}, bf16[8,512,384]{2,1,0:T(8,128)(2,1)}, f32[1024,384]{1,0:T(8,128)}, f32[8,384]{1,0:T(8,128)}, bf16[3,2,4,...) custom-call(s32[1,1]{1,0:T(1,128)S(6)} %copy.185.offs_ref, ...), custom_call_target="tpu_custom_call" | custom-call | flops 60000002048 | bytes 8388608 | tf_op jit(solution)/shard_map/pallas_call | solution.py:805
  494.0 1.8 convert_reduce_fusion
  495.9 1.0 fusion.5.ffn_ref
  497.4 1.8 convert_reduce_fusion.1
  500.3 0.9 slice_reduce_fusion.5
  503.1 0.9 copy.131
  504.0 1.3 fusion.27
  505.3 0.7 constant_dynamic-update-slice_fusion.16
  507.7 1.2 pad_maximum_fusion.1.late_ref
  508.9 60.1 %shard_map.262 = (bf16[8,16,64,256]{3,2,1,0:T(8,128)(2,1)}, bf16[8,768,128]{2,1,0:T(8,128)(2,1)}, bf16[8,1328,128]{2,1,0:T(8,128)(2,1)}, f32[512,1024]{1,0:T(8,128)}, f32[256,1024]{1,0:T(8,128)}) custom-call(bf16[4,1328,128]{2,1,0:T(8,128)(2,1)} %pad_maximum_fusion.1.late_ref, bf16[768,128]{1,0:T(8,128)(2,1)} %pad_maximum_fusion.5.done_ref, ...), custom_call_target="tpu_custom_call" | custom-call | flops 49999998976 | bytes 33554432 | tf_op jit(solution)/shard_map/pallas_call | solution.py:1423
  569.0 0.9 convert_reduce_fusion.6
  572.4 12.6 %shard_map.263 = (f32[256,4096]{1,0:T(8,128)}, f32[4,4,64,1024]{3,2,1,0:T(8,128)}, f32[256,3072]{1,0:T(8,128)}, f32[256,2048]{1,0:T(8,128)}, f32[256,1024]{1,0:T...) custom-call(bf16[8,16,64,256]{3,2,1,0:T(8,128)(2,1)} %get-tuple-element.135.refs, ...), custom_call_target="tpu_custom_call" | custom-call | bytes 33554432 | tf_op jit(solution)/shard_map/pallas_call | solution.py:1534
  (195 shorter events, 19.2 us)
Async XLA Ops:
  7.2 73.4 %copy-start = (bf16[1024,1024]{1,0:T(8,128)(2,1)S(1)}, bf16[1024,1024]{1,0:T(8,128)(2,1)}, u32[]{:S(2)}) copy-start(bf16[1024,1024]{1,0:T(8,128)(2,1)} %param.27) | copy-start | bytes 6291460
  7.2 4.6 copy-start.44
  7.2 4.6 copy-start.46
  7.2 4.6 copy-start.30
  7.2 220.5 %all-gather.2.cloned.1.call-start = ((), (), s32[]{:S(2)}) async-start(), calls=%async_computation | async-start | bytes 17301504 | tf_op jit(solution)/shard_map/all_gather | solution.py:1570
  7.3 4.6 copy-start.31
  10.0 4.4 copy-start.43
  10.0 4.4 copy-start.45
  78.7 3.2 copy-start.8
  136.7 3.8 copy-start.32
  138.8 3.2 copy-start.11
  140.5 0.6 copy-start.29
  141.8 5.0 copy-start.37
  141.8 73.7 %copy-start.38 = (f32[1,4,256]{2,0,1:T(1,128)}, f32[1,4,256]{2,0,1:T(1,128)S(1)}, u32[]{:S(2)}) copy-start(f32[1,4,256]{2,0,1:T(1,128)S(1)} %get-tuple-element.170) | copy-start | bytes 12292
  142.1 1.6 copy-start.15
  143.7 1.2 copy-start.5
  144.0 2.3 copy-start.4
  144.0 3.1 copy-start.14
  146.3 65.2 %copy-start.2 = (f32[512,1024]{1,0:T(8,128)}, f32[512,1024]{1,0:T(8,128)S(1)}, u32[]{:S(2)}) copy-start(f32[512,1024]{1,0:T(8,128)S(1)} %get-tuple-element.178.refs_3_) | copy-start | bytes 6291460
  147.1 1.0 copy-start.21
  207.7 2.7 copy-start.20
  210.2 1.2 copy-start.19
  210.4 1.3 copy-start.23
  211.5 1.7 copy-start.13
  211.8 1.8 copy-start.9
  213.2 2.3 copy-start.3
  213.2 2.2 copy-start.6
  294.0 15.7 %copy-start.12 = (f32[512,1024]{1,0:T(8,128)S(1)}, f32[512,1024]{1,0:T(8,128)}, u32[]{:S(2)}) copy-start(f32[512,1024]{1,0:T(8,128)} %get-tuple-element.97) | copy-start | bytes 6291460
  302.6 8.3 %collective-permute-start = (bf16[1,1024,512]{2,1,0:T(8,128)(2,1)}, bf16[1,1024,512]{2,1,0:T(8,128)(2,1)}, u32[]{:S(2)}, u32[]{:S(2)}) collective-permute-start(bf16[1,1024,512]{2,1,0:T(8,128)(2,1)} %get-tuple-element.106), channel_id=1, source_target_pairs={{0,4},{4,0},{8,12},{12,8},{16,20},{20,16},{24,28},{28,24},{1,5},{5... | collective-permute-start | bytes 3145736 | tf_op jit(solution)/shard_map/ppermute | solution.py:1547
  303.5 7.4 %copy-start.18 = (bf16[1,1024,512]{2,1,0:T(8,128)(2,1)S(1)}, bf16[1,1024,512]{2,1,0:T(8,128)(2,1)}, u32[]{:S(2)}) copy-start(bf16[1,1024,512]{2,1,0:T(8,128)(2,1)} %get-tuple-element.105) | copy-start | bytes 3145732
  379.4 14.5 %copy-start.16 = (bf16[2048,128]{1,0:T(8,128)(2,1)S(1)}, bf16[2048,128]{1,0:T(8,128)(2,1)}, u32[]{:S(2)}) copy-start(bf16[2048,128]{1,0:T(8,128)(2,1)} %get-tuple-element.118) | copy-start | bytes 1572868
  391.1 11.8 %collective-permute-start.1 = (bf16[2,1024,512]{2,1,0:T(8,128)(2,1)}, bf16[2,1024,512]{2,1,0:T(8,128)(2,1)}, u32[]{:S(2)}, u32[]{:S(2)}) collective-permute-start(bf16[2,1024,512]{2,1,0:T(8,128)(2,1)} %get-tuple-element.110), channel_id=1, source_target_pairs={{0,4},{4,0},{8,12},{12,8},{16,20},{20,16},{24,28},{28,24},{1,5},{5... | collective-permute-start | bytes 6291464 | tf_op jit(solution)/shard_map/ppermute | solution.py:1547
  393.8 4.1 copy-start.25
  394.0 3.9 copy-start.27
  394.0 4.1 copy-start.33
  397.9 0.8 copy-start.34
  398.0 2.9 copy-start.22
  398.7 2.3 copy-start.24
  401.4 2.4 copy-start.10
  495.9 1.0 copy-start.28
  495.9 1.1 copy-start.26
  499.9 1.4 copy-start.7
  499.9 1.7 copy-start.17
  499.9 1.7 copy-start.36
  502.2 4.6 copy-start.42
  502.2 4.7 copy-start.41
  502.2 4.7 copy-start.40
  502.2 4.8 copy-start.39
  502.2 4.8 copy-start.35
  572.3 12.6 %copy-start.1 = (bf16[1024,1024]{1,0:T(8,128)(2,1)S(1)}, bf16[1024,1024]{1,0:T(8,128)(2,1)}, u32[]{:S(2)}) copy-start(bf16[1024,1024]{1,0:T(8,128)(2,1)} %param.27) | copy-start | bytes 6291460
Sparse Core Ops, SparseCore 0:
  81.9 145.7 all-gather.1
